TPU v7x, 32 devices: a whole 2x2x4 slice. The times are simulated.
32 devices in a mesh: grp: 4 (over y, x), fsdp: 4 (over z), tp: 2 (over core).
Axes of the slice: x: 2, y: 2, z: 4, core: 2. Of those that a mesh axis runs over, the one named last changes fastest.
Arguments:
- image_rows: bfloat16 [6144, 8192], P(('grp', 'fsdp'), 'tp'), may hold values from -6 to 6
- enc_gain: bfloat16 [8192], P('tp'), may hold values from 0.099609375 to 1.8984375
- key_value_w: bfloat16 [8192, 1024], P(('tp', 'fsdp')), may hold values from -0.0625 to 0.0625
- tiles: int32 [24], P('fsdp'), may hold values from 1 to 4
- queries: bfloat16 [4096, 4096], P(('grp', 'fsdp'), 'tp'), may hold values from -6 to 6
Outputs:
- attended: bfloat16 [4096, 4096], P(('grp', 'fsdp'), 'tp')
Inputs may be any that keep to these rules, and one draw needn't show every extreme that they name: Each sample has 1 to 4 tiles.
All inputs are finite; a program needn't handle non-finite values.
Results may differ from a plain program's by a relative error of at most 0.0077.
Values may be sent and summed in bfloat16 or wider, within the bound.
No kernel may reach another device: no remote copies, remote signals or barrier semaphores. Data moves between devices by JAX's collectives and lax.ppermute only.
A program may use at most 64 MiB of HBM per device.

v0:
```python
import jax
import jax.numpy as jnp
from jax import lax
from jax.sharding import PartitionSpec as P

D = 8192
HD = 128
KVH = 4
QH = 32
TILE_TOK = 16
SAMP = 2
TXT_S = 128
CAP = 64


def into_slots(block, per_group):
    parts = block.reshape((3, per_group) + block.shape[1:])
    empty = jnp.zeros((1, per_group) + block.shape[1:], block.dtype)
    return jnp.concatenate([empty, parts], axis=0)


def fold_rows(rows, piece):
    return jnp.dot(rows, piece, preferred_element_type=jnp.float32)


def shards(image_rows, enc_gain, key_value_w, tiles, queries):
    group = lax.axis_index("grp")
    per_group = image_rows.shape[0] // 3
    width = key_value_w.shape[1]
    heads_kv = width // (2 * HD)
    rows = image_rows.astype(jnp.float32)
    squares = lax.psum(jnp.sum(rows * rows, axis=1, keepdims=True), "tp")
    normed = (rows * lax.rsqrt(squares / D + 1e-05) * enc_gain.astype(jnp.float32)).astype(
        jnp.bfloat16
    )
    received = lax.all_to_all(
        into_slots(normed, per_group), "grp", split_axis=0, concat_axis=0, tiled=True
    )
    mine = received[0]
    total = fold_rows(mine, lax.all_gather(key_value_w, "fsdp", axis=0, tiled=True))
    heads = lax.psum_scatter(
        total.reshape(per_group, heads_kv, 2 * HD), "tp", scatter_dimension=1, tiled=True
    )
    kv = heads.astype(jnp.bfloat16)
    local_kv = kv.shape[1]
    groups_q = QH // KVH
    kv = kv.reshape(SAMP, CAP, local_kv, 2 * HD)
    keys = kv[..., :HD]
    values = kv[..., HD:]
    query = queries.reshape(SAMP, TXT_S, local_kv, groups_q, HD)
    counts = lax.dynamic_slice_in_dim(tiles, jnp.maximum(group - 1, 0) * SAMP, SAMP) * TILE_TOK
    live = jnp.arange(CAP)[None, :] < counts[:, None]
    scores = jnp.einsum("sikgd,sjkd->skgij", query, keys, preferred_element_type=jnp.float32) * (
        1.0 / HD**0.5
    )
    scores = jnp.where(live[:, None, None, None, :], scores, -1e30)
    top = jnp.max(scores, axis=-1, keepdims=True)
    expo = jnp.exp(scores - top)
    weights = (expo / jnp.sum(expo, axis=-1, keepdims=True)).astype(jnp.bfloat16)
    out = jnp.einsum(
        "skgij,sjkd->sikgd", weights, values, preferred_element_type=jnp.float32
    ).astype(jnp.bfloat16)
    out = jnp.where(group > 0, out, jnp.zeros_like(out))
    return out.reshape(queries.shape[0], queries.shape[1])


def solution(mesh):
    return jax.shard_map(
        shards,
        mesh=mesh,
        in_specs=(
            P(("grp", "fsdp"), "tp"),
            P("tp"),
            P(("tp", "fsdp"), None),
            P("fsdp"),
            P(("grp", "fsdp"), "tp"),
        ),
        out_specs=P(("grp", "fsdp"), "tp"),
        check_vma=False,
    )
```

profile of v0, /device:TPU:0, one launch (start us, length us, event | category | flops | bytes accessed | tf_op | source)
XLA Modules:
  0.0 198.0 jit_solution(12229138271863760455)
XLA Ops:
  6.5 0.0 copy-start
  6.5 0.0 all-gather.2.cloned.1.call-start
  6.5 0.7 all-gather.2.cloned.1.call-update
  7.3 0.9 convert_element_type.20
  8.2 2.6 %fusion.1 = f32[384]{0:T(512)S(1)} fusion(bf16[384,4096]{1,0:T(8,128)(2,1)} %param.5), kind=kLoop, calls=%fused_computation.3 | loop fusion | flops 4718208 | bytes 3147264 | tf_op jit(solution)/shard_map/reduce_sum | solution.py:32
  10.8 2.6 %psum.7 = f32[384,1]{0,1:T(1,128)S(1)} all-reduce(f32[384,1]{0,1:T(1,128)S(1)} %broadcast_in_dim.16), channel_id=1, replica_groups=mesh['grp'=4,'fsdp'=4,'tp'=2] {'tp'}, use_global_device_ids=true, to_apply=%region_1.0 | all-reduce | flops 384 | bytes 3072 | tf_op jit(solution)/shard_map/psum | solution.py:32
  13.4 0.0 copy-done
  13.4 1.0 fusion.3
  14.4 2.5 %concatenate.3 = bf16[4,128,4096]{2,1,0:T(8,128)(2,1)} pad(bf16[3,128,4096]{2,1,0:T(8,128)(2,1)S(1)} %bitcast.31, bf16[]{:T(256)} %constant.7.clone.1), padding=1_0x0_0x0_0 | pad | bytes 7340034 | tf_op jit(solution)/shard_map/concatenate | solution.py:19
  16.9 5.0 %all-to-all-start = ((bf16[4,128,4096]{2,1,0:T(8,128)(2,1)}), bf16[4,128,4096]{2,1,0:T(8,128)(2,1)}, u32[]{:S(2)}, u32[]{:S(2)}) async-start(bf16[4,128,4096]{2,1,0:T(8,128)(2,1)} %concatenate.3), calls=%async_computation | async-start | bytes 8388608 | tf_op jit(solution)/shard_map/all_to_all | solution.py:36
  22.0 0.0 reduce-scatter.2.cloned.1.call-start
  22.0 139.3 %all-gather.2.cloned.1.call-done = bf16[4096,1024]{1,0:T(8,128)(2,1)} async-done(((bf16[1024,1024]{1,0:T(8,128)(2,1)}), bf16[4096,1024]{1,0:T(8,128)(2,1)}) %all-gather.2.cloned.1.call-update) | async-done | bytes 8388624 | tf_op jit(solution)/shard_map/all_gather | solution.py:40
  161.3 11.5 %copy.10 = bf16[1024,4096]{1,0:T(8,128)(2,1)} copy(bf16[1024,4096]{0,1:T(8,128)(2,1)} %bitcast.32) | data formatting | bytes 16777216 | tf_op jit(solution)/shard_map/dot_general | solution.py:23
  172.8 0.0 copy-start.1
  172.8 0.0 all-to-all-done
  172.8 0.0 copy-start.2
  172.8 7.5 %fusion.10 = f32[128,4,256]{2,0,1:T(8,128)} fusion(bf16[4,256,4096]{2,1,0:T(8,128)(2,1)} %bitcast.30, bf16[4,128,4096]{2,1,0:T(8,128)(2,1)} %all-to-all-done), kind=kOutput, calls=%fused_computation.15 | convolution fusion | flops 1073741824 | bytes 9961472 | tf_op jit(solution)/shard_map/dot_general | solution.py:23
  180.3 0.0 reduce-scatter.2.cloned.1.call-update
  180.3 0.0 copy-done.1
  180.3 0.2 copy.19
  180.6 0.0 copy-done.2
  180.6 0.1 dynamic-slice_multiply_fusion
  180.7 0.1 iota_compare_fusion
  180.7 5.9 %reduce-scatter.2.cloned.1.call-done = f32[128,2,256]{2,0,1:T(8,128)} async-done(((f32[128,4,256]{2,0,1:T(8,128)}), f32[128,2,256]{2,0,1:T(8,128)}) %reduce-scatter.2.cloned.1.call-update) | async-done | bytes 262160 | tf_op jit(solution)/shard_map/reduce_scatter | solution.py:41
  186.7 1.0 convert_element_type.22
  187.7 0.5 fusion.9
  188.1 0.2 fusion.15
  188.4 0.5 fusion.6
  188.9 1.0 copy.14
  189.9 1.3 reshape.37
  (3 shorter events, 0.1 us)
Async XLA Ops:
  6.5 6.8 %copy-start = (bf16[384,4096]{1,0:T(8,128)(2,1)S(1)}, bf16[384,4096]{1,0:T(8,128)(2,1)}, u32[]{:S(2)}) copy-start(bf16[384,4096]{1,0:T(8,128)(2,1)} %param.5) | copy-start | bytes 9437188
  6.5 154.8 %all-gather.2.cloned.1.call-start = ((), (), s32[]{:S(2)}) async-start(), calls=%async_computation.2 | async-start | bytes 10485760 | tf_op jit(solution)/shard_map/all_gather | solution.py:40
  16.9 155.9 %all-to-all-start = ((bf16[4,128,4096]{2,1,0:T(8,128)(2,1)}), bf16[4,128,4096]{2,1,0:T(8,128)(2,1)}, u32[]{:S(2)}, u32[]{:S(2)}) async-start(bf16[4,128,4096]{2,1,0:T(8,128)(2,1)} %concatenate.3), calls=%async_computation | async-start | bytes 8388608 | tf_op jit(solution)/shard_map/all_to_all | solution.py:36
  22.0 164.7 %reduce-scatter.2.cloned.1.call-start = ((), (), s32[]{:S(2)}) async-start(), calls=%async_computation.3 | async-start | bytes 786432 | tf_op jit(solution)/shard_map/reduce_scatter | solution.py:41
  172.8 7.5 %copy-start.1 = (bf16[256,2048]{1,0:T(8,128)(2,1)S(1)}, bf16[256,2048]{1,0:T(8,128)(2,1)}, u32[]{:S(2)}) copy-start(bf16[256,2048]{1,0:T(8,128)(2,1)} %param.9) | copy-start | bytes 3145732
  172.8 7.8 %copy-start.2 = (s32[6]{0:T(128)S(1)}, s32[6]{0:T(128)}, u32[]{:S(2)}) copy-start(s32[6]{0:T(128)} %param.8) | copy-start | bytes 76
Sparse Core Ops, SparseCore 0:
  8.9 152.3 all-gather.1
  180.4 6.1 reduce-scatter.1
where the time goes:
time: 199 us; the launch traced here: 198 us
  waiting for transfers between devices  146 us (73%)
  local copies, waits for them, and re-layouts  16.5 us (8%)
  between operations  13.5 us (7%)
  matrix products  8.47 us (4%)
  other arithmetic  5.88 us (3%)
  starting transfers between devices  5.05 us (3%)
  blocking collectives  2.58 us (1%)
    all_gather x1, waiting for transfers between devices, shards(): lax.all_gather(key_value_w, 'fsdp', axis=0, tiled=True)  139 us
    dot_general x1, local copies, waits for them, and re-layouts, fold_rows(): return jnp.dot(rows, piece, preferred_element_type=jnp.float32)  11.5 us
    dot_general x1, matrix products, fold_rows(): return jnp.dot(rows, piece, preferred_element_type=jnp.float32)  7.48 us
    reduce_scatter x1, waiting for transfers between devices, shards(): lax.psum_scatter(total.reshape(per_group, heads_kv, 2 * HD), 'tp', scatte...  5.92 us
    all_to_all x1, starting transfers between devices, shards(): lax.all_to_all(into_slots(normed, per_group), 'grp', split_axis=0, concat...  5.05 us
  transfers between devices with their start and end apart: 3, of which 2 were waited for; matrix products, arithmetic and copies ran while one was open for 10% of the time, Pallas kernels for 0%

commit v1 on v0

v1 whole, which is shorter than its diff:
```python
import jax
import jax.numpy as jnp
from jax import lax
from jax.sharding import PartitionSpec as P

D = 8192
HD = 128
KVH = 4
QH = 32
TILE_TOK = 16
SAMP = 2
TXT_S = 128
CAP = 64
AXES = ("grp", "fsdp", "tp")


def normed_rows(image_rows, enc_gain, sum_cores):
    rows = image_rows.astype(jnp.float32)
    squares = sum_cores(jnp.sum(rows * rows, axis=1, keepdims=True))
    return (rows * lax.rsqrt(squares / D + 1e-05) * enc_gain.astype(jnp.float32)).astype(
        jnp.bfloat16
    )


def attend(kv, tiles, queries, group):
    local_kv = kv.shape[1]
    groups_q = QH // KVH
    kv = kv.reshape(SAMP, CAP, local_kv, 2 * HD)
    keys = kv[..., :HD]
    values = kv[..., HD:]
    query = queries.reshape(SAMP, TXT_S, local_kv, groups_q, HD)
    counts = lax.dynamic_slice_in_dim(tiles, jnp.maximum(group - 1, 0) * SAMP, SAMP) * TILE_TOK
    live = jnp.arange(CAP)[None, :] < counts[:, None]
    scores = jnp.einsum("sikgd,sjkd->skgij", query, keys, preferred_element_type=jnp.float32) * (
        1.0 / HD**0.5
    )
    scores = jnp.where(live[:, None, None, None, :], scores, -1e30)
    top = jnp.max(scores, axis=-1, keepdims=True)
    expo = jnp.exp(scores - top)
    weights = (expo / jnp.sum(expo, axis=-1, keepdims=True)).astype(jnp.bfloat16)
    out = jnp.einsum(
        "skgij,sjkd->sikgd", weights, values, preferred_element_type=jnp.float32
    ).astype(jnp.bfloat16)
    out = jnp.where(group > 0, out, jnp.zeros_like(out))
    return out.reshape(queries.shape[0], queries.shape[1])


def shards_any(image_rows, enc_gain, key_value_w, tiles, queries):
    group = lax.axis_index("grp")
    per_group = image_rows.shape[0] // 3
    heads_kv = key_value_w.shape[1] // (2 * HD)
    normed = normed_rows(image_rows, enc_gain, lambda s: lax.psum(s, "tp"))
    parts = normed.reshape((3, per_group, normed.shape[1]))
    slots = jnp.concatenate([jnp.zeros_like(parts[:1]), parts], axis=0)
    mine = lax.all_to_all(slots, "grp", split_axis=0, concat_axis=0, tiled=True)[0]
    total = jnp.dot(
        mine,
        lax.all_gather(key_value_w, "fsdp", axis=0, tiled=True),
        preferred_element_type=jnp.float32,
    )
    heads = lax.psum_scatter(
        total.reshape(per_group, heads_kv, 2 * HD), "tp", scatter_dimension=1, tiled=True
    )
    return attend(heads.astype(jnp.bfloat16), tiles, queries, group)


def shards_line(image_rows, enc_gain, key_value_w, tiles, queries):
    g, f, t = (lax.axis_index(a) for a in AXES)
    n_rows = image_rows.shape[0]
    per_group = n_rows // 3
    width = key_value_w.shape[1]
    half = width // 2
    depth = key_value_w.shape[0]
    quarter = depth // 4

    def send(x, pairs):
        index = lambda p, c: (p[0] * 4 + p[1]) * 2 + c
        return lax.ppermute(x, AXES, [(index(a, c), index(b, c)) for a, b in pairs for c in (0, 1)])

    def swap(x):
        return lax.ppermute(x, "tp", [(0, 1), (1, 0)])

    own_rows = lax.dynamic_slice_in_dim(key_value_w, g * quarter, quarter, axis=0)
    kept = lax.dynamic_slice_in_dim(own_rows, t * half, half, axis=1)
    given = lax.dynamic_slice_in_dim(own_rows, (1 - t) * half, half, axis=1)
    own = jnp.concatenate([kept, swap(given)], axis=0)
    from_below = send(own, [((c, z), (c, z + 1)) for c in range(4) for z in range(3)])
    from_above = send(own, [((c, z + 1), (c, z)) for c in range(4) for z in range(3)])
    onward = jnp.where((f == 0) | (f == 3), own, jnp.where(f == 2, from_below, from_above))
    from_two = send(
        onward, [((c, a), (c, b)) for c in range(4) for a, b in ((0, 2), (3, 1), (2, 3), (1, 0))]
    )
    from_three = send(from_two, [((c, a), (c, b)) for c in range(4) for a, b in ((2, 3), (1, 0))])

    normed = normed_rows(image_rows, enc_gain, lambda s: s + swap(s))
    pieces = normed.reshape(n_rows, 4, 4, quarter).transpose(2, 1, 0, 3)
    planes = range(4)
    at_d = send(pieces[3, :2], [((0, z), (3, z)) for z in planes])
    at_b = send(pieces[1], [((0, z), (1, z)) for z in planes])
    at_c = send(
        jnp.concatenate([pieces[3, 2:], pieces[2]], axis=0), [((0, z), (2, z)) for z in planes]
    )
    at_d2 = send(at_c[:2], [((2, z), (3, z)) for z in planes])
    mine = jnp.where(
        g == 0,
        pieces[0],
        jnp.where(
            g == 1, at_b, jnp.where(g == 2, at_c[2:], jnp.concatenate([at_d, at_d2], axis=0))
        ),
    )
    rows = jnp.concatenate([mine, swap(mine)], axis=2)

    def part(block, plane):
        return jnp.dot(
            lax.dynamic_index_in_dim(rows, plane, 0, keepdims=False),
            block,
            preferred_element_type=jnp.float32,
        )

    total = (
        part(own, f)
        + part(from_below, jnp.maximum(f - 1, 0))
        + part(from_above, jnp.minimum(f + 1, 3))
        + part(from_two, f ^ 2)
        + part(from_three, 3 - f)
    ).reshape(3, per_group, half)

    def for_group(h):
        return lax.dynamic_index_in_dim(total, jnp.maximum(h - 1, 0), 0, keepdims=False)

    kv = for_group(g)
    for k in (1, 2, 3):
        kv = kv + send(
            for_group(g ^ k).astype(jnp.bfloat16),
            [((a, z), (a ^ k, z)) for a in range(4) if a ^ k for z in planes],
        ).astype(jnp.float32)
    kv = kv.astype(jnp.bfloat16).reshape(per_group, half // (2 * HD), 2 * HD)
    return attend(kv, tiles, queries, g)


def solution(mesh):
    sizes = tuple(mesh.shape[a] for a in AXES)
    return jax.shard_map(
        shards_line if sizes == (4, 4, 2) else shards_any,
        mesh=mesh,
        in_specs=(
            P(("grp", "fsdp"), "tp"),
            P("tp"),
            P(("tp", "fsdp"), None),
            P("fsdp"),
            P(("grp", "fsdp"), "tp"),
        ),
        out_specs=P(("grp", "fsdp"), "tp"),
        check_vma=False,
    )
```

time: 199 us -> 104 us (0.52)
  waiting for transfers between devices: 146 us -> 52.2 us
  starting transfers between devices: 5.05 us -> 28.3 us
  between operations: 13.5 us -> 0.34 us
  local copies, waits for them, and re-layouts: 16.5 us -> 11 us
  matrix products: 8.47 us -> 5.07 us
  blocking collectives: 2.58 us -> 0 us
    all_gather x1 -> x0, waiting for transfers between devices: 139 us -> none  [shards(): lax.all_gather(key_value_w, 'fsdp', axis=0, tiled=True)]
    ppermute x0 -> x14, waiting for transfers between devices: none -> 52.2 us  [the longest x11 51.3 us: send(): lax.ppermute(x, AXES, [(index(a, c), index(b, c)) for a, b in pairs for c...]
    ppermute x0 -> x14, starting transfers between devices: none -> 28.3 us  [the longest x11 27.7 us: send(): lax.ppermute(x, AXES, [(index(a, c), index(b, c)) for a, b in pairs for c...]
    dot_general x1 -> x0, local copies, waits for them, and re-layouts: 11.5 us -> none  [fold_rows(): return jnp.dot(rows, piece, preferred_element_type=jnp.float32)]
    reduce_scatter x1 -> x0, waiting for transfers between devices: 5.92 us -> none  [shards(): lax.psum_scatter(total.reshape(per_group, heads_kv, 2 * HD), 'tp', scatte...]
    all_to_all x1 -> x0, starting transfers between devices: 5.05 us -> none  [shards(): lax.all_to_all(into_slots(normed, per_group), 'grp', split_axis=0, concat...]
    unnamed x7 -> x16, local copies, waits for them, and re-layouts: 0.24 us -> 5.19 us
    dot_general x3 -> x7, matrix products: 8.47 us -> 5.07 us  [the longest x5 4.09 us: part(): jnp.dot(lax.dynamic_index_in_dim(rows, plane, 0, keepdims=False), block,...]
  transfers between devices with their start and end apart: 3 -> 14, of which waited for: 2 -> 7; matrix products, arithmetic and copies ran while one was open for 10% -> 10% of each run, Pallas kernels for 0% -> 0%
where the time goes in v1:
time: 104 us; the launch traced here: 103 us
  waiting for transfers between devices  52.2 us (50%)
  starting transfers between devices  28.3 us (27%)
  local copies, waits for them, and re-layouts  11 us (11%)
  other arithmetic  5.64 us (5%)
  matrix products  5.07 us (5%)
    ppermute x11, waiting for transfers between devices, send(): lax.ppermute(x, AXES, [(index(a, c), index(b, c)) for a, b in pairs for c...  51.3 us
    ppermute x11, starting transfers between devices, send(): lax.ppermute(x, AXES, [(index(a, c), index(b, c)) for a, b in pairs for c...  27.7 us
    unnamed x16, local copies, waits for them, and re-layouts  5.19 us
    dot_general x5, matrix products, part(): jnp.dot(lax.dynamic_index_in_dim(rows, plane, 0, keepdims=False), block,...  4.09 us
  transfers between devices with their start and end apart: 14, of which 7 were waited for; matrix products, arithmetic and copies ran while one was open for 10% of the time, Pallas kernels for 0%

profile of v1, /device:TPU:0, one launch (start us, length us, event | category | flops | bytes accessed | tf_op | source)
XLA Modules:
  0.0 102.6 jit_solution(9047073284822692166)
XLA Ops:
  0.0 3.4 %copy.15 = bf16[384,4096]{0,1:T(8,128)(2,1)S(1)} copy(bf16[384,4096]{1,0:T(8,128)(2,1)} %param.5) | data formatting | bytes 6291456 | tf_op args[0]
  3.4 0.0 copy-start.5
  3.4 0.8 fusion.1
  4.2 0.5 collective-permute-start
  4.7 0.0 copy-done.5
  4.7 0.8 collective-permute-done
  5.6 0.9 fusion.3
  6.4 0.0 copy-start
  6.5 1.2 %slice_bitcast_fusion = (bf16[4,384,256]{1,2,0:T(8,128)(2,1)S(1)}, bf16[4,384,256]{1,2,0:T(8,128)(2,1)}) fusion(bf16[4,4,384,256]{2,3,0,1:T(8,128)(2,1)S(1)} %bitcast.81), kind=kLoop, calls=%fused_computation.34 | loop fusion | bytes 3145728 | tf_op jit(solution)/shard_map/squeeze | solution.py:101
  7.6 0.8 slice_bitcast_fusion.3
  8.5 0.0 copy-done
  8.5 0.1 pad_maximum_fusion
  8.6 4.8 %collective-permute-start.2 = (bf16[6,384,256]{1,2,0:T(8,128)(2,1)S(1)}, bf16[6,384,256]{1,2,0:T(8,128)(2,1)S(1)}, u32[]{:S(2)}, u32[]{:S(2)}) collective-permute-start(bf16[6,384,256]{1,2,0:T(8,128)(2,1)S(1)} %pad_maximum_fusion), channel_id=1, source_target_pairs={{0,16},{1,17},{2,18},{3,19},{4,20},{5,21},{6,22},{7,23}} | collective-permute-start | bytes 3538952 | tf_op jit(solution)/shard_map/ppermute | solution.py:78
  13.4 2.2 %collective-permute-start.1 = (bf16[4,384,256]{1,2,0:T(8,128)(2,1)}, bf16[4,384,256]{1,2,0:T(8,128)(2,1)}, u32[]{:S(2)}, u32[]{:S(2)}) collective-permute-start(bf16[4,384,256]{1,2,0:T(8,128)(2,1)} %get-tuple-element.8), channel_id=1, source_target_pairs={{0,8},{1,9},{2,10},{3,11},{4,12},{5,13},{6,14},{7,15}} | collective-permute-start | bytes 2359304 | tf_op jit(solution)/shard_map/ppermute | solution.py:78
  15.6 1.3 %fusion.51 = (bf16[256,512]{1,0:T(8,128)(2,1)S(1)}, bf16[256,512]{1,0:T(8,128)(2,1)S(1)}) fusion(bf16[1024,1024]{1,0:T(8,128)(2,1)} %param.7, s32[]{:T(128)S(6)} %select_n.98, s32[]{:T(128)S(6)} %select_n.100, s32[]{:T(128)S(6)} %select_n.102), kind=kLoop, calls=%fused_computation.81 | loop fusion | bytes 1048588 | tf_op jit(solution)/shard_map/dynamic_slice | solution.py:84
  17.0 0.1 collective-permute-start.6
  17.1 1.3 %collective-permute-start.3 = (bf16[2,384,256]{1,2,0:T(8,128)(2,1)}, bf16[2,384,256]{1,2,0:T(8,128)(2,1)S(1)}, u32[]{:S(2)}, u32[]{:S(2)}) collective-permute-start(bf16[2,384,256]{1,2,0:T(8,128)(2,1)} %get-tuple-element.5), channel_id=1, source_target_pairs={{0,24},{1,25},{2,26},{3,27},{4,28},{5,29},{6,30},{7,31}} | collective-permute-start | bytes 1179656 | tf_op jit(solution)/shard_map/ppermute | solution.py:78
  18.4 20.5 %collective-permute-done.2 = bf16[6,384,256]{1,2,0:T(8,128)(2,1)S(1)} collective-permute-done((bf16[6,384,256]{1,2,0:T(8,128)(2,1)S(1)}, bf16[6,384,256]{1,2,0:T(8,128)(2,1)S(1)}, u32[]{:S(2)}, u32[]{:S(2)}) %collective-permute-start.2) | collective-permute-done | bytes 1179680 | tf_op jit(solution)/shard_map/ppermute | solution.py:78
  39.0 0.7 collective-permute-start.4
  39.7 0.0 collective-permute-done.6
  39.7 0.3 copy-done.4
  40.0 0.9 pad_maximum_fusion.1
  40.8 3.5 %collective-permute-start.7 = (bf16[512,512]{1,0:T(8,128)(2,1)}, bf16[512,512]{1,0:T(8,128)(2,1)S(1)}, u32[]{:S(2)}, u32[]{:S(2)}) collective-permute-start(bf16[512,512]{1,0:T(8,128)(2,1)} %pad_maximum_fusion.1), channel_id=1, source_target_pairs={{0,2},{1,3},{2,4},{3,5},{4,6},{5,7},{8,10},{9,11},{10,12},{11,13},... | collective-permute-start | bytes 1572872 | tf_op jit(solution)/shard_map/ppermute | solution.py:78
  44.3 1.3 %collective-permute-start.8 = (bf16[512,512]{1,0:T(8,128)(2,1)}, bf16[512,512]{1,0:T(8,128)(2,1)S(1)}, u32[]{:S(2)}, u32[]{:S(2)}) collective-permute-start(bf16[512,512]{1,0:T(8,128)(2,1)} %pad_maximum_fusion.1), channel_id=1, source_target_pairs={{2,0},{3,1},{4,2},{5,3},{6,4},{7,5},{10,8},{11,9},{12,10},{13,11},... | collective-permute-start | bytes 1572872 | tf_op jit(solution)/shard_map/ppermute | solution.py:78
  45.6 0.0 collective-permute-done.3
  45.6 0.0 collective-permute-done.1
  45.7 0.0 collective-permute-done.4
  45.7 1.6 %fusion.14 = bf16[4,384,256]{1,2,0:T(8,128)(2,1)S(1)} fusion(bf16[4,384,256]{1,2,0:T(8,128)(2,1)} %collective-permute-done.1, bf16[6,384,256]{1,2,0:T(8,128)(2,1)} %copy-done.4, bf16[4,4,384,256]{2,3,0,1:T(8,128)(2,1)} %bitcast.83, bf16[2,384,256]{1,2,0:T(8,128)(2,1)S(1)} %collective-permute-done.4, bf16[2,384,256]{1,2,0:T(8,128)(2,1)S(1)} %collective-permute-done.3, ...), kind=kLoop, calls=%fused_computation.33 | loop fusion | flops 1572864 | bytes 3932163 | tf_op jit(solution)/shard_map/jit(_where)/select_n | solution.py:104
  47.2 0.0 copy-start.6
  47.2 0.1 collective-permute-start.5
  47.3 8.0 %collective-permute-done.7 = bf16[512,512]{1,0:T(8,128)(2,1)S(1)} collective-permute-done((bf16[512,512]{1,0:T(8,128)(2,1)}, bf16[512,512]{1,0:T(8,128)(2,1)S(1)}, u32[]{:S(2)}, u32[]{:S(2)}) %collective-permute-start.7) | collective-permute-done | bytes 524320 | tf_op jit(solution)/shard_map/ppermute | solution.py:78
  55.3 4.0 %collective-permute-done.8 = bf16[512,512]{1,0:T(8,128)(2,1)S(1)} collective-permute-done((bf16[512,512]{1,0:T(8,128)(2,1)}, bf16[512,512]{1,0:T(8,128)(2,1)S(1)}, u32[]{:S(2)}, u32[]{:S(2)}) %collective-permute-start.8) | collective-permute-done | bytes 524320 | tf_op jit(solution)/shard_map/ppermute | solution.py:78
  59.3 1.0 select_select_fusion
  60.3 2.6 %collective-permute-start.9 = (bf16[512,512]{1,0:T(8,128)(2,1)}, bf16[512,512]{1,0:T(8,128)(2,1)}, u32[]{:S(2)}, u32[]{:S(2)}) collective-permute-start(bf16[512,512]{1,0:T(8,128)(2,1)} %select_select_fusion), channel_id=1, source_target_pairs={{0,4},{1,5},{6,2},{7,3},{4,6},{5,7},{2,0},{3,1},{8,12},{9,13},{14,... | collective-permute-start | bytes 1572872 | tf_op jit(solution)/shard_map/ppermute | solution.py:78
  62.9 0.0 copy-done.1
  62.9 0.0 copy-done.2
  62.9 1.4 %copy.38 = bf16[32,8,16,128]{3,2,1,0:T(8,128)(2,1)S(1)} copy(bf16[32,8,16,128]{3,1,2,0:T(8,128)(2,1)} %bitcast.87) | data formatting | bytes 2097152
  64.4 0.0 copy-done.6
  64.4 0.0 copy-start.3
  64.4 0.1 dynamic-slice_multiply_fusion
  64.5 8.2 %collective-permute-done.9 = bf16[512,512]{1,0:T(8,128)(2,1)} collective-permute-done((bf16[512,512]{1,0:T(8,128)(2,1)}, bf16[512,512]{1,0:T(8,128)(2,1)}, u32[]{:S(2)}, u32[]{:S(2)}) %collective-permute-start.9) | collective-permute-done | bytes 524320 | tf_op jit(solution)/shard_map/ppermute | solution.py:78
  72.7 1.3 %collective-permute-start.10 = (bf16[512,512]{1,0:T(8,128)(2,1)}, bf16[512,512]{1,0:T(8,128)(2,1)S(1)}, u32[]{:S(2)}, u32[]{:S(2)}) collective-permute-start(bf16[512,512]{1,0:T(8,128)(2,1)} %collective-permute-done.9), channel_id=1, source_target_pairs={{4,6},{5,7},{2,0},{3,1},{12,14},{13,15},{10,8},{11,9},{20,22},{21,... | collective-permute-start | bytes 1572872 | tf_op jit(solution)/shard_map/ppermute | solution.py:78
  74.0 0.0 collective-permute-done.5
  74.0 1.4 %fusion.24 = f32[384,512]{1,0:T(8,128)S(1)} fusion(bf16[512,512]{1,0:T(8,128)(2,1)} %copy-done.1, s32[]{:T(128)S(6)} %max.16, bf16[4,384,256]{1,2,0:T(8,128)(2,1)S(1)} %fusion.14, bf16[4,384,256]{1,2,0:T(8,128)(2,1)S(1)} %collective-permute-done.5), kind=kOutput, calls=%fused_computation.46 | convolution fusion | flops 202113024 | bytes 2883588 | tf_op jit(solution)/shard_map/dot_general | solution.py:114
  75.5 0.4 fusion.28
  75.9 1.4 %fusion.32 = f32[384,512]{1,0:T(8,128)S(1)} fusion(bf16[512,512]{1,0:T(8,128)(2,1)} %collective-permute-done.9, s32[]{:T(128)S(6)} %select_n.104, bf16[4,384,256]{1,2,0:T(8,128)(2,1)S(1)} %fusion.14, bf16[4,384,256]{1,2,0:T(8,128)(2,1)S(1)} %collective-permute-done.5), kind=kOutput, calls=%fused_computation.52 | convolution fusion | flops 202113024 | bytes 2883588 | tf_op jit(solution)/shard_map/dot_general | solution.py:114
  77.3 0.4 fusion.11
  77.7 8.1 %collective-permute-done.10 = bf16[512,512]{1,0:T(8,128)(2,1)S(1)} collective-permute-done((bf16[512,512]{1,0:T(8,128)(2,1)}, bf16[512,512]{1,0:T(8,128)(2,1)S(1)}, u32[]{:S(2)}, u32[]{:S(2)}) %collective-permute-start.10) | collective-permute-done | bytes 524320 | tf_op jit(solution)/shard_map/ppermute | solution.py:78
  85.9 0.4 convolution_add_fusion
  86.3 0.1 fusion.37
  86.3 1.3 %collective-permute-start.11 = (bf16[128,512]{1,0:T(8,128)(2,1)S(1)}, bf16[128,512]{1,0:T(8,128)(2,1)S(1)}, u32[]{:S(2)}, u32[]{:S(2)}) collective-permute-start(bf16[128,512]{1,0:T(8,128)(2,1)S(1)} %get-tuple-element.11), channel_id=1, source_target_pairs={{0,8},{1,9},{2,10},{3,11},{4,12},{5,13},{6,14},{7,15},{16,24},{17,... | collective-permute-start | bytes 393224 | tf_op jit(solution)/shard_map/ppermute | solution.py:78
  87.6 5.4 %collective-permute-start.12 = (bf16[128,512]{1,0:T(8,128)(2,1)S(1)}, bf16[128,512]{1,0:T(8,128)(2,1)S(1)}, u32[]{:S(2)}, u32[]{:S(2)}) collective-permute-start(bf16[128,512]{1,0:T(8,128)(2,1)S(1)} %get-tuple-element.13), channel_id=1, source_target_pairs={{0,16},{1,17},{2,18},{3,19},{4,20},{5,21},{6,22},{7,23},{8,24},{9,... | collective-permute-start | bytes 393224 | tf_op jit(solution)/shard_map/ppermute | solution.py:78
  93.0 3.4 %collective-permute-start.13 = (bf16[128,512]{1,0:T(8,128)(2,1)S(1)}, bf16[128,512]{1,0:T(8,128)(2,1)S(1)}, u32[]{:S(2)}, u32[]{:S(2)}) collective-permute-start(bf16[128,512]{1,0:T(8,128)(2,1)S(1)} %get-tuple-element.12), channel_id=1, source_target_pairs={{0,24},{1,25},{2,26},{3,27},{4,28},{5,29},{6,30},{7,31},{8,16},{9,... | collective-permute-start | bytes 393224 | tf_op jit(solution)/shard_map/ppermute | solution.py:78
  96.4 0.1 iota_compare_fusion
  96.5 0.0 collective-permute-done.11
  96.5 0.0 collective-permute-done.12
  96.5 2.4 %collective-permute-done.13 = bf16[128,512]{1,0:T(8,128)(2,1)S(1)} collective-permute-done((bf16[128,512]{1,0:T(8,128)(2,1)S(1)}, bf16[128,512]{1,0:T(8,128)(2,1)S(1)}, u32[]{:S(2)}, u32[]{:S(2)}) %collective-permute-start.13) | collective-permute-done | bytes 131104 | tf_op jit(solution)/shard_map/ppermute | solution.py:78
  98.9 0.1 fusion.36
  99.0 0.1 fusion.52
  99.1 0.5 fusion.9
  99.6 0.2 fusion.53
  99.8 0.5 fusion.6
  100.3 1.0 copy.29
  101.3 1.3 %reshape.38 = bf16[256,2048]{1,0:T(8,128)(2,1)} reshape(bf16[2,128,2,8,128]{4,3,2,1,0:T(8,128)(2,1)S(1)} %copy.29) | data formatting | bytes 2097152 | tf_op jit(solution)/shard_map/reshape | solution.py:45
  (9 shorter events, 0.1 us)
Async XLA Ops:
  3.4 1.3 %copy-start.5 = (bf16[4096]{0:T(1024)(128)(2,1)S(1)}, bf16[4096]{0:T(1024)(128)(2,1)}, u32[]{:S(2)}) copy-start(bf16[4096]{0:T(1024)(128)(2,1)} %param.6) | copy-start | bytes 24580
  4.2 1.3 %collective-permute-start = (f32[384,1]{0,1:T(1,128)S(1)}, f32[384,1]{0,1:T(1,128)S(1)}, u32[]{:S(2)}, u32[]{:S(2)}) collective-permute-start(f32[384,1]{0,1:T(1,128)S(1)} %broadcast_in_dim.24), channel_id=1, source_target_pairs={{0,1},{1,0},{2,3},{3,2},{4,5},{5,4},{6,7},{7,6},{8,9},{9,8},{10,11... | collective-permute-start | bytes 4616 | tf_op jit(solution)/shard_map/ppermute | solution.py:81
  6.4 2.0 %copy-start = (bf16[384,4096]{0,1:T(8,128)(2,1)}, bf16[384,4096]{0,1:T(8,128)(2,1)S(1)}, u32[]{:S(2)}) copy-start(bf16[384,4096]{0,1:T(8,128)(2,1)S(1)} %fusion.3) | copy-start | bytes 9437188
  8.6 30.3 %collective-permute-start.2 = (bf16[6,384,256]{1,2,0:T(8,128)(2,1)S(1)}, bf16[6,384,256]{1,2,0:T(8,128)(2,1)S(1)}, u32[]{:S(2)}, u32[]{:S(2)}) collective-permute-start(bf16[6,384,256]{1,2,0:T(8,128)(2,1)S(1)} %pad_maximum_fusion), channel_id=1, source_target_pairs={{0,16},{1,17},{2,18},{3,19},{4,20},{5,21},{6,22},{7,23}} | collective-permute-start | bytes 3538952 | tf_op jit(solution)/shard_map/ppermute | solution.py:78
  13.4 32.2 %collective-permute-start.1 = (bf16[4,384,256]{1,2,0:T(8,128)(2,1)}, bf16[4,384,256]{1,2,0:T(8,128)(2,1)}, u32[]{:S(2)}, u32[]{:S(2)}) collective-permute-start(bf16[4,384,256]{1,2,0:T(8,128)(2,1)} %get-tuple-element.8), channel_id=1, source_target_pairs={{0,8},{1,9},{2,10},{3,11},{4,12},{5,13},{6,14},{7,15}} | collective-permute-start | bytes 2359304 | tf_op jit(solution)/shard_map/ppermute | solution.py:78
  17.0 22.7 %collective-permute-start.6 = (bf16[256,512]{1,0:T(8,128)(2,1)S(1)}, bf16[256,512]{1,0:T(8,128)(2,1)S(1)}, u32[]{:S(2)}, u32[]{:S(2)}) collective-permute-start(bf16[256,512]{1,0:T(8,128)(2,1)S(1)} %get-tuple-element.10), channel_id=1, source_target_pairs={{0,1},{1,0},{2,3},{3,2},{4,5},{5,4},{6,7},{7,6},{8,9},{9,8},{10,11... | collective-permute-start | bytes 786440 | tf_op jit(solution)/shard_map/ppermute | solution.py:81
  17.1 28.6 %collective-permute-start.3 = (bf16[2,384,256]{1,2,0:T(8,128)(2,1)}, bf16[2,384,256]{1,2,0:T(8,128)(2,1)S(1)}, u32[]{:S(2)}, u32[]{:S(2)}) collective-permute-start(bf16[2,384,256]{1,2,0:T(8,128)(2,1)} %get-tuple-element.5), channel_id=1, source_target_pairs={{0,24},{1,25},{2,26},{3,27},{4,28},{5,29},{6,30},{7,31}} | collective-permute-start | bytes 1179656 | tf_op jit(solution)/shard_map/ppermute | solution.py:78
  38.9 1.0 %copy-start.4 = (bf16[6,384,256]{1,2,0:T(8,128)(2,1)}, bf16[6,384,256]{1,2,0:T(8,128)(2,1)S(1)}, u32[]{:S(2)}) copy-start(bf16[6,384,256]{1,2,0:T(8,128)(2,1)S(1)} %collective-permute-done.2) | copy-start | bytes 3538948
  39.0 6.7 %collective-permute-start.4 = (bf16[2,384,256]{1,2,0:T(8,128)(2,1)S(1)}, bf16[2,384,256]{1,2,0:T(8,128)(2,1)S(1)}, u32[]{:S(2)}, u32[]{:S(2)}) collective-permute-start(bf16[2,384,256]{1,2,0:T(8,128)(2,1)S(1)} %slice.42), channel_id=1, source_target_pairs={{16,24},{17,25},{18,26},{19,27},{20,28},{21,29},{22,30},{23,31}} | collective-permute-start | bytes 1179656 | tf_op jit(solution)/shard_map/ppermute | solution.py:78
  40.8 14.5 %collective-permute-start.7 = (bf16[512,512]{1,0:T(8,128)(2,1)}, bf16[512,512]{1,0:T(8,128)(2,1)S(1)}, u32[]{:S(2)}, u32[]{:S(2)}) collective-permute-start(bf16[512,512]{1,0:T(8,128)(2,1)} %pad_maximum_fusion.1), channel_id=1, source_target_pairs={{0,2},{1,3},{2,4},{3,5},{4,6},{5,7},{8,10},{9,11},{10,12},{11,13},... | collective-permute-start | bytes 1572872 | tf_op jit(solution)/shard_map/ppermute | solution.py:78
  44.3 15.0 %collective-permute-start.8 = (bf16[512,512]{1,0:T(8,128)(2,1)}, bf16[512,512]{1,0:T(8,128)(2,1)S(1)}, u32[]{:S(2)}, u32[]{:S(2)}) collective-permute-start(bf16[512,512]{1,0:T(8,128)(2,1)} %pad_maximum_fusion.1), channel_id=1, source_target_pairs={{2,0},{3,1},{4,2},{5,3},{6,4},{7,5},{10,8},{11,9},{12,10},{13,11},... | collective-permute-start | bytes 1572872 | tf_op jit(solution)/shard_map/ppermute | solution.py:78
  47.2 17.1 %copy-start.6 = (s32[6]{0:T(128)S(1)}, s32[6]{0:T(128)}, u32[]{:S(2)}) copy-start(s32[6]{0:T(128)} %param.8) | copy-start | bytes 76
  47.2 26.8 %collective-permute-start.5 = (bf16[4,384,256]{1,2,0:T(8,128)(2,1)S(1)}, bf16[4,384,256]{1,2,0:T(8,128)(2,1)S(1)}, u32[]{:S(2)}, u32[]{:S(2)}) collective-permute-start(bf16[4,384,256]{1,2,0:T(8,128)(2,1)S(1)} %fusion.14), channel_id=1, source_target_pairs={{0,1},{1,0},{2,3},{3,2},{4,5},{5,4},{6,7},{7,6},{8,9},{9,8},{10,11... | collective-permute-start | bytes 2359304 | tf_op jit(solution)/shard_map/ppermute | solution.py:81
  55.3 7.6 %copy-start.1 = (bf16[512,512]{1,0:T(8,128)(2,1)}, bf16[512,512]{1,0:T(8,128)(2,1)S(1)}, u32[]{:S(2)}) copy-start(bf16[512,512]{1,0:T(8,128)(2,1)S(1)} %collective-permute-done.7) | copy-start | bytes 1572868
  59.3 3.6 %copy-start.2 = (bf16[512,512]{1,0:T(8,128)(2,1)}, bf16[512,512]{1,0:T(8,128)(2,1)S(1)}, u32[]{:S(2)}) copy-start(bf16[512,512]{1,0:T(8,128)(2,1)S(1)} %collective-permute-done.8) | copy-start | bytes 1572868
  60.3 12.4 %collective-permute-start.9 = (bf16[512,512]{1,0:T(8,128)(2,1)}, bf16[512,512]{1,0:T(8,128)(2,1)}, u32[]{:S(2)}, u32[]{:S(2)}) collective-permute-start(bf16[512,512]{1,0:T(8,128)(2,1)} %select_select_fusion), channel_id=1, source_target_pairs={{0,4},{1,5},{6,2},{7,3},{4,6},{5,7},{2,0},{3,1},{8,12},{9,13},{14,... | collective-permute-start | bytes 1572872 | tf_op jit(solution)/shard_map/ppermute | solution.py:78
  64.4 11.1 %copy-start.3 = (bf16[512,512]{1,0:T(8,128)(2,1)S(1)}, bf16[512,512]{1,0:T(8,128)(2,1)}, u32[]{:S(2)}) copy-start(bf16[512,512]{1,0:T(8,128)(2,1)} %copy-done.2) | copy-start | bytes 1572868
  72.7 13.2 %collective-permute-start.10 = (bf16[512,512]{1,0:T(8,128)(2,1)}, bf16[512,512]{1,0:T(8,128)(2,1)S(1)}, u32[]{:S(2)}, u32[]{:S(2)}) collective-permute-start(bf16[512,512]{1,0:T(8,128)(2,1)} %collective-permute-done.9), channel_id=1, source_target_pairs={{4,6},{5,7},{2,0},{3,1},{12,14},{13,15},{10,8},{11,9},{20,22},{21,... | collective-permute-start | bytes 1572872 | tf_op jit(solution)/shard_map/ppermute | solution.py:78
  86.3 10.1 %collective-permute-start.11 = (bf16[128,512]{1,0:T(8,128)(2,1)S(1)}, bf16[128,512]{1,0:T(8,128)(2,1)S(1)}, u32[]{:S(2)}, u32[]{:S(2)}) collective-permute-start(bf16[128,512]{1,0:T(8,128)(2,1)S(1)} %get-tuple-element.11), channel_id=1, source_target_pairs={{0,8},{1,9},{2,10},{3,11},{4,12},{5,13},{6,14},{7,15},{16,24},{17,... | collective-permute-start | bytes 393224 | tf_op jit(solution)/shard_map/ppermute | solution.py:78
  87.6 8.8 %collective-permute-start.12 = (bf16[128,512]{1,0:T(8,128)(2,1)S(1)}, bf16[128,512]{1,0:T(8,128)(2,1)S(1)}, u32[]{:S(2)}, u32[]{:S(2)}) collective-permute-start(bf16[128,512]{1,0:T(8,128)(2,1)S(1)} %get-tuple-element.13), channel_id=1, source_target_pairs={{0,16},{1,17},{2,18},{3,19},{4,20},{5,21},{6,22},{7,23},{8,24},{9,... | collective-permute-start | bytes 393224 | tf_op jit(solution)/shard_map/ppermute | solution.py:78
  93.0 5.9 %collective-permute-start.13 = (bf16[128,512]{1,0:T(8,128)(2,1)S(1)}, bf16[128,512]{1,0:T(8,128)(2,1)S(1)}, u32[]{:S(2)}, u32[]{:S(2)}) collective-permute-start(bf16[128,512]{1,0:T(8,128)(2,1)S(1)} %get-tuple-element.12), channel_id=1, source_target_pairs={{0,24},{1,25},{2,26},{3,27},{4,28},{5,29},{6,30},{7,31},{8,16},{9,... | collective-permute-start | bytes 393224 | tf_op jit(solution)/shard_map/ppermute | solution.py:78

commit v2 on v0

v2 whole, which is shorter than its diff:
```python
import jax
import jax.numpy as jnp
from jax import lax
from jax.experimental import pallas as pl
from jax.experimental.pallas import tpu as pltpu
from jax.sharding import PartitionSpec as P

D = 8192
HD = 128
KVH = 4
QH = 32
TILE_TOK = 16
SAMP = 2
TXT_S = 128
CAP = 64
AXES = ("grp", "fsdp", "tp")
VMEM = pl.BlockSpec(memory_space=pltpu.VMEM)
SMEM = pl.BlockSpec(memory_space=pltpu.SMEM)
ANY = pl.BlockSpec(memory_space=pl.ANY)
HBM = pl.BlockSpec(memory_space=pltpu.HBM)
LIMIT = 16 * 1024 * 1024
COST = 10


def attend_any(kv, tiles, queries, group):
    local_kv = kv.shape[1]
    groups_q = QH // KVH
    kv = kv.reshape(SAMP, CAP, local_kv, 2 * HD)
    keys = kv[..., :HD]
    values = kv[..., HD:]
    query = queries.reshape(SAMP, TXT_S, local_kv, groups_q, HD)
    counts = lax.dynamic_slice_in_dim(tiles, jnp.maximum(group - 1, 0) * SAMP, SAMP) * TILE_TOK
    live = jnp.arange(CAP)[None, :] < counts[:, None]
    scores = jnp.einsum("sikgd,sjkd->skgij", query, keys, preferred_element_type=jnp.float32) * (
        1.0 / HD**0.5
    )
    scores = jnp.where(live[:, None, None, None, :], scores, -1e30)
    top = jnp.max(scores, axis=-1, keepdims=True)
    expo = jnp.exp(scores - top)
    weights = (expo / jnp.sum(expo, axis=-1, keepdims=True)).astype(jnp.bfloat16)
    out = jnp.einsum(
        "skgij,sjkd->sikgd", weights, values, preferred_element_type=jnp.float32
    ).astype(jnp.bfloat16)
    out = jnp.where(group > 0, out, jnp.zeros_like(out))
    return out.reshape(queries.shape[0], queries.shape[1])


def shards_any(image_rows, enc_gain, key_value_w, tiles, queries):
    group = lax.axis_index("grp")
    per_group = image_rows.shape[0] // 3
    heads_kv = key_value_w.shape[1] // (2 * HD)
    rows = image_rows.astype(jnp.float32)
    squares = lax.psum(jnp.sum(rows * rows, axis=1, keepdims=True), "tp")
    normed = (rows * lax.rsqrt(squares / D + 1e-05) * enc_gain.astype(jnp.float32)).astype(
        jnp.bfloat16
    )
    parts = normed.reshape((3, per_group, normed.shape[1]))
    slots = jnp.concatenate([jnp.zeros_like(parts[:1]), parts], axis=0)
    mine = lax.all_to_all(slots, "grp", split_axis=0, concat_axis=0, tiled=True)[0]
    total = jnp.dot(
        mine,
        lax.all_gather(key_value_w, "fsdp", axis=0, tiled=True),
        preferred_element_type=jnp.float32,
    )
    heads = lax.psum_scatter(
        total.reshape(per_group, heads_kv, 2 * HD), "tp", scatter_dimension=1, tiled=True
    )
    return attend_any(heads.astype(jnp.bfloat16), tiles, queries, group)


def call(body, outs, *args, specs=None, cost=None):
    outs = [jax.ShapeDtypeStruct(s, d) for s, d in outs]
    if cost is not None:
        cost = pl.CostEstimate(flops=cost * 10**9, bytes_accessed=0, transcendentals=0)
    return pl.pallas_call(
        body,
        out_shape=outs,
        in_specs=specs or [SMEM] + [VMEM] * (len(args) - 1),
        out_specs=[VMEM] * len(outs),
        cost_estimate=cost,
        compiler_params=pltpu.CompilerParams(vmem_limit_bytes=LIMIT),
    )(*args)


def join(kept, other, out):
    rows = kept.shape[0]
    out[:rows, :] = kept[...]
    out[rows:, :] = other[...]


def normalise(place, x, squares, other, gain, a, b, c, d_low, d_high):
    width = x.shape[1] // 16

    @pl.when(place[0] == 0)
    def _():
        scale = lax.rsqrt((squares[...] + other[...]) / D + 1e-05)
        for z in range(4):
            for h in range(4):
                cols = slice((z * 4 + h) * width, (z * 4 + h + 1) * width)
                y = x[:, cols].astype(jnp.float32) * scale * gain[:, cols].astype(jnp.float32)
                out, at = ((a, b, c)[h], z) if h < 3 else ((d_low, d_high)[z // 2], z % 2)
                out[at] = y.astype(jnp.bfloat16)


def onward(place, own, below, above, out):
    f = place[1]

    @pl.when((f == 0) | (f == 3))
    def _():
        out[...] = own[...]

    @pl.when(f == 1)
    def _():
        out[...] = above[...]

    @pl.when(f == 2)
    def _():
        out[...] = below[...]


def later(x, after, out):
    del after
    out[...] = x[...]


def landed(place, a, b, c, d_low, d_high, low, high):
    g = place[0]
    for who, source in ((0, a), (1, b), (2, c)):

        @pl.when(g == who)
        def _(source=source):
            low[...] = source[:2]
            high[...] = source[2:]

    @pl.when(g == 3)
    def _():
        low[...] = d_low[...]
        high[...] = d_high[...]


def product(rows, others, plane, w):
    low, high = rows
    other_low, other_high = others
    depth = low.shape[2]

    def pick(low, high):
        return jnp.where(plane < 2, low[plane % 2], high[plane % 2])

    x = jnp.dot(pick(low, high), w[:depth, :], preferred_element_type=jnp.float32)
    return x + jnp.dot(
        pick(other_low, other_high), w[depth:, :], preferred_element_type=jnp.float32
    )


def products(place, own, below, above, two, three, low, high, other_low, other_high, out):
    f, rows, other = place[1], (low, high), (other_low, other_high)
    total = (
        product(rows, other, f, own)
        + product(rows, other, jnp.maximum(f - 1, 0), below)
        + product(rows, other, jnp.minimum(f + 1, 3), above)
        + product(rows, other, f ^ 2, two)
        + product(rows, other, 3 - f, three)
    )
    out[1:] = total.reshape(3, -1, total.shape[1]).astype(jnp.bfloat16)


def attention(place, tiles, parts, q_ref, out_ref):
    g = place[0]
    groups_q = QH // KVH

    @pl.when(g == 0)
    def _():
        out_ref[...] = jnp.zeros_like(out_ref)

    @pl.when(g > 0)
    def _():
        kv = parts[0].astype(jnp.float32)
        for h in range(1, 4):
            kv = kv + parts[h].astype(jnp.float32)
        kv = kv.astype(jnp.bfloat16)
        slot = lax.broadcasted_iota(jnp.int32, (1, CAP), 1)
        for s in range(SAMP):
            live = slot < tiles[(g - 1) * SAMP + s] * TILE_TOK
            rows = slice(s * TXT_S, s * TXT_S + TXT_S)
            for k in range(kv.shape[1] // (2 * HD)):
                block = kv[s * CAP : s * CAP + CAP, k * 2 * HD : (k + 1) * 2 * HD]
                heads = [
                    slice((k * groups_q + j) * HD, (k * groups_q + j + 1) * HD)
                    for j in range(groups_q)
                ]
                query = jnp.concatenate([q_ref[rows, h] for h in heads], axis=0)
                scores = lax.dot_general(
                    query,
                    block[:, :HD],
                    (((1,), (1,)), ((), ())),
                    preferred_element_type=jnp.float32,
                ) * (1.0 / HD**0.5)
                scores = jnp.where(live, scores, -1e30)
                expo = jnp.exp(scores - jnp.max(scores, axis=-1, keepdims=True))
                weights = (expo / jnp.sum(expo, axis=-1, keepdims=True)).astype(jnp.bfloat16)
                out = jnp.dot(weights, block[:, HD:], preferred_element_type=jnp.float32)
                for j, h in enumerate(heads):
                    out_ref[rows, h] = out[j * TXT_S : (j + 1) * TXT_S].astype(jnp.bfloat16)


def shards_line(image_rows, enc_gain, key_value_w, tiles, queries):
    g, f, t = (lax.axis_index(a) for a in AXES)
    place = jnp.stack([g, f, t]).astype(jnp.int32)
    n_rows = image_rows.shape[0]
    per_group = n_rows // 3
    half = key_value_w.shape[1] // 2
    quarter = key_value_w.shape[0] // 4
    bf16, f32 = jnp.bfloat16, jnp.float32
    planes = range(4)

    def send(x, pairs):
        index = lambda p, c: (p[0] * 4 + p[1]) * 2 + c
        return lax.ppermute(x, AXES, [(index(a, c), index(b, c)) for a, b in pairs for c in (0, 1)])

    def swap(x):
        return lax.ppermute(x, "tp", [(0, 1), (1, 0)])

    w = lax.dynamic_slice_in_dim(key_value_w, g * quarter, quarter, axis=0)
    kept = lax.dynamic_slice_in_dim(w, t * half, half, axis=1)
    given = lax.dynamic_slice_in_dim(w, (1 - t) * half, half, axis=1)
    shape = (2 * quarter, half)
    own = call(join, [(shape, bf16)], kept, swap(given), specs=[VMEM, VMEM])[0]
    below = send(own, [((c, z), (c, z + 1)) for c in range(4) for z in range(3)])
    above = send(own, [((c, z + 1), (c, z)) for c in range(4) for z in range(3)])
    ready = call(onward, [(shape, bf16)], place, own, below, above, cost=COST)[0]
    pairs = ((0, 2), (3, 1), (2, 3), (1, 0))
    two = send(ready, [((c, a), (c, b)) for c in range(4) for a, b in pairs])
    three = send(two, [((c, a), (c, b)) for c in range(4) for a, b in pairs[2:]])

    x = image_rows.astype(f32)
    squares = jnp.sum(x * x, axis=1, keepdims=True)
    whole, part = ((4, n_rows, quarter), bf16), ((2, n_rows, quarter), bf16)
    a, b, c, d_low, d_high = call(
        normalise,
        [whole] * 3 + [part] * 2,
        place,
        image_rows,
        squares,
        swap(squares),
        enc_gain.reshape(1, -1),
    )
    to_b, to_c, to_d = ([((0, z), (h, z)) for z in planes] for h in (1, 2, 3))
    d_low, d_high = send(d_low, to_d), send(d_high, to_c)
    b, c = send(b, to_b), send(c, to_c)
    d_high = call(later, [part], d_high, ready, specs=[VMEM, ANY])[0]
    d_high = send(d_high, [((2, z), (3, z)) for z in planes])
    rows = call(landed, [part] * 2, place, a, b, c, d_low, d_high)
    rows = (*rows, *[swap(x) for x in rows])

    parts = ((4, per_group, half), bf16)
    parts = call(products, [parts], place, own, below, above, two, three, *rows)[0]
    parts = lax.all_to_all(parts, "grp", 0, 0, tiled=True)
    specs = [SMEM, SMEM, VMEM, VMEM]
    return call(attention, [(queries.shape, bf16)], place, tiles, parts, queries, specs=specs)[0]


def solution(mesh):
    sizes = tuple(mesh.shape[a] for a in AXES)
    return jax.shard_map(
        shards_line if sizes == (4, 4, 2) else shards_any,
        mesh=mesh,
        in_specs=(
            P(("grp", "fsdp"), "tp"),
            P("tp"),
            P(("tp", "fsdp"), None),
            P("fsdp"),
            P(("grp", "fsdp"), "tp"),
        ),
        out_specs=P(("grp", "fsdp"), "tp"),
        check_vma=False,
    )
```

time: 199 us -> 68.8 us (0.35)
  waiting for transfers between devices: 146 us -> 23.3 us
  starting transfers between devices: 5.05 us -> 21.2 us
  local copies, waits for them, and re-layouts: 16.5 us -> 1.65 us
  between operations: 13.5 us -> 0.18 us
  Pallas kernels: 0 us -> 8.81 us
  matrix products: 8.47 us -> 0 us
  blocking collectives: 2.58 us -> 10.6 us
  other arithmetic: 5.88 us -> 2.66 us
    all_gather x1 -> x0, waiting for transfers between devices: 139 us -> none  [shards(): lax.all_gather(key_value_w, 'fsdp', axis=0, tiled=True)]
    ppermute x0 -> x13, waiting for transfers between devices: none -> 23.3 us  [the longest x9 19.1 us: send(): lax.ppermute(x, AXES, [(index(a, c), index(b, c)) for a, b in pairs for c...]
    ppermute x0 -> x13, starting transfers between devices: none -> 21.2 us  [the longest x9 20 us: send(): lax.ppermute(x, AXES, [(index(a, c), index(b, c)) for a, b in pairs for c...]
    dot_general x1 -> x0, local copies, waits for them, and re-layouts: 11.5 us -> none  [fold_rows(): return jnp.dot(rows, piece, preferred_element_type=jnp.float32)]
    all_to_all x0 -> x1, blocking collectives: none -> 10.6 us  [shards_line(): parts = lax.all_to_all(parts, 'grp', 0, 0, tiled=True)]
    pallas_call x0 -> x7, Pallas kernels: none -> 8.81 us  [call(): pl.pallas_call(body, out_shape=outs, in_specs=specs or [SMEM] + [VMEM] *...]
    dot_general x3 -> x0, matrix products: 8.47 us -> none  [the longest x1 7.48 us: fold_rows(): return jnp.dot(rows, piece, preferred_element_type=jnp.float32)]
    reduce_scatter x1 -> x0, waiting for transfers between devices: 5.92 us -> none  [shards(): lax.psum_scatter(total.reshape(per_group, heads_kv, 2 * HD), 'tp', scatte...]
  transfers between devices with their start and end apart: 3 -> 13, of which waited for: 2 -> 8; matrix products, arithmetic and copies ran while one was open for 10% -> 4% of each run, Pallas kernels for 0% -> 6%
where the time goes in v2:
time: 68.8 us; the launch traced here: 68.4 us
  waiting for transfers between devices  23.3 us (34%)
  starting transfers between devices  21.2 us (31%)
  blocking collectives  10.6 us (15%)
  Pallas kernels  8.81 us (13%)
  other arithmetic  2.66 us (4%)
  local copies, waits for them, and re-layouts  1.65 us (2%)
    ppermute x9, starting transfers between devices, send(): lax.ppermute(x, AXES, [(index(a, c), index(b, c)) for a, b in pairs for c...  20 us
    ppermute x9, waiting for transfers between devices, send(): lax.ppermute(x, AXES, [(index(a, c), index(b, c)) for a, b in pairs for c...  19.1 us
    all_to_all x1, blocking collectives, shards_line(): parts = lax.all_to_all(parts, 'grp', 0, 0, tiled=True)  10.6 us
    pallas_call x7, Pallas kernels, call(): pl.pallas_call(body, out_shape=outs, in_specs=specs or [SMEM] + [VMEM] *...  8.81 us
    ppermute x4, waiting for transfers between devices, swap(): return lax.ppermute(x, 'tp', [(0, 1), (1, 0)])  4.26 us
    reduce_sum x1, other arithmetic, shards_line(): squares = jnp.sum(x * x, axis=1, keepdims=True)  2.58 us
    dynamic_slice x1, local copies, waits for them, and re-layouts, shards_line(): given = lax.dynamic_slice_in_dim(w, (1 - t) * half, half, axis=1)  1.51 us
  transfers between devices with their start and end apart: 13, of which 8 were waited for; matrix products, arithmetic and copies ran while one was open for 4% of the time, Pallas kernels for 6%

profile of v2, /device:TPU:0, one launch (start us, length us, event | category | flops | bytes accessed | tf_op | source)
XLA Modules:
  0.0 68.4 jit_solution(13795933714450743071)
XLA Ops:
  0.0 0.0 copy-start
  0.0 0.0 copy-start.3
  0.0 1.5 %fusion = (bf16[256,512]{1,0:T(8,128)(2,1)S(1)}, bf16[256,512]{1,0:T(8,128)(2,1)S(1)}) fusion(bf16[1024,1024]{1,0:T(8,128)(2,1)} %param.7, s32[]{:T(128)S(6)} %select_n.16, s32[]{:T(128)S(6)} %select_n.20, s32[]{:T(128)S(6)} %select_n.18), kind=kLoop, calls=%fused_computation.2 | loop fusion | bytes 1048588 | tf_op jit(solution)/shard_map/dynamic_slice | solution.py:225
  1.5 0.5 collective-permute-start
  2.0 1.2 %collective-permute-done.other = bf16[256,512]{1,0:T(8,128)(2,1)S(1)} collective-permute-done((bf16[256,512]{1,0:T(8,128)(2,1)S(1)}, bf16[256,512]{1,0:T(8,128)(2,1)S(1)}, u32[]{:S(2)}, u32[]{:S(2)}) %collective-permute-start) | collective-permute-done | bytes 262176 | tf_op jit(solution)/shard_map/ppermute | solution.py:221
  3.2 0.8 %shard_map.55.own = bf16[512,512]{1,0:T(8,128)(2,1)} custom-call(bf16[256,512]{1,0:T(8,128)(2,1)S(1)} %get-tuple-element.20.kept, bf16[256,512]{1,0:T(8,128)(2,1)S(1)} %collective-permute-done.other), custom_call_target="tpu_custom_call" | custom-call | tf_op jit(solution)/shard_map/pallas_call | solution.py:75
  4.0 5.6 %collective-permute-start.1 = (bf16[512,512]{1,0:T(8,128)(2,1)}, bf16[512,512]{1,0:T(8,128)(2,1)}, u32[]{:S(2)}, u32[]{:S(2)}) collective-permute-start(bf16[512,512]{1,0:T(8,128)(2,1)} %shard_map.55.own), channel_id=1, source_target_pairs={{0,2},{1,3},{2,4},{3,5},{4,6},{5,7},{8,10},{9,11},{10,12},{11,13},... | collective-permute-start | bytes 1572872 | tf_op jit(solution)/shard_map/ppermute | solution.py:218
  9.7 1.3 %collective-permute-start.2 = (bf16[512,512]{1,0:T(8,128)(2,1)}, bf16[512,512]{1,0:T(8,128)(2,1)}, u32[]{:S(2)}, u32[]{:S(2)}) collective-permute-start(bf16[512,512]{1,0:T(8,128)(2,1)} %shard_map.55.own), channel_id=1, source_target_pairs={{2,0},{3,1},{4,2},{5,3},{6,4},{7,5},{10,8},{11,9},{12,10},{13,11},... | collective-permute-start | bytes 1572872 | tf_op jit(solution)/shard_map/ppermute | solution.py:218
  11.0 2.6 %multiply_reduce_fusion = f32[384]{0:T(512)S(1)} fusion(bf16[384,4096]{1,0:T(8,128)(2,1)} %x.1), kind=kLoop, calls=%fused_computation | loop fusion | flops 4718208 | bytes 3147264 | tf_op jit(solution)/shard_map/reduce_sum | solution.py:236
  13.5 0.1 broadcast_in_dim.4.squares
  13.7 0.1 collective-permute-start.5
  13.7 0.1 pad_add_fusion.place
  13.8 0.0 copy-done.3
  13.8 1.3 %collective-permute-done.5.other = f32[384,1]{1,0:T(8,128)S(1)} collective-permute-done((f32[384,1]{1,0:T(8,128)S(1)}, f32[384,1]{1,0:T(8,128)S(1)}, u32[]{:S(2)}, u32[]{:S(2)}) %collective-permute-start.5) | collective-permute-done | bytes 1568 | tf_op jit(solution)/shard_map/ppermute | solution.py:221
  15.2 0.0 copy-done
  15.2 1.8 %shard_map.57 = (bf16[4,384,256]{2,1,0:T(8,128)(2,1)S(1)}, bf16[4,384,256]{2,1,0:T(8,128)(2,1)S(1)}, bf16[4,384,256]{2,1,0:T(8,128)(2,1)S(1)}, bf16[2,384,256]{2,1,0:T(8,128)(2,1)S(1)}, bf16[2,384,256]{2,1,0:T(8,128)(2,1)S(1)}) custom-call(s32[3]{0:T(128)S(1)} %pad_add_fusion.place, bf16[384,4096]{1,0:T(8,128)(2,1)S(1)} %copy-done, ...), custom_call_target="tpu_custom_call" | custom-call | tf_op jit(solution)/shard_map/pallas_call | solution.py:75
  17.0 2.2 %collective-permute-start.9 = (bf16[2,384,256]{2,1,0:T(8,128)(2,1)S(1)}, bf16[2,384,256]{2,1,0:T(8,128)(2,1)S(1)}, u32[]{:S(2)}, u32[]{:S(2)}) collective-permute-start(bf16[2,384,256]{2,1,0:T(8,128)(2,1)S(1)} %get-tuple-element.16), channel_id=1, source_target_pairs={{0,16},{1,17},{2,18},{3,19},{4,20},{5,21},{6,22},{7,23}} | collective-permute-start | bytes 1179656 | tf_op jit(solution)/shard_map/ppermute | solution.py:218
  19.2 1.3 %collective-permute-start.6 = (bf16[4,384,256]{2,1,0:T(8,128)(2,1)S(1)}, bf16[4,384,256]{2,1,0:T(8,128)(2,1)S(1)}, u32[]{:S(2)}, u32[]{:S(2)}) collective-permute-start(bf16[4,384,256]{2,1,0:T(8,128)(2,1)S(1)} %get-tuple-element.13), channel_id=1, source_target_pairs={{0,8},{1,9},{2,10},{3,11},{4,12},{5,13},{6,14},{7,15}} | collective-permute-start | bytes 2359304 | tf_op jit(solution)/shard_map/ppermute | solution.py:218
  20.5 1.3 %collective-permute-start.7 = (bf16[4,384,256]{2,1,0:T(8,128)(2,1)S(1)}, bf16[4,384,256]{2,1,0:T(8,128)(2,1)S(1)}, u32[]{:S(2)}, u32[]{:S(2)}) collective-permute-start(bf16[4,384,256]{2,1,0:T(8,128)(2,1)S(1)} %get-tuple-element.14), channel_id=1, source_target_pairs={{0,16},{1,17},{2,18},{3,19},{4,20},{5,21},{6,22},{7,23}} | collective-permute-start | bytes 2359304 | tf_op jit(solution)/shard_map/ppermute | solution.py:218
  21.9 0.0 collective-permute-done.1.below
  21.9 3.7 %collective-permute-done.2.above = bf16[512,512]{1,0:T(8,128)(2,1)} collective-permute-done((bf16[512,512]{1,0:T(8,128)(2,1)}, bf16[512,512]{1,0:T(8,128)(2,1)}, u32[]{:S(2)}, u32[]{:S(2)}) %collective-permute-start.2) | collective-permute-done | bytes 524320 | tf_op jit(solution)/shard_map/ppermute | solution.py:218
  25.6 1.4 %shard_map.56.after = bf16[512,512]{1,0:T(8,128)(2,1)S(1)} custom-call(s32[3]{0:T(128)S(1)} %pad_add_fusion.place, bf16[512,512]{1,0:T(8,128)(2,1)} %shard_map.55.own, bf16[512,512]{1,0:T(8,128)(2,1)} %collective-permute-done.1.below, bf16[512,512]{1,0:T(8,128)(2,1)} %collective-permute-done.2.above), custom_call_target="tpu_custom_call" | custom-call | flops 10000000000 | tf_op jit(solution)/shard_map/pallas_call | solution.py:75
  27.0 1.9 %collective-permute-start.3 = (bf16[512,512]{1,0:T(8,128)(2,1)S(1)}, bf16[512,512]{1,0:T(8,128)(2,1)S(1)}, u32[]{:S(2)}, u32[]{:S(2)}) collective-permute-start(bf16[512,512]{1,0:T(8,128)(2,1)S(1)} %shard_map.56.after), channel_id=1, source_target_pairs={{0,4},{1,5},{6,2},{7,3},{4,6},{5,7},{2,0},{3,1},{8,12},{9,13},{14,... | collective-permute-start | bytes 1572872 | tf_op jit(solution)/shard_map/ppermute | solution.py:218
  28.8 4.4 %collective-permute-start.8 = (bf16[2,384,256]{2,1,0:T(8,128)(2,1)S(1)}, bf16[2,384,256]{2,1,0:T(8,128)(2,1)S(1)}, u32[]{:S(2)}, u32[]{:S(2)}) collective-permute-start(bf16[2,384,256]{2,1,0:T(8,128)(2,1)S(1)} %get-tuple-element.15), channel_id=1, source_target_pairs={{0,24},{1,25},{2,26},{3,27},{4,28},{5,29},{6,30},{7,31}} | collective-permute-start | bytes 1179656 | tf_op jit(solution)/shard_map/ppermute | solution.py:218
  33.2 0.0 collective-permute-done.9.x
  33.3 0.7 %collective-permute-start.10 = (bf16[2,384,256]{2,1,0:T(8,128)(2,1)S(1)}, bf16[2,384,256]{2,1,0:T(8,128)(2,1)S(1)}, u32[]{:S(2)}, u32[]{:S(2)}) collective-permute-start(bf16[2,384,256]{2,1,0:T(8,128)(2,1)S(1)} %shard_map.58), channel_id=1, source_target_pairs={{16,24},{17,25},{18,26},{19,27},{20,28},{21,29},{22,30},{23,31}} | collective-permute-start | bytes 1179656 | tf_op jit(solution)/shard_map/ppermute | solution.py:218
  33.9 5.9 %collective-permute-done.3.two = bf16[512,512]{1,0:T(8,128)(2,1)S(1)} collective-permute-done((bf16[512,512]{1,0:T(8,128)(2,1)S(1)}, bf16[512,512]{1,0:T(8,128)(2,1)S(1)}, u32[]{:S(2)}, u32[]{:S(2)}) %collective-permute-start.3) | collective-permute-done | bytes 524320 | tf_op jit(solution)/shard_map/ppermute | solution.py:218
  39.8 1.3 %collective-permute-start.4 = (bf16[512,512]{1,0:T(8,128)(2,1)S(1)}, bf16[512,512]{1,0:T(8,128)(2,1)S(1)}, u32[]{:S(2)}, u32[]{:S(2)}) collective-permute-start(bf16[512,512]{1,0:T(8,128)(2,1)S(1)} %collective-permute-done.3.two), channel_id=1, source_target_pairs={{4,6},{5,7},{2,0},{3,1},{12,14},{13,15},{10,8},{11,9},{20,22},{21,... | collective-permute-start | bytes 1572872 | tf_op jit(solution)/shard_map/ppermute | solution.py:218
  41.1 4.9 %collective-permute-done.8.d_low = bf16[2,384,256]{2,1,0:T(8,128)(2,1)S(1)} collective-permute-done((bf16[2,384,256]{2,1,0:T(8,128)(2,1)S(1)}, bf16[2,384,256]{2,1,0:T(8,128)(2,1)S(1)}, u32[]{:S(2)}, u32[]{:S(2)}) %collective-permute-start.8) | collective-permute-done | bytes 393248 | tf_op jit(solution)/shard_map/ppermute | solution.py:218
  46.0 0.0 collective-permute-done.6.b
  46.0 0.0 collective-permute-done.7.c
  46.0 0.0 collective-permute-done.10.d_high
  46.0 0.6 shard_map.59
  46.6 0.0 copy-start.1
  46.6 0.0 copy-start.2
  46.6 0.1 collective-permute-start.11
  46.7 0.5 collective-permute-start.12
  47.2 1.2 %collective-permute-done.11.other_low = bf16[2,384,256]{2,1,0:T(8,128)(2,1)S(1)} collective-permute-done((bf16[2,384,256]{2,1,0:T(8,128)(2,1)S(1)}, bf16[2,384,256]{2,1,0:T(8,128)(2,1)S(1)}, u32[]{:S(2)}, u32[]{:S(2)}) %collective-permute-start.11) | collective-permute-done | bytes 393248 | tf_op jit(solution)/shard_map/ppermute | solution.py:221
  48.4 0.6 collective-permute-done.12.other_high
  49.0 4.6 %collective-permute-done.4.three = bf16[512,512]{1,0:T(8,128)(2,1)S(1)} collective-permute-done((bf16[512,512]{1,0:T(8,128)(2,1)S(1)}, bf16[512,512]{1,0:T(8,128)(2,1)S(1)}, u32[]{:S(2)}, u32[]{:S(2)}) %collective-permute-start.4) | collective-permute-done | bytes 524320 | tf_op jit(solution)/shard_map/ppermute | solution.py:218
  53.6 2.6 %shard_map.60 = bf16[4,128,512]{2,1,0:T(8,128)(2,1)S(1)} custom-call(s32[3]{0:T(128)S(1)} %pad_add_fusion.place, bf16[512,512]{1,0:T(8,128)(2,1)} %shard_map.55.own, bf16[512,512]{1,0:T(8,128)(2,1)} %collective-permute-done.1.below, bf16[512,512]{1,0:T(8,128)(2,1)} %collective-permute-done.2.above, bf16[512,512]{1,0:T(8,128)(2,1)S(1)} %collective-permute-done.3.two, ...), custom_call_target="tpu_custom_call" | custom-call | tf_op jit(solution)/shard_map/pallas_call | solution.py:75
  56.2 10.6 %all_to_all.5.parts = bf16[4,128,512]{2,1,0:T(8,128)(2,1)S(1)} all-to-all(bf16[4,128,512]{2,1,0:T(8,128)(2,1)S(1)} %shard_map.60), channel_id=1, replica_groups=mesh['grp'=4,'fsdp'=4,'tp'=2] {'grp'}, dimensions={0} | all-to-all | bytes 1048576 | tf_op jit(solution)/shard_map/all_to_all | solution.py:257
  66.8 0.0 copy-done.1
  66.8 0.0 copy-done.2
  66.8 1.6 %shard_map.61 = bf16[256,2048]{1,0:T(8,128)(2,1)} custom-call(s32[3]{0:T(128)S(1)} %pad_add_fusion.place, s32[6]{0:T(128)S(1)} %copy-done.2, bf16[4,128,512]{2,1,0:T(8,128)(2,1)S(1)} %all_to_all.5.parts, bf16[256,2048]{1,0:T(8,128)(2,1)S(1)} %copy-done.1), custom_call_target="tpu_custom_call" | custom-call | tf_op jit(solution)/shard_map/pallas_call | solution.py:75
  (2 shorter events, 0.0 us)
Async XLA Ops:
  0.0 15.2 %copy-start = (bf16[384,4096]{1,0:T(8,128)(2,1)S(1)}, bf16[384,4096]{1,0:T(8,128)(2,1)}, u32[]{:S(2)}) copy-start(bf16[384,4096]{1,0:T(8,128)(2,1)} %x.1) | copy-start | bytes 9437188
  0.0 13.8 %copy-start.3 = (bf16[4096]{0:T(1024)(128)(2,1)S(1)}, bf16[4096]{0:T(1024)(128)(2,1)}, u32[]{:S(2)}) copy-start(bf16[4096]{0:T(1024)(128)(2,1)} %param.6) | copy-start | bytes 24580
  1.5 1.7 %collective-permute-start = (bf16[256,512]{1,0:T(8,128)(2,1)S(1)}, bf16[256,512]{1,0:T(8,128)(2,1)S(1)}, u32[]{:S(2)}, u32[]{:S(2)}) collective-permute-start(bf16[256,512]{1,0:T(8,128)(2,1)S(1)} %get-tuple-element.19), channel_id=1, source_target_pairs={{0,1},{1,0},{2,3},{3,2},{4,5},{5,4},{6,7},{7,6},{8,9},{9,8},{10,11... | collective-permute-start | bytes 786440 | tf_op jit(solution)/shard_map/ppermute | solution.py:221
  4.0 17.8 %collective-permute-start.1 = (bf16[512,512]{1,0:T(8,128)(2,1)}, bf16[512,512]{1,0:T(8,128)(2,1)}, u32[]{:S(2)}, u32[]{:S(2)}) collective-permute-start(bf16[512,512]{1,0:T(8,128)(2,1)} %shard_map.55.own), channel_id=1, source_target_pairs={{0,2},{1,3},{2,4},{3,5},{4,6},{5,7},{8,10},{9,11},{10,12},{11,13},... | collective-permute-start | bytes 1572872 | tf_op jit(solution)/shard_map/ppermute | solution.py:218
  9.7 15.9 %collective-permute-start.2 = (bf16[512,512]{1,0:T(8,128)(2,1)}, bf16[512,512]{1,0:T(8,128)(2,1)}, u32[]{:S(2)}, u32[]{:S(2)}) collective-permute-start(bf16[512,512]{1,0:T(8,128)(2,1)} %shard_map.55.own), channel_id=1, source_target_pairs={{2,0},{3,1},{4,2},{5,3},{6,4},{7,5},{10,8},{11,9},{12,10},{13,11},... | collective-permute-start | bytes 1572872 | tf_op jit(solution)/shard_map/ppermute | solution.py:218
  13.7 1.5 %collective-permute-start.5 = (f32[384,1]{1,0:T(8,128)S(1)}, f32[384,1]{1,0:T(8,128)S(1)}, u32[]{:S(2)}, u32[]{:S(2)}) collective-permute-start(f32[384,1]{1,0:T(8,128)S(1)} %broadcast_in_dim.4.squares), channel_id=1, source_target_pairs={{0,1},{1,0},{2,3},{3,2},{4,5},{5,4},{6,7},{7,6},{8,9},{9,8},{10,11... | collective-permute-start | bytes 4616 | tf_op jit(solution)/shard_map/ppermute | solution.py:221
  17.0 16.2 %collective-permute-start.9 = (bf16[2,384,256]{2,1,0:T(8,128)(2,1)S(1)}, bf16[2,384,256]{2,1,0:T(8,128)(2,1)S(1)}, u32[]{:S(2)}, u32[]{:S(2)}) collective-permute-start(bf16[2,384,256]{2,1,0:T(8,128)(2,1)S(1)} %get-tuple-element.16), channel_id=1, source_target_pairs={{0,16},{1,17},{2,18},{3,19},{4,20},{5,21},{6,22},{7,23}} | collective-permute-start | bytes 1179656 | tf_op jit(solution)/shard_map/ppermute | solution.py:218
  19.2 26.8 %collective-permute-start.6 = (bf16[4,384,256]{2,1,0:T(8,128)(2,1)S(1)}, bf16[4,384,256]{2,1,0:T(8,128)(2,1)S(1)}, u32[]{:S(2)}, u32[]{:S(2)}) collective-permute-start(bf16[4,384,256]{2,1,0:T(8,128)(2,1)S(1)} %get-tuple-element.13), channel_id=1, source_target_pairs={{0,8},{1,9},{2,10},{3,11},{4,12},{5,13},{6,14},{7,15}} | collective-permute-start | bytes 2359304 | tf_op jit(solution)/shard_map/ppermute | solution.py:218
  20.5 25.5 %collective-permute-start.7 = (bf16[4,384,256]{2,1,0:T(8,128)(2,1)S(1)}, bf16[4,384,256]{2,1,0:T(8,128)(2,1)S(1)}, u32[]{:S(2)}, u32[]{:S(2)}) collective-permute-start(bf16[4,384,256]{2,1,0:T(8,128)(2,1)S(1)} %get-tuple-element.14), channel_id=1, source_target_pairs={{0,16},{1,17},{2,18},{3,19},{4,20},{5,21},{6,22},{7,23}} | collective-permute-start | bytes 2359304 | tf_op jit(solution)/shard_map/ppermute | solution.py:218
  27.0 12.9 %collective-permute-start.3 = (bf16[512,512]{1,0:T(8,128)(2,1)S(1)}, bf16[512,512]{1,0:T(8,128)(2,1)S(1)}, u32[]{:S(2)}, u32[]{:S(2)}) collective-permute-start(bf16[512,512]{1,0:T(8,128)(2,1)S(1)} %shard_map.56.after), channel_id=1, source_target_pairs={{0,4},{1,5},{6,2},{7,3},{4,6},{5,7},{2,0},{3,1},{8,12},{9,13},{14,... | collective-permute-start | bytes 1572872 | tf_op jit(solution)/shard_map/ppermute | solution.py:218
  28.8 17.1 %collective-permute-start.8 = (bf16[2,384,256]{2,1,0:T(8,128)(2,1)S(1)}, bf16[2,384,256]{2,1,0:T(8,128)(2,1)S(1)}, u32[]{:S(2)}, u32[]{:S(2)}) collective-permute-start(bf16[2,384,256]{2,1,0:T(8,128)(2,1)S(1)} %get-tuple-element.15), channel_id=1, source_target_pairs={{0,24},{1,25},{2,26},{3,27},{4,28},{5,29},{6,30},{7,31}} | collective-permute-start | bytes 1179656 | tf_op jit(solution)/shard_map/ppermute | solution.py:218
  33.3 12.7 %collective-permute-start.10 = (bf16[2,384,256]{2,1,0:T(8,128)(2,1)S(1)}, bf16[2,384,256]{2,1,0:T(8,128)(2,1)S(1)}, u32[]{:S(2)}, u32[]{:S(2)}) collective-permute-start(bf16[2,384,256]{2,1,0:T(8,128)(2,1)S(1)} %shard_map.58), channel_id=1, source_target_pairs={{16,24},{17,25},{18,26},{19,27},{20,28},{21,29},{22,30},{23,31}} | collective-permute-start | bytes 1179656 | tf_op jit(solution)/shard_map/ppermute | solution.py:218
  39.8 13.8 %collective-permute-start.4 = (bf16[512,512]{1,0:T(8,128)(2,1)S(1)}, bf16[512,512]{1,0:T(8,128)(2,1)S(1)}, u32[]{:S(2)}, u32[]{:S(2)}) collective-permute-start(bf16[512,512]{1,0:T(8,128)(2,1)S(1)} %collective-permute-done.3.two), channel_id=1, source_target_pairs={{4,6},{5,7},{2,0},{3,1},{12,14},{13,15},{10,8},{11,9},{20,22},{21,... | collective-permute-start | bytes 1572872 | tf_op jit(solution)/shard_map/ppermute | solution.py:218
  46.6 20.2 %copy-start.1 = (bf16[256,2048]{1,0:T(8,128)(2,1)S(1)}, bf16[256,2048]{1,0:T(8,128)(2,1)}, u32[]{:S(2)}) copy-start(bf16[256,2048]{1,0:T(8,128)(2,1)} %q_ref.1) | copy-start | bytes 3145732
  46.6 20.2 %copy-start.2 = (s32[6]{0:T(128)S(1)}, s32[6]{0:T(128)}, u32[]{:S(2)}) copy-start(s32[6]{0:T(128)} %tiles.1) | copy-start | bytes 76
  46.6 1.8 %collective-permute-start.11 = (bf16[2,384,256]{2,1,0:T(8,128)(2,1)S(1)}, bf16[2,384,256]{2,1,0:T(8,128)(2,1)S(1)}, u32[]{:S(2)}, u32[]{:S(2)}) collective-permute-start(bf16[2,384,256]{2,1,0:T(8,128)(2,1)S(1)} %get-tuple-element.17.low), channel_id=1, source_target_pairs={{0,1},{1,0},{2,3},{3,2},{4,5},{5,4},{6,7},{7,6},{8,9},{9,8},{10,11... | collective-permute-start | bytes 1179656 | tf_op jit(solution)/shard_map/ppermute | solution.py:221
  46.7 2.3 %collective-permute-start.12 = (bf16[2,384,256]{2,1,0:T(8,128)(2,1)S(1)}, bf16[2,384,256]{2,1,0:T(8,128)(2,1)S(1)}, u32[]{:S(2)}, u32[]{:S(2)}) collective-permute-start(bf16[2,384,256]{2,1,0:T(8,128)(2,1)S(1)} %get-tuple-element.18.high), channel_id=1, source_target_pairs={{0,1},{1,0},{2,3},{3,2},{4,5},{5,4},{6,7},{7,6},{8,9},{9,8},{10,11... | collective-permute-start | bytes 1179656 | tf_op jit(solution)/shard_map/ppermute | solution.py:221

commit v3 on v2

--- a/solution.py
+++ b/solution.py
@@ -68,7 +68,7 @@
     return attend_any(heads.astype(jnp.bfloat16), tiles, queries, group)
 
 
-def call(body, outs, *args, specs=None, cost=None):
+def call(body, outs, *args, specs=None, out_spec=VMEM, cost=None, scratch=()):
     outs = [jax.ShapeDtypeStruct(s, d) for s, d in outs]
     if cost is not None:
         cost = pl.CostEstimate(flops=cost * 10**9, bytes_accessed=0, transcendentals=0)
@@ -76,8 +76,9 @@
         body,
         out_shape=outs,
         in_specs=specs or [SMEM] + [VMEM] * (len(args) - 1),
-        out_specs=[VMEM] * len(outs),
+        out_specs=[out_spec] * len(outs),
         cost_estimate=cost,
+        scratch_shapes=list(scratch),
         compiler_params=pltpu.CompilerParams(vmem_limit_bytes=LIMIT),
     )(*args)
 
@@ -88,12 +89,23 @@
     out[rows:, :] = other[...]
 
 
+def row_squares(place, x, squares):
+    @pl.when(place[0] == 0)
+    def _():
+        total = None
+        for col in range(0, x.shape[1], 128):
+            part = x[:, col : col + 128].astype(jnp.float32)
+            total = part * part if total is None else total + part * part
+        squares[...] = total
+
+
 def normalise(place, x, squares, other, gain, a, b, c, d_low, d_high):
     width = x.shape[1] // 16
 
     @pl.when(place[0] == 0)
     def _():
-        scale = lax.rsqrt((squares[...] + other[...]) / D + 1e-05)
+        total = jnp.sum(squares[...] + other[...], axis=1, keepdims=True)
+        scale = lax.rsqrt(total / D + 1e-05)
         for z in range(4):
             for h in range(4):
                 cols = slice((z * 4 + h) * width, (z * 4 + h + 1) * width)
@@ -102,20 +114,16 @@
                 out[at] = y.astype(jnp.bfloat16)
 
 
-def onward(place, own, below, above, out):
-    f = place[1]
-
-    @pl.when((f == 0) | (f == 3))
-    def _():
-        out[...] = own[...]
-
-    @pl.when(f == 1)
-    def _():
-        out[...] = above[...]
-
-    @pl.when(f == 2)
-    def _():
-        out[...] = below[...]
+def onward(place, own, middle, near, out, sem):
+    del near
+    end = (place[1] == 0) | (place[1] == 3)
+    for use, source in ((end, own), (jnp.logical_not(end), middle)):
+
+        @pl.when(use)
+        def _(source=source):
+            copy = pltpu.make_async_copy(source, out, sem)
+            copy.start()
+            copy.wait()
 
 
 def later(x, after, out):
@@ -138,48 +146,79 @@
         high[...] = d_high[...]
 
 
-def product(rows, others, plane, w):
-    low, high = rows
-    other_low, other_high = others
-    depth = low.shape[2]
-
-    def pick(low, high):
-        return jnp.where(plane < 2, low[plane % 2], high[plane % 2])
-
-    x = jnp.dot(pick(low, high), w[:depth, :], preferred_element_type=jnp.float32)
-    return x + jnp.dot(
-        pick(other_low, other_high), w[depth:, :], preferred_element_type=jnp.float32
-    )
-
-
-def products(place, own, below, above, two, three, low, high, other_low, other_high, out):
-    f, rows, other = place[1], (low, high), (other_low, other_high)
-    total = (
-        product(rows, other, f, own)
-        + product(rows, other, jnp.maximum(f - 1, 0), below)
-        + product(rows, other, jnp.minimum(f + 1, 3), above)
-        + product(rows, other, f ^ 2, two)
-        + product(rows, other, 3 - f, three)
-    )
-    out[1:] = total.reshape(3, -1, total.shape[1]).astype(jnp.bfloat16)
-
-
-def attention(place, tiles, parts, q_ref, out_ref):
+def products(place, own, near, middle, two, *refs):
+    rows, total = refs[:4], refs[4]
+    depth = rows[0].shape[2]
+    for f in range(4):
+        planes = {f: own, f ^ 1: near, f ^ 2: two}
+        if f in (1, 2):
+            planes[3 - f] = middle
+
+        @pl.when(place[1] == f)
+        def _(planes=planes):
+            out = None
+            for z, w in planes.items():
+                for core in range(2):
+                    y = jnp.dot(
+                        rows[2 * core + z // 2][z % 2],
+                        w[core * depth : (core + 1) * depth, :],
+                        preferred_element_type=jnp.float32,
+                    )
+                    out = y if out is None else out + y
+            total[...] = out
+
+
+def last_product(place, three, *refs):
+    rows, (total, mine, one, two, other, held) = refs[:4], refs[4:]
+    depth = rows[0].shape[2]
+    g, n = place[0], mine.shape[0]
+
+    def put(x):
+        held[...] = x
+        for k, out in enumerate((mine, one, two, other)):
+            at = pl.multiple_of(jnp.maximum((g ^ k) - 1, 0) * n, n)
+            out[...] = held[pl.ds(at, n), :].astype(out.dtype)
+
+    for f in (0, 3):
+
+        @pl.when(place[1] == f)
+        def _(z=3 - f):
+            x = total[...]
+            for core in range(2):
+                x = x + jnp.dot(
+                    rows[2 * core + z // 2][z % 2],
+                    three[core * depth : (core + 1) * depth, :],
+                    preferred_element_type=jnp.float32,
+                )
+            put(x)
+
+    @pl.when((place[1] == 1) | (place[1] == 2))
+    def _():
+        put(total[...])
+
+
+def attention(place, tiles, mine, one, two, three, q_ref, out_ref, held, sems):
     g = place[0]
     groups_q = QH // KVH
+    copies = [
+        pltpu.make_async_copy(held.at[at, :], out_ref.at[at, :], sems.at[s])
+        for s, at in enumerate(pl.ds(s * TXT_S, TXT_S) for s in range(SAMP))
+    ]
 
     @pl.when(g == 0)
     def _():
-        out_ref[...] = jnp.zeros_like(out_ref)
+        held[...] = jnp.zeros_like(held)
+        for copy in copies:
+            copy.start()
 
     @pl.when(g > 0)
     def _():
-        kv = parts[0].astype(jnp.float32)
-        for h in range(1, 4):
-            kv = kv + parts[h].astype(jnp.float32)
+        kv = mine[...]
+        for part in (one, two, three):
+            kv = kv + part[...].astype(jnp.float32)
         kv = kv.astype(jnp.bfloat16)
-        slot = lax.broadcasted_iota(jnp.int32, (1, CAP), 1)
-        for s in range(SAMP):
+        slot = lax.broadcasted_iota(jnp.int32, (CAP, 1), 0)
+        for s, copy in enumerate(copies):
             live = slot < tiles[(g - 1) * SAMP + s] * TILE_TOK
             rows = slice(s * TXT_S, s * TXT_S + TXT_S)
             for k in range(kv.shape[1] // (2 * HD)):
@@ -190,17 +229,26 @@
                 ]
                 query = jnp.concatenate([q_ref[rows, h] for h in heads], axis=0)
                 scores = lax.dot_general(
+                    block[:, :HD],
                     query,
-                    block[:, :HD],
                     (((1,), (1,)), ((), ())),
                     preferred_element_type=jnp.float32,
                 ) * (1.0 / HD**0.5)
                 scores = jnp.where(live, scores, -1e30)
-                expo = jnp.exp(scores - jnp.max(scores, axis=-1, keepdims=True))
-                weights = (expo / jnp.sum(expo, axis=-1, keepdims=True)).astype(jnp.bfloat16)
-                out = jnp.dot(weights, block[:, HD:], preferred_element_type=jnp.float32)
+                expo = jnp.exp(scores - jnp.max(scores, axis=0, keepdims=True))
+                weights = (expo / jnp.sum(expo, axis=0, keepdims=True)).astype(jnp.bfloat16)
+                out = lax.dot_general(
+                    weights,
+                    block[:, HD:],
+                    (((0,), (0,)), ((), ())),
+                    preferred_element_type=jnp.float32,
+                )
                 for j, h in enumerate(heads):
-                    out_ref[rows, h] = out[j * TXT_S : (j + 1) * TXT_S].astype(jnp.bfloat16)
+                    held[rows, h] = out[j * TXT_S : (j + 1) * TXT_S].astype(jnp.bfloat16)
+            copy.start()
+
+    for copy in copies:
+        copy.wait()
 
 
 def shards_line(image_rows, enc_gain, key_value_w, tiles, queries):
@@ -225,15 +273,24 @@
     given = lax.dynamic_slice_in_dim(w, (1 - t) * half, half, axis=1)
     shape = (2 * quarter, half)
     own = call(join, [(shape, bf16)], kept, swap(given), specs=[VMEM, VMEM])[0]
-    below = send(own, [((c, z), (c, z + 1)) for c in range(4) for z in range(3)])
-    above = send(own, [((c, z + 1), (c, z)) for c in range(4) for z in range(3)])
-    ready = call(onward, [(shape, bf16)], place, own, below, above, cost=COST)[0]
+    middle = send(own, [((c, z), (c, 3 - z)) for c in range(4) for z in (1, 2)])
+    near = send(own, [((c, z), (c, z ^ 1)) for c in range(4) for z in planes])
+    ready = call(
+        onward,
+        [(shape, bf16)],
+        place,
+        own,
+        middle,
+        near,
+        specs=[SMEM] + [ANY] * 3,
+        cost=COST,
+        scratch=[pltpu.SemaphoreType.DMA],
+    )[0]
     pairs = ((0, 2), (3, 1), (2, 3), (1, 0))
     two = send(ready, [((c, a), (c, b)) for c in range(4) for a, b in pairs])
     three = send(two, [((c, a), (c, b)) for c in range(4) for a, b in pairs[2:]])
 
-    x = image_rows.astype(f32)
-    squares = jnp.sum(x * x, axis=1, keepdims=True)
+    squares = call(row_squares, [((n_rows, 128), f32)], place, image_rows)[0]
     whole, part = ((4, n_rows, quarter), bf16), ((2, n_rows, quarter), bf16)
     a, b, c, d_low, d_high = call(
         normalise,
@@ -252,11 +309,33 @@
     rows = call(landed, [part] * 2, place, a, b, c, d_low, d_high)
     rows = (*rows, *[swap(x) for x in rows])
 
-    parts = ((4, per_group, half), bf16)
-    parts = call(products, [parts], place, own, below, above, two, three, *rows)[0]
-    parts = lax.all_to_all(parts, "grp", 0, 0, tiled=True)
-    specs = [SMEM, SMEM, VMEM, VMEM]
-    return call(attention, [(queries.shape, bf16)], place, tiles, parts, queries, specs=specs)[0]
+    total = call(products, [((n_rows, half), f32)], place, own, near, middle, two, *rows)[0]
+    message = (per_group, half)
+    mine, *parts = call(
+        last_product,
+        [(message, f32)] + [(message, bf16)] * 3,
+        place,
+        three,
+        *rows,
+        total,
+        scratch=[pltpu.VMEM((n_rows, half), f32)],
+    )
+    parts = [
+        send(x, [((c, z), (c ^ k, z)) for c in range(4) for z in planes])
+        for k, x in zip((1, 2, 3), parts)
+    ]
+    return call(
+        attention,
+        [(queries.shape, bf16)],
+        place,
+        tiles,
+        mine,
+        *parts,
+        queries,
+        specs=[SMEM] * 2 + [VMEM] * 5,
+        out_spec=ANY,
+        scratch=[pltpu.VMEM(queries.shape, bf16), pltpu.SemaphoreType.DMA((SAMP,))],
+    )[0]
 
 
 def solution(mesh):

time: 68.8 us -> 62.1 us (0.903)
  blocking collectives: 10.6 us -> 0 us
  waiting for transfers between devices: 23.3 us -> 26.6 us
  other arithmetic: 2.66 us -> 0.08 us
  starting transfers between devices: 21.2 us -> 23.4 us
  local copies, waits for them, and re-layouts: 1.65 us -> 3.27 us
    all_to_all x1 -> x0, blocking collectives: 10.6 us -> none  [shards_line(): parts = lax.all_to_all(parts, 'grp', 0, 0, tiled=True)]
    ppermute x9 -> x12, waiting for transfers between devices: 19.1 us -> 22.3 us  [send(): lax.ppermute(x, AXES, [(index(a, c), index(b, c)) for a, b in pairs for c...]
    reduce_sum x1 -> x0, other arithmetic: 2.58 us -> none  [shards_line(): squares = jnp.sum(x * x, axis=1, keepdims=True)]
    ppermute x9 -> x12, starting transfers between devices: 20 us -> 22.2 us  [send(): lax.ppermute(x, AXES, [(index(a, c), index(b, c)) for a, b in pairs for c...]
    unnamed x8, local copies, waits for them, and re-layouts: 0.02 us -> 1.91 us
    pallas_call x7 -> x9, Pallas kernels: 8.81 us -> 8.21 us  [call(): pl.pallas_call(body, out_shape=outs, in_specs=specs or [SMEM] + [VMEM] *...]
  transfers between devices with their start and end apart: 13 -> 16, of which waited for: 8 -> 10; matrix products, arithmetic and copies ran while one was open for 4% -> 0% of each run, Pallas kernels for 6% -> 9%
where the time goes in v3:
time: 62.1 us; the launch traced here: 61.8 us
  waiting for transfers between devices  26.6 us (43%)
  starting transfers between devices  23.4 us (38%)
  Pallas kernels  8.21 us (13%)
  local copies, waits for them, and re-layouts  3.27 us (5%)
    ppermute x12, waiting for transfers between devices, send(): lax.ppermute(x, AXES, [(index(a, c), index(b, c)) for a, b in pairs for c...  22.3 us
    ppermute x12, starting transfers between devices, send(): lax.ppermute(x, AXES, [(index(a, c), index(b, c)) for a, b in pairs for c...  22.2 us
    pallas_call x9, Pallas kernels, call(): pl.pallas_call(body, out_shape=outs, in_specs=specs or [SMEM] + [VMEM] *...  8.21 us
    ppermute x4, waiting for transfers between devices, swap(): return lax.ppermute(x, 'tp', [(0, 1), (1, 0)])  4.34 us
    unnamed x8, local copies, waits for them, and re-layouts  1.91 us
    dynamic_slice x1, local copies, waits for them, and re-layouts, shards_line(): given = lax.dynamic_slice_in_dim(w, (1 - t) * half, half, axis=1)  1.35 us
  transfers between devices with their start and end apart: 16, of which 10 were waited for; matrix products, arithmetic and copies ran while one was open for 0% of the time, Pallas kernels for 9%

profile of v3, /device:TPU:0, one launch (start us, length us, event | category | flops | bytes accessed | tf_op | source)
XLA Modules:
  0.0 61.8 jit_solution(63124763957165445)
XLA Ops:
  0.0 1.4 %fusion = (bf16[256,512]{1,0:T(8,128)(2,1)S(1)}, bf16[256,512]{1,0:T(8,128)(2,1)S(1)}) fusion(bf16[1024,1024]{1,0:T(8,128)(2,1)} %param.7, s32[]{:T(128)S(6)} %select_n.16, s32[]{:T(128)S(6)} %select_n.20, s32[]{:T(128)S(6)} %select_n.18), kind=kLoop, calls=%fused_computation.1 | loop fusion | bytes 1048588 | tf_op jit(solution)/shard_map/dynamic_slice | solution.py:273
  1.4 0.5 collective-permute-start
  1.9 1.2 %collective-permute-done.other = bf16[256,512]{1,0:T(8,128)(2,1)S(1)} collective-permute-done((bf16[256,512]{1,0:T(8,128)(2,1)S(1)}, bf16[256,512]{1,0:T(8,128)(2,1)S(1)}, u32[]{:S(2)}, u32[]{:S(2)}) %collective-permute-start) | collective-permute-done | bytes 262176 | tf_op jit(solution)/shard_map/ppermute | solution.py:269
  3.0 0.0 copy-start.3
  3.1 0.7 %collective-permute-start.1 = (bf16[512,512]{1,0:T(8,128)(2,1)S(1)}, bf16[512,512]{1,0:T(8,128)(2,1)S(1)}, u32[]{:S(2)}, u32[]{:S(2)}) collective-permute-start(bf16[512,512]{1,0:T(8,128)(2,1)S(1)} %shard_map.55.own), channel_id=1, source_target_pairs={{2,4},{3,5},{4,2},{5,3},{10,12},{11,13},{12,10},{13,11},{18,20},{1... | collective-permute-start | bytes 1572872 | tf_op jit(solution)/shard_map/ppermute | solution.py:266
  3.8 5.8 %collective-permute-start.2 = (bf16[512,512]{1,0:T(8,128)(2,1)S(1)}, bf16[512,512]{1,0:T(8,128)(2,1)S(1)}, u32[]{:S(2)}, u32[]{:S(2)}) collective-permute-start(bf16[512,512]{1,0:T(8,128)(2,1)S(1)} %shard_map.55.own), channel_id=1, source_target_pairs={{0,2},{1,3},{2,0},{3,1},{4,6},{5,7},{6,4},{7,5},{8,10},{9,11},{10,... | collective-permute-start | bytes 1572872 | tf_op jit(solution)/shard_map/ppermute | solution.py:266
  9.6 0.1 pad_add_fusion.place
  9.7 0.0 copy-start
  9.7 1.9 %copy-done = bf16[384,4096]{1,0:T(8,128)(2,1)S(1)} copy-done((bf16[384,4096]{1,0:T(8,128)(2,1)S(1)}, bf16[384,4096]{1,0:T(8,128)(2,1)}, u32[]{:S(2)}) %copy-start) | copy-done | bytes 3145752
  11.5 1.2 %shard_map.57.squares = f32[384,128]{1,0:T(8,128)S(1)} custom-call(s32[3]{0:T(128)S(1)} %pad_add_fusion.place, bf16[384,4096]{1,0:T(8,128)(2,1)S(1)} %copy-done), custom_call_target="tpu_custom_call" | custom-call | tf_op jit(solution)/shard_map/pallas_call | solution.py:75
  12.7 0.1 collective-permute-start.5
  12.8 0.0 copy-done.3
  12.8 1.4 %collective-permute-done.5.other = f32[384,128]{1,0:T(8,128)S(1)} collective-permute-done((f32[384,128]{1,0:T(8,128)S(1)}, f32[384,128]{1,0:T(8,128)S(1)}, u32[]{:S(2)}, u32[]{:S(2)}) %collective-permute-start.5) | collective-permute-done | bytes 196640 | tf_op jit(solution)/shard_map/ppermute | solution.py:269
  14.2 1.9 %shard_map.58 = (bf16[4,384,256]{2,1,0:T(8,128)(2,1)S(1)}, bf16[4,384,256]{2,1,0:T(8,128)(2,1)S(1)}, bf16[4,384,256]{2,1,0:T(8,128)(2,1)S(1)}, bf16[2,384,256]{2,1,0:T(8,128)(2,1)S(1)}, bf16[2,384,256]{2,1,0:T(8,128)(2,1)S(1)}) custom-call(s32[3]{0:T(128)S(1)} %pad_add_fusion.place, bf16[384,4096]{1,0:T(8,128)(2,1)S(1)} %copy-done, ...), custom_call_target="tpu_custom_call" | custom-call | tf_op jit(solution)/shard_map/pallas_call | solution.py:75
  16.1 1.5 %collective-permute-start.9 = (bf16[2,384,256]{2,1,0:T(8,128)(2,1)S(1)}, bf16[2,384,256]{2,1,0:T(8,128)(2,1)S(1)}, u32[]{:S(2)}, u32[]{:S(2)}) collective-permute-start(bf16[2,384,256]{2,1,0:T(8,128)(2,1)S(1)} %get-tuple-element.20), channel_id=1, source_target_pairs={{0,16},{1,17},{2,18},{3,19},{4,20},{5,21},{6,22},{7,23}} | collective-permute-start | bytes 1179656 | tf_op jit(solution)/shard_map/ppermute | solution.py:266
  17.6 1.3 %collective-permute-start.6 = (bf16[4,384,256]{2,1,0:T(8,128)(2,1)S(1)}, bf16[4,384,256]{2,1,0:T(8,128)(2,1)S(1)}, u32[]{:S(2)}, u32[]{:S(2)}) collective-permute-start(bf16[4,384,256]{2,1,0:T(8,128)(2,1)S(1)} %get-tuple-element.17), channel_id=1, source_target_pairs={{0,8},{1,9},{2,10},{3,11},{4,12},{5,13},{6,14},{7,15}} | collective-permute-start | bytes 2359304 | tf_op jit(solution)/shard_map/ppermute | solution.py:266
  19.0 1.3 %collective-permute-start.7 = (bf16[4,384,256]{2,1,0:T(8,128)(2,1)S(1)}, bf16[4,384,256]{2,1,0:T(8,128)(2,1)S(1)}, u32[]{:S(2)}, u32[]{:S(2)}) collective-permute-start(bf16[4,384,256]{2,1,0:T(8,128)(2,1)S(1)} %get-tuple-element.18), channel_id=1, source_target_pairs={{0,16},{1,17},{2,18},{3,19},{4,20},{5,21},{6,22},{7,23}} | collective-permute-start | bytes 2359304 | tf_op jit(solution)/shard_map/ppermute | solution.py:266
  20.3 0.0 collective-permute-done.1.middle
  20.3 1.2 %collective-permute-done.2.near = bf16[512,512]{1,0:T(8,128)(2,1)S(1)} collective-permute-done((bf16[512,512]{1,0:T(8,128)(2,1)S(1)}, bf16[512,512]{1,0:T(8,128)(2,1)S(1)}, u32[]{:S(2)}, u32[]{:S(2)}) %collective-permute-start.2) | collective-permute-done | bytes 524320 | tf_op jit(solution)/shard_map/ppermute | solution.py:266
  21.5 0.6 shard_map.56.after
  22.1 1.7 %collective-permute-start.3 = (bf16[512,512]{1,0:T(8,128)(2,1)S(1)}, bf16[512,512]{1,0:T(8,128)(2,1)S(1)}, u32[]{:S(2)}, u32[]{:S(2)}) collective-permute-start(bf16[512,512]{1,0:T(8,128)(2,1)S(1)} %shard_map.56.after), channel_id=1, source_target_pairs={{0,4},{1,5},{6,2},{7,3},{4,6},{5,7},{2,0},{3,1},{8,12},{9,13},{14,... | collective-permute-start | bytes 1572872 | tf_op jit(solution)/shard_map/ppermute | solution.py:266
  23.8 4.4 %collective-permute-start.8 = (bf16[2,384,256]{2,1,0:T(8,128)(2,1)S(1)}, bf16[2,384,256]{2,1,0:T(8,128)(2,1)S(1)}, u32[]{:S(2)}, u32[]{:S(2)}) collective-permute-start(bf16[2,384,256]{2,1,0:T(8,128)(2,1)S(1)} %get-tuple-element.19), channel_id=1, source_target_pairs={{0,24},{1,25},{2,26},{3,27},{4,28},{5,29},{6,30},{7,31}} | collective-permute-start | bytes 1179656 | tf_op jit(solution)/shard_map/ppermute | solution.py:266
  28.2 0.0 collective-permute-done.9.x
  28.2 0.7 %collective-permute-start.10 = (bf16[2,384,256]{2,1,0:T(8,128)(2,1)S(1)}, bf16[2,384,256]{2,1,0:T(8,128)(2,1)S(1)}, u32[]{:S(2)}, u32[]{:S(2)}) collective-permute-start(bf16[2,384,256]{2,1,0:T(8,128)(2,1)S(1)} %shard_map.59), channel_id=1, source_target_pairs={{16,24},{17,25},{18,26},{19,27},{20,28},{21,29},{22,30},{23,31}} | collective-permute-start | bytes 1179656 | tf_op jit(solution)/shard_map/ppermute | solution.py:266
  28.9 6.4 %collective-permute-done.3.two = bf16[512,512]{1,0:T(8,128)(2,1)S(1)} collective-permute-done((bf16[512,512]{1,0:T(8,128)(2,1)S(1)}, bf16[512,512]{1,0:T(8,128)(2,1)S(1)}, u32[]{:S(2)}, u32[]{:S(2)}) %collective-permute-start.3) | collective-permute-done | bytes 524320 | tf_op jit(solution)/shard_map/ppermute | solution.py:266
  35.3 1.3 %collective-permute-start.4 = (bf16[512,512]{1,0:T(8,128)(2,1)S(1)}, bf16[512,512]{1,0:T(8,128)(2,1)S(1)}, u32[]{:S(2)}, u32[]{:S(2)}) collective-permute-start(bf16[512,512]{1,0:T(8,128)(2,1)S(1)} %collective-permute-done.3.two), channel_id=1, source_target_pairs={{4,6},{5,7},{2,0},{3,1},{12,14},{13,15},{10,8},{11,9},{20,22},{21,... | collective-permute-start | bytes 1572872 | tf_op jit(solution)/shard_map/ppermute | solution.py:266
  36.6 7.9 %collective-permute-done.8.d_low = bf16[2,384,256]{2,1,0:T(8,128)(2,1)S(1)} collective-permute-done((bf16[2,384,256]{2,1,0:T(8,128)(2,1)S(1)}, bf16[2,384,256]{2,1,0:T(8,128)(2,1)S(1)}, u32[]{:S(2)}, u32[]{:S(2)}) %collective-permute-start.8) | collective-permute-done | bytes 393248 | tf_op jit(solution)/shard_map/ppermute | solution.py:266
  44.5 0.0 collective-permute-done.6.b
  44.5 0.0 collective-permute-done.7.c
  44.5 0.0 collective-permute-done.10.d_high
  44.5 0.6 shard_map.60
  45.1 0.1 collective-permute-start.11
  45.2 0.5 collective-permute-start.12
  45.7 1.2 %collective-permute-done.11.refs_2_ = bf16[2,384,256]{2,1,0:T(8,128)(2,1)S(1)} collective-permute-done((bf16[2,384,256]{2,1,0:T(8,128)(2,1)S(1)}, bf16[2,384,256]{2,1,0:T(8,128)(2,1)S(1)}, u32[]{:S(2)}, u32[]{:S(2)}) %collective-permute-start.11) | collective-permute-done | bytes 393248 | tf_op jit(solution)/shard_map/ppermute | solution.py:269
  46.9 0.6 collective-permute-done.12.refs_3_
  47.5 1.3 %shard_map.61.refs_4_ = f32[384,512]{1,0:T(8,128)S(1)} custom-call(s32[3]{0:T(128)S(1)} %pad_add_fusion.place, bf16[512,512]{1,0:T(8,128)(2,1)S(1)} %shard_map.55.own, bf16[512,512]{1,0:T(8,128)(2,1)S(1)} %collective-permute-done.2.near, bf16[512,512]{1,0:T(8,128)(2,1)S(1)} %collective-permute-done.1.middle, ...), custom_call_target="tpu_custom_call" | custom-call | tf_op jit(solution)/shard_map/pallas_call | solution.py:75
  48.8 0.0 copy-start.1
  48.8 0.0 copy-start.2
  48.9 0.6 collective-permute-done.4.three
  49.4 1.0 %shard_map.62 = (f32[128,512]{1,0:T(8,128)S(1)}, bf16[128,512]{1,0:T(8,128)(2,1)S(1)}, bf16[128,512]{1,0:T(8,128)(2,1)S(1)}, bf16[128,512]{1,0:T(8,128)(2,1)S(1)}) custom-call(s32[3]{0:T(128)S(1)} %pad_add_fusion.place, bf16[512,512]{1,0:T(8,128)(2,1)S(1)} %collective-permute-done.4.three, bf16[2,384,256]{2,1,0:T(8,128)(2,1)S(1)} %get-tuple-element.21.refs_0_, ...), custom_call_target="tpu_custom_call" | custom-call | tf_op jit(solution)/shard_map/pallas_call | solution.py:75
  50.4 1.6 %collective-permute-start.13 = (bf16[128,512]{1,0:T(8,128)(2,1)S(1)}, bf16[128,512]{1,0:T(8,128)(2,1)S(1)}, u32[]{:S(2)}, u32[]{:S(2)}) collective-permute-start(bf16[128,512]{1,0:T(8,128)(2,1)S(1)} %get-tuple-element.24), channel_id=1, source_target_pairs={{0,8},{1,9},{2,10},{3,11},{4,12},{5,13},{6,14},{7,15},{8,0},{9,1},... | collective-permute-start | bytes 393224 | tf_op jit(solution)/shard_map/ppermute | solution.py:266
  52.0 1.9 %collective-permute-start.14 = (bf16[128,512]{1,0:T(8,128)(2,1)S(1)}, bf16[128,512]{1,0:T(8,128)(2,1)S(1)}, u32[]{:S(2)}, u32[]{:S(2)}) collective-permute-start(bf16[128,512]{1,0:T(8,128)(2,1)S(1)} %get-tuple-element.25), channel_id=1, source_target_pairs={{0,16},{1,17},{2,18},{3,19},{4,20},{5,21},{6,22},{7,23},{8,24},{9,... | collective-permute-start | bytes 393224 | tf_op jit(solution)/shard_map/ppermute | solution.py:266
  53.9 0.1 collective-permute-start.15
  54.0 1.5 %collective-permute-done.13.one = bf16[128,512]{1,0:T(8,128)(2,1)S(1)} collective-permute-done((bf16[128,512]{1,0:T(8,128)(2,1)S(1)}, bf16[128,512]{1,0:T(8,128)(2,1)S(1)}, u32[]{:S(2)}, u32[]{:S(2)}) %collective-permute-start.13) | collective-permute-done | bytes 131104 | tf_op jit(solution)/shard_map/ppermute | solution.py:266
  55.5 4.7 %collective-permute-done.14.two = bf16[128,512]{1,0:T(8,128)(2,1)S(1)} collective-permute-done((bf16[128,512]{1,0:T(8,128)(2,1)S(1)}, bf16[128,512]{1,0:T(8,128)(2,1)S(1)}, u32[]{:S(2)}, u32[]{:S(2)}) %collective-permute-start.14) | collective-permute-done | bytes 131104 | tf_op jit(solution)/shard_map/ppermute | solution.py:266
  60.2 0.0 collective-permute-done.15.three
  60.2 0.0 copy-done.1
  60.2 0.0 copy-done.2
  60.2 1.6 %shard_map.63 = bf16[256,2048]{1,0:T(8,128)(2,1)} custom-call(s32[3]{0:T(128)S(1)} %pad_add_fusion.place, s32[6]{0:T(128)S(1)} %copy-done.2, f32[128,512]{1,0:T(8,128)S(1)} %get-tuple-element.23.mine, bf16[128,512]{1,0:T(8,128)(2,1)S(1)} %collective-permute-done.13.one, bf16[128,512]{1,0:T(8,128)(2,1)S(1)} %collective-permute-done.14.two, ...), custom_call_target="tpu_custom_call" | custom-call | tf_op jit(solution)/shard_map/pallas_call | solution.py:75
  (3 shorter events, 0.1 us)
Async XLA Ops:
  1.4 1.7 %collective-permute-start = (bf16[256,512]{1,0:T(8,128)(2,1)S(1)}, bf16[256,512]{1,0:T(8,128)(2,1)S(1)}, u32[]{:S(2)}, u32[]{:S(2)}) collective-permute-start(bf16[256,512]{1,0:T(8,128)(2,1)S(1)} %get-tuple-element.27), channel_id=1, source_target_pairs={{0,1},{1,0},{2,3},{3,2},{4,5},{5,4},{6,7},{7,6},{8,9},{9,8},{10,11... | collective-permute-start | bytes 786440 | tf_op jit(solution)/shard_map/ppermute | solution.py:269
  3.0 9.8 %copy-start.3 = (bf16[4096]{0:T(1024)(128)(2,1)S(1)}, bf16[4096]{0:T(1024)(128)(2,1)}, u32[]{:S(2)}) copy-start(bf16[4096]{0:T(1024)(128)(2,1)} %param.6) | copy-start | bytes 24580
  3.1 17.2 %collective-permute-start.1 = (bf16[512,512]{1,0:T(8,128)(2,1)S(1)}, bf16[512,512]{1,0:T(8,128)(2,1)S(1)}, u32[]{:S(2)}, u32[]{:S(2)}) collective-permute-start(bf16[512,512]{1,0:T(8,128)(2,1)S(1)} %shard_map.55.own), channel_id=1, source_target_pairs={{2,4},{3,5},{4,2},{5,3},{10,12},{11,13},{12,10},{13,11},{18,20},{1... | collective-permute-start | bytes 1572872 | tf_op jit(solution)/shard_map/ppermute | solution.py:266
  3.8 17.8 %collective-permute-start.2 = (bf16[512,512]{1,0:T(8,128)(2,1)S(1)}, bf16[512,512]{1,0:T(8,128)(2,1)S(1)}, u32[]{:S(2)}, u32[]{:S(2)}) collective-permute-start(bf16[512,512]{1,0:T(8,128)(2,1)S(1)} %shard_map.55.own), channel_id=1, source_target_pairs={{0,2},{1,3},{2,0},{3,1},{4,6},{5,7},{6,4},{7,5},{8,10},{9,11},{10,... | collective-permute-start | bytes 1572872 | tf_op jit(solution)/shard_map/ppermute | solution.py:266
  9.7 1.9 %copy-start = (bf16[384,4096]{1,0:T(8,128)(2,1)S(1)}, bf16[384,4096]{1,0:T(8,128)(2,1)}, u32[]{:S(2)}) copy-start(bf16[384,4096]{1,0:T(8,128)(2,1)} %x.3) | copy-start | bytes 9437188
  12.7 1.5 %collective-permute-start.5 = (f32[384,128]{1,0:T(8,128)S(1)}, f32[384,128]{1,0:T(8,128)S(1)}, u32[]{:S(2)}, u32[]{:S(2)}) collective-permute-start(f32[384,128]{1,0:T(8,128)S(1)} %shard_map.57.squares), channel_id=1, source_target_pairs={{0,1},{1,0},{2,3},{3,2},{4,5},{5,4},{6,7},{7,6},{8,9},{9,8},{10,11... | collective-permute-start | bytes 589832 | tf_op jit(solution)/shard_map/ppermute | solution.py:269
  16.1 12.1 %collective-permute-start.9 = (bf16[2,384,256]{2,1,0:T(8,128)(2,1)S(1)}, bf16[2,384,256]{2,1,0:T(8,128)(2,1)S(1)}, u32[]{:S(2)}, u32[]{:S(2)}) collective-permute-start(bf16[2,384,256]{2,1,0:T(8,128)(2,1)S(1)} %get-tuple-element.20), channel_id=1, source_target_pairs={{0,16},{1,17},{2,18},{3,19},{4,20},{5,21},{6,22},{7,23}} | collective-permute-start | bytes 1179656 | tf_op jit(solution)/shard_map/ppermute | solution.py:266
  17.6 26.9 %collective-permute-start.6 = (bf16[4,384,256]{2,1,0:T(8,128)(2,1)S(1)}, bf16[4,384,256]{2,1,0:T(8,128)(2,1)S(1)}, u32[]{:S(2)}, u32[]{:S(2)}) collective-permute-start(bf16[4,384,256]{2,1,0:T(8,128)(2,1)S(1)} %get-tuple-element.17), channel_id=1, source_target_pairs={{0,8},{1,9},{2,10},{3,11},{4,12},{5,13},{6,14},{7,15}} | collective-permute-start | bytes 2359304 | tf_op jit(solution)/shard_map/ppermute | solution.py:266
  19.0 25.5 %collective-permute-start.7 = (bf16[4,384,256]{2,1,0:T(8,128)(2,1)S(1)}, bf16[4,384,256]{2,1,0:T(8,128)(2,1)S(1)}, u32[]{:S(2)}, u32[]{:S(2)}) collective-permute-start(bf16[4,384,256]{2,1,0:T(8,128)(2,1)S(1)} %get-tuple-element.18), channel_id=1, source_target_pairs={{0,16},{1,17},{2,18},{3,19},{4,20},{5,21},{6,22},{7,23}} | collective-permute-start | bytes 2359304 | tf_op jit(solution)/shard_map/ppermute | solution.py:266
  22.1 13.2 %collective-permute-start.3 = (bf16[512,512]{1,0:T(8,128)(2,1)S(1)}, bf16[512,512]{1,0:T(8,128)(2,1)S(1)}, u32[]{:S(2)}, u32[]{:S(2)}) collective-permute-start(bf16[512,512]{1,0:T(8,128)(2,1)S(1)} %shard_map.56.after), channel_id=1, source_target_pairs={{0,4},{1,5},{6,2},{7,3},{4,6},{5,7},{2,0},{3,1},{8,12},{9,13},{14,... | collective-permute-start | bytes 1572872 | tf_op jit(solution)/shard_map/ppermute | solution.py:266
  23.8 20.7 %collective-permute-start.8 = (bf16[2,384,256]{2,1,0:T(8,128)(2,1)S(1)}, bf16[2,384,256]{2,1,0:T(8,128)(2,1)S(1)}, u32[]{:S(2)}, u32[]{:S(2)}) collective-permute-start(bf16[2,384,256]{2,1,0:T(8,128)(2,1)S(1)} %get-tuple-element.19), channel_id=1, source_target_pairs={{0,24},{1,25},{2,26},{3,27},{4,28},{5,29},{6,30},{7,31}} | collective-permute-start | bytes 1179656 | tf_op jit(solution)/shard_map/ppermute | solution.py:266
  28.2 16.3 %collective-permute-start.10 = (bf16[2,384,256]{2,1,0:T(8,128)(2,1)S(1)}, bf16[2,384,256]{2,1,0:T(8,128)(2,1)S(1)}, u32[]{:S(2)}, u32[]{:S(2)}) collective-permute-start(bf16[2,384,256]{2,1,0:T(8,128)(2,1)S(1)} %shard_map.59), channel_id=1, source_target_pairs={{16,24},{17,25},{18,26},{19,27},{20,28},{21,29},{22,30},{23,31}} | collective-permute-start | bytes 1179656 | tf_op jit(solution)/shard_map/ppermute | solution.py:266
  35.3 14.1 %collective-permute-start.4 = (bf16[512,512]{1,0:T(8,128)(2,1)S(1)}, bf16[512,512]{1,0:T(8,128)(2,1)S(1)}, u32[]{:S(2)}, u32[]{:S(2)}) collective-permute-start(bf16[512,512]{1,0:T(8,128)(2,1)S(1)} %collective-permute-done.3.two), channel_id=1, source_target_pairs={{4,6},{5,7},{2,0},{3,1},{12,14},{13,15},{10,8},{11,9},{20,22},{21,... | collective-permute-start | bytes 1572872 | tf_op jit(solution)/shard_map/ppermute | solution.py:266
  45.1 1.8 %collective-permute-start.11 = (bf16[2,384,256]{2,1,0:T(8,128)(2,1)S(1)}, bf16[2,384,256]{2,1,0:T(8,128)(2,1)S(1)}, u32[]{:S(2)}, u32[]{:S(2)}) collective-permute-start(bf16[2,384,256]{2,1,0:T(8,128)(2,1)S(1)} %get-tuple-element.21.refs_0_), channel_id=1, source_target_pairs={{0,1},{1,0},{2,3},{3,2},{4,5},{5,4},{6,7},{7,6},{8,9},{9,8},{10,11... | collective-permute-start | bytes 1179656 | tf_op jit(solution)/shard_map/ppermute | solution.py:269
  45.2 2.3 %collective-permute-start.12 = (bf16[2,384,256]{2,1,0:T(8,128)(2,1)S(1)}, bf16[2,384,256]{2,1,0:T(8,128)(2,1)S(1)}, u32[]{:S(2)}, u32[]{:S(2)}) collective-permute-start(bf16[2,384,256]{2,1,0:T(8,128)(2,1)S(1)} %get-tuple-element.22.refs_1_), channel_id=1, source_target_pairs={{0,1},{1,0},{2,3},{3,2},{4,5},{5,4},{6,7},{7,6},{8,9},{9,8},{10,11... | collective-permute-start | bytes 1179656 | tf_op jit(solution)/shard_map/ppermute | solution.py:269
  48.8 11.4 %copy-start.1 = (bf16[256,2048]{1,0:T(8,128)(2,1)S(1)}, bf16[256,2048]{1,0:T(8,128)(2,1)}, u32[]{:S(2)}) copy-start(bf16[256,2048]{1,0:T(8,128)(2,1)} %q_ref.1) | copy-start | bytes 3145732
  48.8 11.4 %copy-start.2 = (s32[6]{0:T(128)S(1)}, s32[6]{0:T(128)}, u32[]{:S(2)}) copy-start(s32[6]{0:T(128)} %tiles.1) | copy-start | bytes 76
  50.4 5.1 %collective-permute-start.13 = (bf16[128,512]{1,0:T(8,128)(2,1)S(1)}, bf16[128,512]{1,0:T(8,128)(2,1)S(1)}, u32[]{:S(2)}, u32[]{:S(2)}) collective-permute-start(bf16[128,512]{1,0:T(8,128)(2,1)S(1)} %get-tuple-element.24), channel_id=1, source_target_pairs={{0,8},{1,9},{2,10},{3,11},{4,12},{5,13},{6,14},{7,15},{8,0},{9,1},... | collective-permute-start | bytes 393224 | tf_op jit(solution)/shard_map/ppermute | solution.py:266
  52.0 8.2 %collective-permute-start.14 = (bf16[128,512]{1,0:T(8,128)(2,1)S(1)}, bf16[128,512]{1,0:T(8,128)(2,1)S(1)}, u32[]{:S(2)}, u32[]{:S(2)}) collective-permute-start(bf16[128,512]{1,0:T(8,128)(2,1)S(1)} %get-tuple-element.25), channel_id=1, source_target_pairs={{0,16},{1,17},{2,18},{3,19},{4,20},{5,21},{6,22},{7,23},{8,24},{9,... | collective-permute-start | bytes 393224 | tf_op jit(solution)/shard_map/ppermute | solution.py:266
  53.9 6.3 %collective-permute-start.15 = (bf16[128,512]{1,0:T(8,128)(2,1)S(1)}, bf16[128,512]{1,0:T(8,128)(2,1)S(1)}, u32[]{:S(2)}, u32[]{:S(2)}) collective-permute-start(bf16[128,512]{1,0:T(8,128)(2,1)S(1)} %get-tuple-element.26), channel_id=1, source_target_pairs={{0,24},{1,25},{2,26},{3,27},{4,28},{5,29},{6,30},{7,31},{8,16},{9,... | collective-permute-start | bytes 393224 | tf_op jit(solution)/shard_map/ppermute | solution.py:266

commit v4 on v3

--- a/solution.py
+++ b/solution.py
@@ -15,7 +15,6 @@
 CAP = 64
 AXES = ("grp", "fsdp", "tp")
 VMEM = pl.BlockSpec(memory_space=pltpu.VMEM)
-SMEM = pl.BlockSpec(memory_space=pltpu.SMEM)
 ANY = pl.BlockSpec(memory_space=pl.ANY)
 HBM = pl.BlockSpec(memory_space=pltpu.HBM)
 LIMIT = 16 * 1024 * 1024
@@ -75,7 +74,7 @@
     return pl.pallas_call(
         body,
         out_shape=outs,
-        in_specs=specs or [SMEM] + [VMEM] * (len(args) - 1),
+        in_specs=specs or [VMEM] * len(args),
         out_specs=[out_spec] * len(outs),
         cost_estimate=cost,
         scratch_shapes=list(scratch),
@@ -89,8 +88,8 @@
     out[rows:, :] = other[...]
 
 
-def row_squares(place, x, squares):
-    @pl.when(place[0] == 0)
+def row_squares(x, squares):
+    @pl.when(lax.axis_index("grp") == 0)
     def _():
         total = None
         for col in range(0, x.shape[1], 128):
@@ -99,10 +98,10 @@
         squares[...] = total
 
 
-def normalise(place, x, squares, other, gain, a, b, c, d_low, d_high):
+def normalise(x, squares, other, gain, a, b, c, d_low, d_high):
     width = x.shape[1] // 16
 
-    @pl.when(place[0] == 0)
+    @pl.when(lax.axis_index("grp") == 0)
     def _():
         total = jnp.sum(squares[...] + other[...], axis=1, keepdims=True)
         scale = lax.rsqrt(total / D + 1e-05)
@@ -114,25 +113,12 @@
                 out[at] = y.astype(jnp.bfloat16)
 
 
-def onward(place, own, middle, near, out, sem):
-    del near
-    end = (place[1] == 0) | (place[1] == 3)
-    for use, source in ((end, own), (jnp.logical_not(end), middle)):
-
-        @pl.when(use)
-        def _(source=source):
-            copy = pltpu.make_async_copy(source, out, sem)
-            copy.start()
-            copy.wait()
-
-
-def later(x, after, out):
-    del after
-    out[...] = x[...]
-
-
-def landed(place, a, b, c, d_low, d_high, low, high):
-    g = place[0]
+def later(x, *rest):
+    rest[-1][...] = x[...]
+
+
+def landed(a, b, c, d_low, d_high, low, high):
+    g = lax.axis_index("grp")
     for who, source in ((0, a), (1, b), (2, c)):
 
         @pl.when(g == who)
@@ -146,18 +132,15 @@
         high[...] = d_high[...]
 
 
-def products(place, own, near, middle, two, *refs):
-    rows, total = refs[:4], refs[4]
+def add_products(rows, blocks, total):
     depth = rows[0].shape[2]
     for f in range(4):
-        planes = {f: own, f ^ 1: near, f ^ 2: two}
-        if f in (1, 2):
-            planes[3 - f] = middle
-
-        @pl.when(place[1] == f)
-        def _(planes=planes):
+
+        @pl.when(lax.axis_index("fsdp") == f)
+        def _(f=f):
             out = None
-            for z, w in planes.items():
+            for k, w in blocks.items():
+                z = f ^ k
                 for core in range(2):
                     y = jnp.dot(
                         rows[2 * core + z // 2][z % 2],
@@ -165,40 +148,31 @@
                         preferred_element_type=jnp.float32,
                     )
                     out = y if out is None else out + y
-            total[...] = out
-
-
-def last_product(place, three, *refs):
+            total(out)
+
+
+def products(own, near, far, *refs):
+    def put(x):
+        refs[4][...] = x
+
+    add_products(refs[:4], {0: own, 1: near, 2: far}, put)
+
+
+def last_product(last, *refs):
     rows, (total, mine, one, two, other, held) = refs[:4], refs[4:]
-    depth = rows[0].shape[2]
-    g, n = place[0], mine.shape[0]
+    g, n = lax.axis_index("grp"), mine.shape[0]
 
     def put(x):
-        held[...] = x
-        for k, out in enumerate((mine, one, two, other)):
-            at = pl.multiple_of(jnp.maximum((g ^ k) - 1, 0) * n, n)
-            out[...] = held[pl.ds(at, n), :].astype(out.dtype)
-
-    for f in (0, 3):
-
-        @pl.when(place[1] == f)
-        def _(z=3 - f):
-            x = total[...]
-            for core in range(2):
-                x = x + jnp.dot(
-                    rows[2 * core + z // 2][z % 2],
-                    three[core * depth : (core + 1) * depth, :],
-                    preferred_element_type=jnp.float32,
-                )
-            put(x)
-
-    @pl.when((place[1] == 1) | (place[1] == 2))
-    def _():
-        put(total[...])
-
-
-def attention(place, tiles, mine, one, two, three, q_ref, out_ref, held, sems):
-    g = place[0]
+        held[...] = total[...] + x
+
+    add_products(rows, {3: last}, put)
+    for k, out in enumerate((mine, one, two, other)):
+        at = pl.multiple_of(jnp.maximum((g ^ k) - 1, 0) * n, n)
+        out[...] = held[pl.ds(at, n), :].astype(out.dtype)
+
+
+def attention(counts, mine, one, two, three, q_ref, out_ref, held, sems):
+    g = lax.axis_index("grp")
     groups_q = QH // KVH
     copies = [
         pltpu.make_async_copy(held.at[at, :], out_ref.at[at, :], sems.at[s])
@@ -219,7 +193,7 @@
         kv = kv.astype(jnp.bfloat16)
         slot = lax.broadcasted_iota(jnp.int32, (CAP, 1), 0)
         for s, copy in enumerate(copies):
-            live = slot < tiles[(g - 1) * SAMP + s] * TILE_TOK
+            live = slot < counts[s : s + 1, :1]
             rows = slice(s * TXT_S, s * TXT_S + TXT_S)
             for k in range(kv.shape[1] // (2 * HD)):
                 block = kv[s * CAP : s * CAP + CAP, k * 2 * HD : (k + 1) * 2 * HD]
@@ -252,8 +226,7 @@
 
 
 def shards_line(image_rows, enc_gain, key_value_w, tiles, queries):
-    g, f, t = (lax.axis_index(a) for a in AXES)
-    place = jnp.stack([g, f, t]).astype(jnp.int32)
+    g, t = lax.axis_index("grp"), lax.axis_index("tp")
     n_rows = image_rows.shape[0]
     per_group = n_rows // 3
     half = key_value_w.shape[1] // 2
@@ -272,30 +245,18 @@
     kept = lax.dynamic_slice_in_dim(w, t * half, half, axis=1)
     given = lax.dynamic_slice_in_dim(w, (1 - t) * half, half, axis=1)
     shape = (2 * quarter, half)
-    own = call(join, [(shape, bf16)], kept, swap(given), specs=[VMEM, VMEM])[0]
-    middle = send(own, [((c, z), (c, 3 - z)) for c in range(4) for z in (1, 2)])
-    near = send(own, [((c, z), (c, z ^ 1)) for c in range(4) for z in planes])
-    ready = call(
-        onward,
-        [(shape, bf16)],
-        place,
-        own,
-        middle,
-        near,
-        specs=[SMEM] + [ANY] * 3,
-        cost=COST,
-        scratch=[pltpu.SemaphoreType.DMA],
-    )[0]
-    pairs = ((0, 2), (3, 1), (2, 3), (1, 0))
-    two = send(ready, [((c, a), (c, b)) for c in range(4) for a, b in pairs])
-    three = send(two, [((c, a), (c, b)) for c in range(4) for a, b in pairs[2:]])
-
-    squares = call(row_squares, [((n_rows, 128), f32)], place, image_rows)[0]
+    own = call(join, [(shape, bf16)], kept, swap(given), cost=1)[0]
+
+    def swap_planes(x, k):
+        return send(x, [((c, z), (c, z ^ k)) for c in range(4) for z in planes])
+
+    near, far = swap_planes(own, 1), swap_planes(own, 2)
+
+    squares = call(row_squares, [((n_rows, 128), f32)], image_rows)[0]
     whole, part = ((4, n_rows, quarter), bf16), ((2, n_rows, quarter), bf16)
     a, b, c, d_low, d_high = call(
         normalise,
         [whole] * 3 + [part] * 2,
-        place,
         image_rows,
         squares,
         swap(squares),
@@ -304,18 +265,19 @@
     to_b, to_c, to_d = ([((0, z), (h, z)) for z in planes] for h in (1, 2, 3))
     d_low, d_high = send(d_low, to_d), send(d_high, to_c)
     b, c = send(b, to_b), send(c, to_c)
-    d_high = call(later, [part], d_high, ready, specs=[VMEM, ANY])[0]
+    last = call(later, [(shape, bf16)], far, near, d_low, specs=[VMEM, ANY, ANY], cost=COST)[0]
+    last = swap_planes(last, 1)
     d_high = send(d_high, [((2, z), (3, z)) for z in planes])
-    rows = call(landed, [part] * 2, place, a, b, c, d_low, d_high)
+    rows = call(landed, [part] * 2, a, b, c, d_low, d_high)
     rows = (*rows, *[swap(x) for x in rows])
 
-    total = call(products, [((n_rows, half), f32)], place, own, near, middle, two, *rows)[0]
+    total = call(products, [((n_rows, half), f32)], own, near, far, *rows)[0]
+    counts = lax.dynamic_slice_in_dim(tiles, jnp.maximum(g - 1, 0) * SAMP, SAMP) * TILE_TOK
     message = (per_group, half)
     mine, *parts = call(
         last_product,
         [(message, f32)] + [(message, bf16)] * 3,
-        place,
-        three,
+        last,
         *rows,
         total,
         scratch=[pltpu.VMEM((n_rows, half), f32)],
@@ -327,12 +289,10 @@
     return call(
         attention,
         [(queries.shape, bf16)],
-        place,
-        tiles,
+        jnp.broadcast_to(counts[:, None], (SAMP, 128)),
         mine,
         *parts,
         queries,
-        specs=[SMEM] * 2 + [VMEM] * 5,
         out_spec=ANY,
         scratch=[pltpu.VMEM(queries.shape, bf16), pltpu.SemaphoreType.DMA((SAMP,))],
     )[0]

time: 62.1 us -> 55.7 us (0.90)
  starting transfers between devices: 23.4 us -> 19 us
  Pallas kernels: 8.21 us -> 4.34 us
  waiting for transfers between devices: 26.6 us -> 28.5 us
    ppermute x12 -> x11, starting transfers between devices: 22.2 us -> 17.8 us  [send(): lax.ppermute(x, AXES, [(index(a, c), index(b, c)) for a, b in pairs for c...]
    ppermute x12 -> x11, waiting for transfers between devices: 22.3 us -> 26.7 us  [send(): lax.ppermute(x, AXES, [(index(a, c), index(b, c)) for a, b in pairs for c...]
    pallas_call x9 -> x8, Pallas kernels: 8.21 us -> 4.34 us  [call(): pl.pallas_call(body, out_shape=outs, in_specs=specs or [VMEM] * len(args)...]
    ppermute x4, waiting for transfers between devices: 4.34 us -> 1.78 us  [swap(): return lax.ppermute(x, 'tp', [(0, 1), (1, 0)])]
    unnamed x8 -> x10, local copies, waits for them, and re-layouts: 1.91 us -> 1.91 us
  transfers between devices with their start and end apart: 16 -> 15, of which waited for: 10 -> 10; matrix products, arithmetic and copies ran while one was open for 0% -> 0% of each run, Pallas kernels for 9% -> 5%
where the time goes in v4:
time: 55.7 us; the launch traced here: 55.4 us
  waiting for transfers between devices  28.5 us (51%)
  starting transfers between devices  19 us (34%)
  Pallas kernels  4.34 us (8%)
  local copies, waits for them, and re-layouts  3.34 us (6%)
    ppermute x11, waiting for transfers between devices, send(): lax.ppermute(x, AXES, [(index(a, c), index(b, c)) for a, b in pairs for c...  26.7 us
    ppermute x11, starting transfers between devices, send(): lax.ppermute(x, AXES, [(index(a, c), index(b, c)) for a, b in pairs for c...  17.8 us
    pallas_call x8, Pallas kernels, call(): pl.pallas_call(body, out_shape=outs, in_specs=specs or [VMEM] * len(args)...  4.34 us
    unnamed x10, local copies, waits for them, and re-layouts  1.91 us
    ppermute x4, waiting for transfers between devices, swap(): return lax.ppermute(x, 'tp', [(0, 1), (1, 0)])  1.78 us
    dynamic_slice x1, local copies, waits for them, and re-layouts, shards_line(): given = lax.dynamic_slice_in_dim(w, (1 - t) * half, half, axis=1)  1.35 us
    ppermute x4, starting transfers between devices, swap(): return lax.ppermute(x, 'tp', [(0, 1), (1, 0)])  1.21 us
  transfers between devices with their start and end apart: 15, of which 10 were waited for; matrix products, arithmetic and copies ran while one was open for 0% of the time, Pallas kernels for 5%

profile of v4, /device:TPU:0, one launch (start us, length us, event | category | flops | bytes accessed | tf_op | source)
XLA Modules:
  0.0 55.4 jit_solution(4799399767752507469)
XLA Ops:
  0.0 1.4 %fusion = (bf16[256,512]{1,0:T(8,128)(2,1)S(1)}, bf16[256,512]{1,0:T(8,128)(2,1)S(1)}) fusion(bf16[1024,1024]{1,0:T(8,128)(2,1)} %param.7, s32[]{:T(128)S(6)} %select_n.20, s32[]{:T(128)S(6)} %select_n.24, s32[]{:T(128)S(6)} %select_n.22), kind=kLoop, calls=%fused_computation.1 | loop fusion | bytes 1048588 | tf_op jit(solution)/shard_map/dynamic_slice | solution.py:246
  1.4 0.5 collective-permute-start
  1.9 0.0 copy-start
  1.9 1.9 %copy-done = bf16[384,4096]{1,0:T(8,128)(2,1)S(1)} copy-done((bf16[384,4096]{1,0:T(8,128)(2,1)S(1)}, bf16[384,4096]{1,0:T(8,128)(2,1)}, u32[]{:S(2)}) %copy-start) | copy-done | bytes 3145752
  3.8 0.6 %shard_map.56.squares = f32[384,128]{1,0:T(8,128)S(1)} custom-call(bf16[384,4096]{1,0:T(8,128)(2,1)S(1)} %copy-done), custom_call_target="tpu_custom_call" | custom-call | tf_op jit(solution)/shard_map/pallas_call | solution.py:74
  4.4 0.0 copy-start.3
  4.4 0.0 copy-start.1
  4.4 0.1 collective-permute-start.3
  4.5 0.0 collective-permute-done.other
  4.6 4.1 %collective-permute-start.1 = (bf16[512,512]{1,0:T(8,128)(2,1)S(1)}, bf16[512,512]{1,0:T(8,128)(2,1)S(1)}, u32[]{:S(2)}, u32[]{:S(2)}) collective-permute-start(bf16[512,512]{1,0:T(8,128)(2,1)S(1)} %shard_map.55.own), channel_id=1, source_target_pairs={{0,4},{1,5},{2,6},{3,7},{4,0},{5,1},{6,2},{7,3},{8,12},{9,13},{10,... | collective-permute-start | bytes 1572872 | tf_op jit(solution)/shard_map/ppermute | solution.py:239
  8.7 1.6 %collective-permute-start.2 = (bf16[512,512]{1,0:T(8,128)(2,1)S(1)}, bf16[512,512]{1,0:T(8,128)(2,1)S(1)}, u32[]{:S(2)}, u32[]{:S(2)}) collective-permute-start(bf16[512,512]{1,0:T(8,128)(2,1)S(1)} %shard_map.55.own), channel_id=1, source_target_pairs={{0,2},{1,3},{2,0},{3,1},{4,6},{5,7},{6,4},{7,5},{8,10},{9,11},{10,... | collective-permute-start | bytes 1572872 | tf_op jit(solution)/shard_map/ppermute | solution.py:239
  10.2 0.0 copy-done.3
  10.3 0.0 collective-permute-done.3.other
  10.3 0.0 copy-done.1
  10.3 1.3 %shard_map.57 = (bf16[4,384,256]{2,1,0:T(8,128)(2,1)S(1)}, bf16[4,384,256]{2,1,0:T(8,128)(2,1)S(1)}, bf16[4,384,256]{2,1,0:T(8,128)(2,1)S(1)}, bf16[2,384,256]{2,1,0:T(8,128)(2,1)S(1)}, bf16[2,384,256]{2,1,0:T(8,128)(2,1)S(1)}) custom-call(bf16[384,4096]{1,0:T(8,128)(2,1)S(1)} %copy-done.1, f32[384,128]{1,0:T(8,128)S(1)} %shard_map.56.squares, ...), custom_call_target="tpu_custom_call" | custom-call | tf_op jit(solution)/shard_map/pallas_call | solution.py:74
  11.6 2.4 %collective-permute-start.4 = (bf16[2,384,256]{2,1,0:T(8,128)(2,1)S(1)}, bf16[2,384,256]{2,1,0:T(8,128)(2,1)S(1)}, u32[]{:S(2)}, u32[]{:S(2)}) collective-permute-start(bf16[2,384,256]{2,1,0:T(8,128)(2,1)S(1)} %get-tuple-element.16), channel_id=1, source_target_pairs={{0,24},{1,25},{2,26},{3,27},{4,28},{5,29},{6,30},{7,31}} | collective-permute-start | bytes 1179656 | tf_op jit(solution)/shard_map/ppermute | solution.py:239
  14.0 1.3 %collective-permute-start.8 = (bf16[2,384,256]{2,1,0:T(8,128)(2,1)S(1)}, bf16[2,384,256]{2,1,0:T(8,128)(2,1)S(1)}, u32[]{:S(2)}, u32[]{:S(2)}) collective-permute-start(bf16[2,384,256]{2,1,0:T(8,128)(2,1)S(1)} %get-tuple-element.20), channel_id=1, source_target_pairs={{0,16},{1,17},{2,18},{3,19},{4,20},{5,21},{6,22},{7,23}} | collective-permute-start | bytes 1179656 | tf_op jit(solution)/shard_map/ppermute | solution.py:239
  15.3 1.3 %collective-permute-start.6 = (bf16[4,384,256]{2,1,0:T(8,128)(2,1)S(1)}, bf16[4,384,256]{2,1,0:T(8,128)(2,1)S(1)}, u32[]{:S(2)}, u32[]{:S(2)}) collective-permute-start(bf16[4,384,256]{2,1,0:T(8,128)(2,1)S(1)} %get-tuple-element.18), channel_id=1, source_target_pairs={{0,8},{1,9},{2,10},{3,11},{4,12},{5,13},{6,14},{7,15}} | collective-permute-start | bytes 2359304 | tf_op jit(solution)/shard_map/ppermute | solution.py:239
  16.7 6.9 %collective-permute-done.4.rest_1_.d_low = bf16[2,384,256]{2,1,0:T(8,128)(2,1)S(1)} collective-permute-done((bf16[2,384,256]{2,1,0:T(8,128)(2,1)S(1)}, bf16[2,384,256]{2,1,0:T(8,128)(2,1)S(1)}, u32[]{:S(2)}, u32[]{:S(2)}) %collective-permute-start.4) | collective-permute-done | bytes 393248 | tf_op jit(solution)/shard_map/ppermute | solution.py:239
  23.5 1.3 %collective-permute-start.7 = (bf16[4,384,256]{2,1,0:T(8,128)(2,1)S(1)}, bf16[4,384,256]{2,1,0:T(8,128)(2,1)S(1)}, u32[]{:S(2)}, u32[]{:S(2)}) collective-permute-start(bf16[4,384,256]{2,1,0:T(8,128)(2,1)S(1)} %get-tuple-element.19), channel_id=1, source_target_pairs={{0,16},{1,17},{2,18},{3,19},{4,20},{5,21},{6,22},{7,23}} | collective-permute-start | bytes 2359304 | tf_op jit(solution)/shard_map/ppermute | solution.py:239
  24.9 0.0 collective-permute-done.8
  24.9 0.7 %collective-permute-start.9 = (bf16[2,384,256]{2,1,0:T(8,128)(2,1)S(1)}, bf16[2,384,256]{2,1,0:T(8,128)(2,1)S(1)}, u32[]{:S(2)}, u32[]{:S(2)}) collective-permute-start(bf16[2,384,256]{2,1,0:T(8,128)(2,1)S(1)} %collective-permute-done.8), channel_id=1, source_target_pairs={{16,24},{17,25},{18,26},{19,27},{20,28},{21,29},{22,30},{23,31}} | collective-permute-start | bytes 1179656 | tf_op jit(solution)/shard_map/ppermute | solution.py:239
  25.6 6.6 %collective-permute-done.1.x.far = bf16[512,512]{1,0:T(8,128)(2,1)S(1)} collective-permute-done((bf16[512,512]{1,0:T(8,128)(2,1)S(1)}, bf16[512,512]{1,0:T(8,128)(2,1)S(1)}, u32[]{:S(2)}, u32[]{:S(2)}) %collective-permute-start.1) | collective-permute-done | bytes 524320 | tf_op jit(solution)/shard_map/ppermute | solution.py:239
  32.1 0.2 collective-permute-done.2.rest_0_.near
  32.4 1.6 %collective-permute-start.5 = (bf16[512,512]{1,0:T(8,128)(2,1)S(1)}, bf16[512,512]{1,0:T(8,128)(2,1)S(1)}, u32[]{:S(2)}, u32[]{:S(2)}) collective-permute-start(bf16[512,512]{1,0:T(8,128)(2,1)S(1)} %shard_map.58), channel_id=1, source_target_pairs={{0,2},{1,3},{2,0},{3,1},{4,6},{5,7},{6,4},{7,5},{8,10},{9,11},{10,... | collective-permute-start | bytes 1572872 | tf_op jit(solution)/shard_map/ppermute | solution.py:239
  33.9 0.0 collective-permute-done.9.d_high
  33.9 4.9 %collective-permute-done.6.b = bf16[4,384,256]{2,1,0:T(8,128)(2,1)S(1)} collective-permute-done((bf16[4,384,256]{2,1,0:T(8,128)(2,1)S(1)}, bf16[4,384,256]{2,1,0:T(8,128)(2,1)S(1)}, u32[]{:S(2)}, u32[]{:S(2)}) %collective-permute-start.6) | collective-permute-done | bytes 786464 | tf_op jit(solution)/shard_map/ppermute | solution.py:239
  38.8 1.3 %collective-permute-done.7.c = bf16[4,384,256]{2,1,0:T(8,128)(2,1)S(1)} collective-permute-done((bf16[4,384,256]{2,1,0:T(8,128)(2,1)S(1)}, bf16[4,384,256]{2,1,0:T(8,128)(2,1)S(1)}, u32[]{:S(2)}, u32[]{:S(2)}) %collective-permute-start.7) | collective-permute-done | bytes 786464 | tf_op jit(solution)/shard_map/ppermute | solution.py:239
  40.1 0.1 shard_map.59
  40.2 0.1 collective-permute-start.10
  40.3 0.5 collective-permute-start.11
  40.8 1.2 %collective-permute-done.10.refs_2_ = bf16[2,384,256]{2,1,0:T(8,128)(2,1)S(1)} collective-permute-done((bf16[2,384,256]{2,1,0:T(8,128)(2,1)S(1)}, bf16[2,384,256]{2,1,0:T(8,128)(2,1)S(1)}, u32[]{:S(2)}, u32[]{:S(2)}) %collective-permute-start.10) | collective-permute-done | bytes 393248 | tf_op jit(solution)/shard_map/ppermute | solution.py:242
  42.0 0.6 %collective-permute-done.11.refs_3_ = bf16[2,384,256]{2,1,0:T(8,128)(2,1)S(1)} collective-permute-done((bf16[2,384,256]{2,1,0:T(8,128)(2,1)S(1)}, bf16[2,384,256]{2,1,0:T(8,128)(2,1)S(1)}, u32[]{:S(2)}, u32[]{:S(2)}) %collective-permute-start.11) | collective-permute-done | bytes 393248 | tf_op jit(solution)/shard_map/ppermute | solution.py:242
  42.5 0.8 %shard_map.60.refs_4_ = f32[384,512]{1,0:T(8,128)S(1)} custom-call(bf16[512,512]{1,0:T(8,128)(2,1)S(1)} %shard_map.55.own, bf16[512,512]{1,0:T(8,128)(2,1)S(1)} %collective-permute-done.2.rest_0_.near, bf16[512,512]{1,0:T(8,128)(2,1)S(1)} %collective-permute-done.1.x.far, bf16[2,384,256]{2,1,0:T(8,128)(2,1)S(1)} %get-tuple-element.21.refs_0_, ...), custom_call_target="tpu_custom_call" | custom-call | tf_op jit(solution)/shard_map/pallas_call | solution.py:74
  43.3 0.0 copy-start.4
  43.3 0.0 copy-start.2
  43.3 2.1 %collective-permute-done.5.last = bf16[512,512]{1,0:T(8,128)(2,1)S(1)} collective-permute-done((bf16[512,512]{1,0:T(8,128)(2,1)S(1)}, bf16[512,512]{1,0:T(8,128)(2,1)S(1)}, u32[]{:S(2)}, u32[]{:S(2)}) %collective-permute-start.5) | collective-permute-done | bytes 524320 | tf_op jit(solution)/shard_map/ppermute | solution.py:239
  45.5 0.4 shard_map.61
  45.9 0.6 %collective-permute-start.12 = (bf16[128,512]{1,0:T(8,128)(2,1)S(1)}, bf16[128,512]{1,0:T(8,128)(2,1)S(1)}, u32[]{:S(2)}, u32[]{:S(2)}) collective-permute-start(bf16[128,512]{1,0:T(8,128)(2,1)S(1)} %get-tuple-element.24), channel_id=1, source_target_pairs={{0,8},{1,9},{2,10},{3,11},{4,12},{5,13},{6,14},{7,15},{8,0},{9,1},... | collective-permute-start | bytes 393224 | tf_op jit(solution)/shard_map/ppermute | solution.py:239
  46.5 1.5 %collective-permute-start.13 = (bf16[128,512]{1,0:T(8,128)(2,1)S(1)}, bf16[128,512]{1,0:T(8,128)(2,1)S(1)}, u32[]{:S(2)}, u32[]{:S(2)}) collective-permute-start(bf16[128,512]{1,0:T(8,128)(2,1)S(1)} %get-tuple-element.25), channel_id=1, source_target_pairs={{0,16},{1,17},{2,18},{3,19},{4,20},{5,21},{6,22},{7,23},{8,24},{9,... | collective-permute-start | bytes 393224 | tf_op jit(solution)/shard_map/ppermute | solution.py:239
  48.0 1.5 %collective-permute-start.14 = (bf16[128,512]{1,0:T(8,128)(2,1)S(1)}, bf16[128,512]{1,0:T(8,128)(2,1)S(1)}, u32[]{:S(2)}, u32[]{:S(2)}) collective-permute-start(bf16[128,512]{1,0:T(8,128)(2,1)S(1)} %get-tuple-element.26), channel_id=1, source_target_pairs={{0,24},{1,25},{2,26},{3,27},{4,28},{5,29},{6,30},{7,31},{8,16},{9,... | collective-permute-start | bytes 393224 | tf_op jit(solution)/shard_map/ppermute | solution.py:239
  49.5 0.0 copy-done.4
  49.5 0.1 dynamic-slice_multiply_fusion
  49.6 2.0 %collective-permute-done.12.one = bf16[128,512]{1,0:T(8,128)(2,1)S(1)} collective-permute-done((bf16[128,512]{1,0:T(8,128)(2,1)S(1)}, bf16[128,512]{1,0:T(8,128)(2,1)S(1)}, u32[]{:S(2)}, u32[]{:S(2)}) %collective-permute-start.12) | collective-permute-done | bytes 131104 | tf_op jit(solution)/shard_map/ppermute | solution.py:239
  51.6 2.7 %collective-permute-done.13.two = bf16[128,512]{1,0:T(8,128)(2,1)S(1)} collective-permute-done((bf16[128,512]{1,0:T(8,128)(2,1)S(1)}, bf16[128,512]{1,0:T(8,128)(2,1)S(1)}, u32[]{:S(2)}, u32[]{:S(2)}) %collective-permute-start.13) | collective-permute-done | bytes 131104 | tf_op jit(solution)/shard_map/ppermute | solution.py:239
  54.3 0.0 collective-permute-done.14.three
  54.3 0.1 broadcast_in_dim.2.counts
  54.4 0.0 copy-done.2
  54.4 1.1 %shard_map.62 = bf16[256,2048]{1,0:T(8,128)(2,1)} custom-call(s32[2,128]{1,0:T(2,128)S(1)} %broadcast_in_dim.2.counts, f32[128,512]{1,0:T(8,128)S(1)} %get-tuple-element.23.mine, bf16[128,512]{1,0:T(8,128)(2,1)S(1)} %collective-permute-done.12.one, bf16[128,512]{1,0:T(8,128)(2,1)S(1)} %collective-permute-done.13.two, ...), custom_call_target="tpu_custom_call" | custom-call | tf_op jit(solution)/shard_map/pallas_call | solution.py:74
  (3 shorter events, 0.1 us)
Async XLA Ops:
  1.4 3.2 %collective-permute-start = (bf16[256,512]{1,0:T(8,128)(2,1)S(1)}, bf16[256,512]{1,0:T(8,128)(2,1)S(1)}, u32[]{:S(2)}, u32[]{:S(2)}) collective-permute-start(bf16[256,512]{1,0:T(8,128)(2,1)S(1)} %get-tuple-element.27), channel_id=1, source_target_pairs={{0,1},{1,0},{2,3},{3,2},{4,5},{5,4},{6,7},{7,6},{8,9},{9,8},{10,11... | collective-permute-start | bytes 786440 | tf_op jit(solution)/shard_map/ppermute | solution.py:242
  1.9 1.9 %copy-start = (bf16[384,4096]{1,0:T(8,128)(2,1)S(1)}, bf16[384,4096]{1,0:T(8,128)(2,1)}, u32[]{:S(2)}) copy-start(bf16[384,4096]{1,0:T(8,128)(2,1)} %x.3) | copy-start | bytes 9437188
  4.4 5.9 %copy-start.3 = (bf16[4096]{0:T(1024)(128)(2,1)S(1)}, bf16[4096]{0:T(1024)(128)(2,1)}, u32[]{:S(2)}) copy-start(bf16[4096]{0:T(1024)(128)(2,1)} %param.6) | copy-start | bytes 24580
  4.4 5.9 %copy-start.1 = (bf16[384,4096]{1,0:T(8,128)(2,1)S(1)}, bf16[384,4096]{1,0:T(8,128)(2,1)}, u32[]{:S(2)}) copy-start(bf16[384,4096]{1,0:T(8,128)(2,1)} %x.3) | copy-start | bytes 9437188
  4.4 5.9 %collective-permute-start.3 = (f32[384,128]{1,0:T(8,128)S(1)}, f32[384,128]{1,0:T(8,128)S(1)}, u32[]{:S(2)}, u32[]{:S(2)}) collective-permute-start(f32[384,128]{1,0:T(8,128)S(1)} %shard_map.56.squares), channel_id=1, source_target_pairs={{0,1},{1,0},{2,3},{3,2},{4,5},{5,4},{6,7},{7,6},{8,9},{9,8},{10,11... | collective-permute-start | bytes 589832 | tf_op jit(solution)/shard_map/ppermute | solution.py:242
  4.6 27.6 %collective-permute-start.1 = (bf16[512,512]{1,0:T(8,128)(2,1)S(1)}, bf16[512,512]{1,0:T(8,128)(2,1)S(1)}, u32[]{:S(2)}, u32[]{:S(2)}) collective-permute-start(bf16[512,512]{1,0:T(8,128)(2,1)S(1)} %shard_map.55.own), channel_id=1, source_target_pairs={{0,4},{1,5},{2,6},{3,7},{4,0},{5,1},{6,2},{7,3},{8,12},{9,13},{10,... | collective-permute-start | bytes 1572872 | tf_op jit(solution)/shard_map/ppermute | solution.py:239
  8.7 23.6 %collective-permute-start.2 = (bf16[512,512]{1,0:T(8,128)(2,1)S(1)}, bf16[512,512]{1,0:T(8,128)(2,1)S(1)}, u32[]{:S(2)}, u32[]{:S(2)}) collective-permute-start(bf16[512,512]{1,0:T(8,128)(2,1)S(1)} %shard_map.55.own), channel_id=1, source_target_pairs={{0,2},{1,3},{2,0},{3,1},{4,6},{5,7},{6,4},{7,5},{8,10},{9,11},{10,... | collective-permute-start | bytes 1572872 | tf_op jit(solution)/shard_map/ppermute | solution.py:239
  11.6 11.9 %collective-permute-start.4 = (bf16[2,384,256]{2,1,0:T(8,128)(2,1)S(1)}, bf16[2,384,256]{2,1,0:T(8,128)(2,1)S(1)}, u32[]{:S(2)}, u32[]{:S(2)}) collective-permute-start(bf16[2,384,256]{2,1,0:T(8,128)(2,1)S(1)} %get-tuple-element.16), channel_id=1, source_target_pairs={{0,24},{1,25},{2,26},{3,27},{4,28},{5,29},{6,30},{7,31}} | collective-permute-start | bytes 1179656 | tf_op jit(solution)/shard_map/ppermute | solution.py:239
  14.0 10.9 %collective-permute-start.8 = (bf16[2,384,256]{2,1,0:T(8,128)(2,1)S(1)}, bf16[2,384,256]{2,1,0:T(8,128)(2,1)S(1)}, u32[]{:S(2)}, u32[]{:S(2)}) collective-permute-start(bf16[2,384,256]{2,1,0:T(8,128)(2,1)S(1)} %get-tuple-element.20), channel_id=1, source_target_pairs={{0,16},{1,17},{2,18},{3,19},{4,20},{5,21},{6,22},{7,23}} | collective-permute-start | bytes 1179656 | tf_op jit(solution)/shard_map/ppermute | solution.py:239
  15.3 23.5 %collective-permute-start.6 = (bf16[4,384,256]{2,1,0:T(8,128)(2,1)S(1)}, bf16[4,384,256]{2,1,0:T(8,128)(2,1)S(1)}, u32[]{:S(2)}, u32[]{:S(2)}) collective-permute-start(bf16[4,384,256]{2,1,0:T(8,128)(2,1)S(1)} %get-tuple-element.18), channel_id=1, source_target_pairs={{0,8},{1,9},{2,10},{3,11},{4,12},{5,13},{6,14},{7,15}} | collective-permute-start | bytes 2359304 | tf_op jit(solution)/shard_map/ppermute | solution.py:239
  23.5 16.6 %collective-permute-start.7 = (bf16[4,384,256]{2,1,0:T(8,128)(2,1)S(1)}, bf16[4,384,256]{2,1,0:T(8,128)(2,1)S(1)}, u32[]{:S(2)}, u32[]{:S(2)}) collective-permute-start(bf16[4,384,256]{2,1,0:T(8,128)(2,1)S(1)} %get-tuple-element.19), channel_id=1, source_target_pairs={{0,16},{1,17},{2,18},{3,19},{4,20},{5,21},{6,22},{7,23}} | collective-permute-start | bytes 2359304 | tf_op jit(solution)/shard_map/ppermute | solution.py:239
  24.9 9.0 %collective-permute-start.9 = (bf16[2,384,256]{2,1,0:T(8,128)(2,1)S(1)}, bf16[2,384,256]{2,1,0:T(8,128)(2,1)S(1)}, u32[]{:S(2)}, u32[]{:S(2)}) collective-permute-start(bf16[2,384,256]{2,1,0:T(8,128)(2,1)S(1)} %collective-permute-done.8), channel_id=1, source_target_pairs={{16,24},{17,25},{18,26},{19,27},{20,28},{21,29},{22,30},{23,31}} | collective-permute-start | bytes 1179656 | tf_op jit(solution)/shard_map/ppermute | solution.py:239
  32.4 13.1 %collective-permute-start.5 = (bf16[512,512]{1,0:T(8,128)(2,1)S(1)}, bf16[512,512]{1,0:T(8,128)(2,1)S(1)}, u32[]{:S(2)}, u32[]{:S(2)}) collective-permute-start(bf16[512,512]{1,0:T(8,128)(2,1)S(1)} %shard_map.58), channel_id=1, source_target_pairs={{0,2},{1,3},{2,0},{3,1},{4,6},{5,7},{6,4},{7,5},{8,10},{9,11},{10,... | collective-permute-start | bytes 1572872 | tf_op jit(solution)/shard_map/ppermute | solution.py:239
  40.2 1.8 %collective-permute-start.10 = (bf16[2,384,256]{2,1,0:T(8,128)(2,1)S(1)}, bf16[2,384,256]{2,1,0:T(8,128)(2,1)S(1)}, u32[]{:S(2)}, u32[]{:S(2)}) collective-permute-start(bf16[2,384,256]{2,1,0:T(8,128)(2,1)S(1)} %get-tuple-element.21.refs_0_), channel_id=1, source_target_pairs={{0,1},{1,0},{2,3},{3,2},{4,5},{5,4},{6,7},{7,6},{8,9},{9,8},{10,11... | collective-permute-start | bytes 1179656 | tf_op jit(solution)/shard_map/ppermute | solution.py:242
  40.3 2.3 %collective-permute-start.11 = (bf16[2,384,256]{2,1,0:T(8,128)(2,1)S(1)}, bf16[2,384,256]{2,1,0:T(8,128)(2,1)S(1)}, u32[]{:S(2)}, u32[]{:S(2)}) collective-permute-start(bf16[2,384,256]{2,1,0:T(8,128)(2,1)S(1)} %get-tuple-element.22.refs_1_), channel_id=1, source_target_pairs={{0,1},{1,0},{2,3},{3,2},{4,5},{5,4},{6,7},{7,6},{8,9},{9,8},{10,11... | collective-permute-start | bytes 1179656 | tf_op jit(solution)/shard_map/ppermute | solution.py:242
  43.3 6.2 %copy-start.4 = (s32[6]{0:T(128)S(1)}, s32[6]{0:T(128)}, u32[]{:S(2)}) copy-start(s32[6]{0:T(128)} %param.8) | copy-start | bytes 76
  43.3 11.0 %copy-start.2 = (bf16[256,2048]{1,0:T(8,128)(2,1)S(1)}, bf16[256,2048]{1,0:T(8,128)(2,1)}, u32[]{:S(2)}) copy-start(bf16[256,2048]{1,0:T(8,128)(2,1)} %q_ref.1) | copy-start | bytes 3145732
  45.9 5.7 %collective-permute-start.12 = (bf16[128,512]{1,0:T(8,128)(2,1)S(1)}, bf16[128,512]{1,0:T(8,128)(2,1)S(1)}, u32[]{:S(2)}, u32[]{:S(2)}) collective-permute-start(bf16[128,512]{1,0:T(8,128)(2,1)S(1)} %get-tuple-element.24), channel_id=1, source_target_pairs={{0,8},{1,9},{2,10},{3,11},{4,12},{5,13},{6,14},{7,15},{8,0},{9,1},... | collective-permute-start | bytes 393224 | tf_op jit(solution)/shard_map/ppermute | solution.py:239
  46.5 7.8 %collective-permute-start.13 = (bf16[128,512]{1,0:T(8,128)(2,1)S(1)}, bf16[128,512]{1,0:T(8,128)(2,1)S(1)}, u32[]{:S(2)}, u32[]{:S(2)}) collective-permute-start(bf16[128,512]{1,0:T(8,128)(2,1)S(1)} %get-tuple-element.25), channel_id=1, source_target_pairs={{0,16},{1,17},{2,18},{3,19},{4,20},{5,21},{6,22},{7,23},{8,24},{9,... | collective-permute-start | bytes 393224 | tf_op jit(solution)/shard_map/ppermute | solution.py:239
  48.0 6.3 %collective-permute-start.14 = (bf16[128,512]{1,0:T(8,128)(2,1)S(1)}, bf16[128,512]{1,0:T(8,128)(2,1)S(1)}, u32[]{:S(2)}, u32[]{:S(2)}) collective-permute-start(bf16[128,512]{1,0:T(8,128)(2,1)S(1)} %get-tuple-element.26), channel_id=1, source_target_pairs={{0,24},{1,25},{2,26},{3,27},{4,28},{5,29},{6,30},{7,31},{8,16},{9,... | collective-permute-start | bytes 393224 | tf_op jit(solution)/shard_map/ppermute | solution.py:239

commit v5 on v4

--- a/solution.py
+++ b/solution.py
@@ -88,7 +88,9 @@
     out[rows:, :] = other[...]
 
 
-def row_squares(x, squares):
+def row_squares(x, after, squares):
+    del after
+
     @pl.when(lax.axis_index("grp") == 0)
     def _():
         total = None
@@ -252,7 +254,7 @@
 
     near, far = swap_planes(own, 1), swap_planes(own, 2)
 
-    squares = call(row_squares, [((n_rows, 128), f32)], image_rows)[0]
+    squares = call(row_squares, [((n_rows, 128), f32)], image_rows, own, specs=[VMEM, ANY])[0]
     whole, part = ((4, n_rows, quarter), bf16), ((2, n_rows, quarter), bf16)
     a, b, c, d_low, d_high = call(
         normalise,
@@ -264,8 +266,9 @@
     )
     to_b, to_c, to_d = ([((0, z), (h, z)) for z in planes] for h in (1, 2, 3))
     d_low, d_high = send(d_low, to_d), send(d_high, to_c)
+    c = call(later, [whole], c, d_low, specs=[VMEM, ANY], cost=0)[0]
     b, c = send(b, to_b), send(c, to_c)
-    last = call(later, [(shape, bf16)], far, near, d_low, specs=[VMEM, ANY, ANY], cost=COST)[0]
+    last = call(later, [(shape, bf16)], far, near, specs=[VMEM, ANY], cost=COST)[0]
     last = swap_planes(last, 1)
     d_high = send(d_high, [((2, z), (3, z)) for z in planes])
     rows = call(landed, [part] * 2, a, b, c, d_low, d_high)
@@ -284,7 +287,7 @@
     )
     parts = [
         send(x, [((c, z), (c ^ k, z)) for c in range(4) for z in planes])
-        for k, x in zip((1, 2, 3), parts)
+        for k, x in zip((3, 1, 2), (parts[2], parts[0], parts[1]))
     ]
     return call(
         attention,

time: 55.7 us -> 55.4 us (level)
  local copies, waits for them, and re-layouts: 3.34 us -> 1.62 us
  waiting for transfers between devices: 28.5 us -> 29.9 us
    unnamed x10 -> x8, local copies, waits for them, and re-layouts: 1.91 us -> 0.19 us
    ppermute x4, waiting for transfers between devices: 1.78 us -> 2.94 us  [swap(): return lax.ppermute(x, 'tp', [(0, 1), (1, 0)])]
    pallas_call x8 -> x9, Pallas kernels: 4.34 us -> 4.4 us  [call(): pl.pallas_call(body, out_shape=outs, in_specs=specs or [VMEM] * len(args)...]
  transfers between devices with their start and end apart: 15 -> 15, of which waited for: 10 -> 12; matrix products, arithmetic and copies ran while one was open for 0% -> 0% of each run, Pallas kernels for 5% -> 4%
where the time goes in v5:
time: 55.4 us; the launch traced here: 55.1 us
  waiting for transfers between devices  29.9 us (54%)
  starting transfers between devices  18.9 us (34%)
  Pallas kernels  4.4 us (8%)
  local copies, waits for them, and re-layouts  1.62 us (3%)
    ppermute x11, waiting for transfers between devices, send(): lax.ppermute(x, AXES, [(index(a, c), index(b, c)) for a, b in pairs for c...  27 us
    ppermute x11, starting transfers between devices, send(): lax.ppermute(x, AXES, [(index(a, c), index(b, c)) for a, b in pairs for c...  17.3 us
    pallas_call x9, Pallas kernels, call(): pl.pallas_call(body, out_shape=outs, in_specs=specs or [VMEM] * len(args)...  4.4 us
    ppermute x4, waiting for transfers between devices, swap(): return lax.ppermute(x, 'tp', [(0, 1), (1, 0)])  2.94 us
    ppermute x4, starting transfers between devices, swap(): return lax.ppermute(x, 'tp', [(0, 1), (1, 0)])  1.59 us
    dynamic_slice x1, local copies, waits for them, and re-layouts, shards_line(): given = lax.dynamic_slice_in_dim(w, (1 - t) * half, half, axis=1)  1.35 us
  transfers between devices with their start and end apart: 15, of which 12 were waited for; matrix products, arithmetic and copies ran while one was open for 0% of the time, Pallas kernels for 4%

profile of v5, /device:TPU:0, one launch (start us, length us, event | category | flops | bytes accessed | tf_op | source)
XLA Modules:
  0.0 55.1 jit_solution(3553929880974211401)
XLA Ops:
  0.0 1.4 %fusion = (bf16[256,512]{1,0:T(8,128)(2,1)S(1)}, bf16[256,512]{1,0:T(8,128)(2,1)S(1)}) fusion(bf16[1024,1024]{1,0:T(8,128)(2,1)} %param.7, s32[]{:T(128)S(6)} %select_n.20, s32[]{:T(128)S(6)} %select_n.24, s32[]{:T(128)S(6)} %select_n.22), kind=kLoop, calls=%fused_computation.1 | loop fusion | bytes 1048588 | tf_op jit(solution)/shard_map/dynamic_slice | solution.py:248
  1.4 0.0 copy-start
  1.4 0.5 collective-permute-start
  1.9 1.2 %collective-permute-done.other = bf16[256,512]{1,0:T(8,128)(2,1)S(1)} collective-permute-done((bf16[256,512]{1,0:T(8,128)(2,1)S(1)}, bf16[256,512]{1,0:T(8,128)(2,1)S(1)}, u32[]{:S(2)}, u32[]{:S(2)}) %collective-permute-start) | collective-permute-done | bytes 262176 | tf_op jit(solution)/shard_map/ppermute | solution.py:244
  3.1 0.2 copy-done
  3.2 0.0 copy-start.2
  3.2 0.6 %shard_map.57.squares = f32[384,128]{1,0:T(8,128)S(1)} custom-call(bf16[384,4096]{1,0:T(8,128)(2,1)S(1)} %copy-done, bf16[512,512]{1,0:T(8,128)(2,1)S(1)} %shard_map.55.after.own), custom_call_target="tpu_custom_call" | custom-call | tf_op jit(solution)/shard_map/pallas_call | solution.py:74
  3.9 0.5 collective-permute-start.4
  4.4 3.7 %collective-permute-start.1 = (bf16[512,512]{1,0:T(8,128)(2,1)S(1)}, bf16[512,512]{1,0:T(8,128)(2,1)S(1)}, u32[]{:S(2)}, u32[]{:S(2)}) collective-permute-start(bf16[512,512]{1,0:T(8,128)(2,1)S(1)} %shard_map.55.after.own), channel_id=1, source_target_pairs={{0,4},{1,5},{2,6},{3,7},{4,0},{5,1},{6,2},{7,3},{8,12},{9,13},{10,... | collective-permute-start | bytes 1572872 | tf_op jit(solution)/shard_map/ppermute | solution.py:241
  8.0 1.6 %collective-permute-start.2 = (bf16[512,512]{1,0:T(8,128)(2,1)S(1)}, bf16[512,512]{1,0:T(8,128)(2,1)S(1)}, u32[]{:S(2)}, u32[]{:S(2)}) collective-permute-start(bf16[512,512]{1,0:T(8,128)(2,1)S(1)} %shard_map.55.after.own), channel_id=1, source_target_pairs={{0,2},{1,3},{2,0},{3,1},{4,6},{5,7},{6,4},{7,5},{8,10},{9,11},{10,... | collective-permute-start | bytes 1572872 | tf_op jit(solution)/shard_map/ppermute | solution.py:241
  9.6 0.0 copy-done.2
  9.6 0.0 collective-permute-done.4.other
  9.6 1.3 %shard_map.58 = (bf16[4,384,256]{2,1,0:T(8,128)(2,1)S(1)}, bf16[4,384,256]{2,1,0:T(8,128)(2,1)S(1)}, bf16[4,384,256]{2,1,0:T(8,128)(2,1)S(1)}, bf16[2,384,256]{2,1,0:T(8,128)(2,1)S(1)}, bf16[2,384,256]{2,1,0:T(8,128)(2,1)S(1)}) custom-call(bf16[384,4096]{1,0:T(8,128)(2,1)S(1)} %copy-done, f32[384,128]{1,0:T(8,128)S(1)} %shard_map.57.squares, ...), custom_call_target="tpu_custom_call" | custom-call | tf_op jit(solution)/shard_map/pallas_call | solution.py:74
  11.0 2.3 %collective-permute-start.6 = (bf16[2,384,256]{2,1,0:T(8,128)(2,1)S(1)}, bf16[2,384,256]{2,1,0:T(8,128)(2,1)S(1)}, u32[]{:S(2)}, u32[]{:S(2)}) collective-permute-start(bf16[2,384,256]{2,1,0:T(8,128)(2,1)S(1)} %get-tuple-element.19), channel_id=1, source_target_pairs={{0,24},{1,25},{2,26},{3,27},{4,28},{5,29},{6,30},{7,31}} | collective-permute-start | bytes 1179656 | tf_op jit(solution)/shard_map/ppermute | solution.py:241
  13.3 1.3 %collective-permute-start.8 = (bf16[2,384,256]{2,1,0:T(8,128)(2,1)S(1)}, bf16[2,384,256]{2,1,0:T(8,128)(2,1)S(1)}, u32[]{:S(2)}, u32[]{:S(2)}) collective-permute-start(bf16[2,384,256]{2,1,0:T(8,128)(2,1)S(1)} %get-tuple-element.20), channel_id=1, source_target_pairs={{0,16},{1,17},{2,18},{3,19},{4,20},{5,21},{6,22},{7,23}} | collective-permute-start | bytes 1179656 | tf_op jit(solution)/shard_map/ppermute | solution.py:241
  14.6 1.3 %collective-permute-start.5 = (bf16[4,384,256]{2,1,0:T(8,128)(2,1)S(1)}, bf16[4,384,256]{2,1,0:T(8,128)(2,1)S(1)}, u32[]{:S(2)}, u32[]{:S(2)}) collective-permute-start(bf16[4,384,256]{2,1,0:T(8,128)(2,1)S(1)} %get-tuple-element.17), channel_id=1, source_target_pairs={{0,8},{1,9},{2,10},{3,11},{4,12},{5,13},{6,14},{7,15}} | collective-permute-start | bytes 2359304 | tf_op jit(solution)/shard_map/ppermute | solution.py:241
  16.0 6.8 %collective-permute-done.6.rest_0_.d_low = bf16[2,384,256]{2,1,0:T(8,128)(2,1)S(1)} collective-permute-done((bf16[2,384,256]{2,1,0:T(8,128)(2,1)S(1)}, bf16[2,384,256]{2,1,0:T(8,128)(2,1)S(1)}, u32[]{:S(2)}, u32[]{:S(2)}) %collective-permute-start.6) | collective-permute-done | bytes 393248 | tf_op jit(solution)/shard_map/ppermute | solution.py:241
  22.8 0.1 shard_map.59
  22.8 1.3 %collective-permute-start.7 = (bf16[4,384,256]{2,1,0:T(8,128)(2,1)S(1)}, bf16[4,384,256]{2,1,0:T(8,128)(2,1)S(1)}, u32[]{:S(2)}, u32[]{:S(2)}) collective-permute-start(bf16[4,384,256]{2,1,0:T(8,128)(2,1)S(1)} %shard_map.59), channel_id=1, source_target_pairs={{0,16},{1,17},{2,18},{3,19},{4,20},{5,21},{6,22},{7,23}} | collective-permute-start | bytes 2359304 | tf_op jit(solution)/shard_map/ppermute | solution.py:241
  24.2 0.0 collective-permute-done.8
  24.2 0.7 %collective-permute-start.9 = (bf16[2,384,256]{2,1,0:T(8,128)(2,1)S(1)}, bf16[2,384,256]{2,1,0:T(8,128)(2,1)S(1)}, u32[]{:S(2)}, u32[]{:S(2)}) collective-permute-start(bf16[2,384,256]{2,1,0:T(8,128)(2,1)S(1)} %collective-permute-done.8), channel_id=1, source_target_pairs={{16,24},{17,25},{18,26},{19,27},{20,28},{21,29},{22,30},{23,31}} | collective-permute-start | bytes 1179656 | tf_op jit(solution)/shard_map/ppermute | solution.py:241
  24.9 7.0 %collective-permute-done.1.x.far = bf16[512,512]{1,0:T(8,128)(2,1)S(1)} collective-permute-done((bf16[512,512]{1,0:T(8,128)(2,1)S(1)}, bf16[512,512]{1,0:T(8,128)(2,1)S(1)}, u32[]{:S(2)}, u32[]{:S(2)}) %collective-permute-start.1) | collective-permute-done | bytes 524320 | tf_op jit(solution)/shard_map/ppermute | solution.py:241
  31.9 0.2 collective-permute-done.2.rest_0_.near
  32.1 1.6 %collective-permute-start.3 = (bf16[512,512]{1,0:T(8,128)(2,1)S(1)}, bf16[512,512]{1,0:T(8,128)(2,1)S(1)}, u32[]{:S(2)}, u32[]{:S(2)}) collective-permute-start(bf16[512,512]{1,0:T(8,128)(2,1)S(1)} %shard_map.56), channel_id=1, source_target_pairs={{0,2},{1,3},{2,0},{3,1},{4,6},{5,7},{6,4},{7,5},{8,10},{9,11},{10,... | collective-permute-start | bytes 1572872 | tf_op jit(solution)/shard_map/ppermute | solution.py:241
  33.7 0.0 collective-permute-done.9.d_high
  33.7 4.9 %collective-permute-done.5.b = bf16[4,384,256]{2,1,0:T(8,128)(2,1)S(1)} collective-permute-done((bf16[4,384,256]{2,1,0:T(8,128)(2,1)S(1)}, bf16[4,384,256]{2,1,0:T(8,128)(2,1)S(1)}, u32[]{:S(2)}, u32[]{:S(2)}) %collective-permute-start.5) | collective-permute-done | bytes 786464 | tf_op jit(solution)/shard_map/ppermute | solution.py:241
  38.6 1.3 %collective-permute-done.7.c = bf16[4,384,256]{2,1,0:T(8,128)(2,1)S(1)} collective-permute-done((bf16[4,384,256]{2,1,0:T(8,128)(2,1)S(1)}, bf16[4,384,256]{2,1,0:T(8,128)(2,1)S(1)}, u32[]{:S(2)}, u32[]{:S(2)}) %collective-permute-start.7) | collective-permute-done | bytes 786464 | tf_op jit(solution)/shard_map/ppermute | solution.py:241
  39.9 0.1 shard_map.60
  40.0 0.1 collective-permute-start.10
  40.1 0.5 collective-permute-start.11
  40.6 1.2 %collective-permute-done.10.refs_2_ = bf16[2,384,256]{2,1,0:T(8,128)(2,1)S(1)} collective-permute-done((bf16[2,384,256]{2,1,0:T(8,128)(2,1)S(1)}, bf16[2,384,256]{2,1,0:T(8,128)(2,1)S(1)}, u32[]{:S(2)}, u32[]{:S(2)}) %collective-permute-start.10) | collective-permute-done | bytes 393248 | tf_op jit(solution)/shard_map/ppermute | solution.py:244
  41.8 0.6 %collective-permute-done.11.refs_3_ = bf16[2,384,256]{2,1,0:T(8,128)(2,1)S(1)} collective-permute-done((bf16[2,384,256]{2,1,0:T(8,128)(2,1)S(1)}, bf16[2,384,256]{2,1,0:T(8,128)(2,1)S(1)}, u32[]{:S(2)}, u32[]{:S(2)}) %collective-permute-start.11) | collective-permute-done | bytes 393248 | tf_op jit(solution)/shard_map/ppermute | solution.py:244
  42.3 0.8 %shard_map.61.refs_4_ = f32[384,512]{1,0:T(8,128)S(1)} custom-call(bf16[512,512]{1,0:T(8,128)(2,1)S(1)} %shard_map.55.after.own, bf16[512,512]{1,0:T(8,128)(2,1)S(1)} %collective-permute-done.2.rest_0_.near, bf16[512,512]{1,0:T(8,128)(2,1)S(1)} %collective-permute-done.1.x.far, bf16[2,384,256]{2,1,0:T(8,128)(2,1)S(1)} %get-tuple-element.21.refs_0_, ...), custom_call_target="tpu_custom_call" | custom-call | tf_op jit(solution)/shard_map/pallas_call | solution.py:74
  43.1 0.0 copy-start.3
  43.1 0.0 copy-start.1
  43.1 2.5 %collective-permute-done.3.last = bf16[512,512]{1,0:T(8,128)(2,1)S(1)} collective-permute-done((bf16[512,512]{1,0:T(8,128)(2,1)S(1)}, bf16[512,512]{1,0:T(8,128)(2,1)S(1)}, u32[]{:S(2)}, u32[]{:S(2)}) %collective-permute-start.3) | collective-permute-done | bytes 524320 | tf_op jit(solution)/shard_map/ppermute | solution.py:241
  45.6 0.4 shard_map.62
  46.1 1.8 %collective-permute-start.12 = (bf16[128,512]{1,0:T(8,128)(2,1)S(1)}, bf16[128,512]{1,0:T(8,128)(2,1)S(1)}, u32[]{:S(2)}, u32[]{:S(2)}) collective-permute-start(bf16[128,512]{1,0:T(8,128)(2,1)S(1)} %get-tuple-element.24), channel_id=1, source_target_pairs={{0,24},{1,25},{2,26},{3,27},{4,28},{5,29},{6,30},{7,31},{8,16},{9,... | collective-permute-start | bytes 393224 | tf_op jit(solution)/shard_map/ppermute | solution.py:241
  47.8 0.5 collective-permute-start.13
  48.4 1.3 %collective-permute-start.14 = (bf16[128,512]{1,0:T(8,128)(2,1)S(1)}, bf16[128,512]{1,0:T(8,128)(2,1)S(1)}, u32[]{:S(2)}, u32[]{:S(2)}) collective-permute-start(bf16[128,512]{1,0:T(8,128)(2,1)S(1)} %get-tuple-element.26), channel_id=1, source_target_pairs={{0,16},{1,17},{2,18},{3,19},{4,20},{5,21},{6,22},{7,23},{8,24},{9,... | collective-permute-start | bytes 393224 | tf_op jit(solution)/shard_map/ppermute | solution.py:241
  49.6 0.0 copy-done.3
  49.6 0.1 dynamic-slice_multiply_fusion
  49.7 2.9 %collective-permute-done.12.one = bf16[128,512]{1,0:T(8,128)(2,1)S(1)} collective-permute-done((bf16[128,512]{1,0:T(8,128)(2,1)S(1)}, bf16[128,512]{1,0:T(8,128)(2,1)S(1)}, u32[]{:S(2)}, u32[]{:S(2)}) %collective-permute-start.12) | collective-permute-done | bytes 131104 | tf_op jit(solution)/shard_map/ppermute | solution.py:241
  52.6 1.3 %collective-permute-done.13.two = bf16[128,512]{1,0:T(8,128)(2,1)S(1)} collective-permute-done((bf16[128,512]{1,0:T(8,128)(2,1)S(1)}, bf16[128,512]{1,0:T(8,128)(2,1)S(1)}, u32[]{:S(2)}, u32[]{:S(2)}) %collective-permute-start.13) | collective-permute-done | bytes 131104 | tf_op jit(solution)/shard_map/ppermute | solution.py:241
  53.9 0.1 collective-permute-done.14.three
  54.0 0.1 broadcast_in_dim.2.counts
  54.1 0.0 copy-done.1
  54.1 1.1 %shard_map.63 = bf16[256,2048]{1,0:T(8,128)(2,1)} custom-call(s32[2,128]{1,0:T(2,128)S(1)} %broadcast_in_dim.2.counts, f32[128,512]{1,0:T(8,128)S(1)} %get-tuple-element.23.mine, bf16[128,512]{1,0:T(8,128)(2,1)S(1)} %collective-permute-done.12.one, bf16[128,512]{1,0:T(8,128)(2,1)S(1)} %collective-permute-done.13.two, ...), custom_call_target="tpu_custom_call" | custom-call | tf_op jit(solution)/shard_map/pallas_call | solution.py:74
  (3 shorter events, 0.1 us)
Async XLA Ops:
  1.4 1.9 %copy-start = (bf16[384,4096]{1,0:T(8,128)(2,1)S(1)}, bf16[384,4096]{1,0:T(8,128)(2,1)}, u32[]{:S(2)}) copy-start(bf16[384,4096]{1,0:T(8,128)(2,1)} %x.3) | copy-start | bytes 9437188
  1.4 1.7 %collective-permute-start = (bf16[256,512]{1,0:T(8,128)(2,1)S(1)}, bf16[256,512]{1,0:T(8,128)(2,1)S(1)}, u32[]{:S(2)}, u32[]{:S(2)}) collective-permute-start(bf16[256,512]{1,0:T(8,128)(2,1)S(1)} %get-tuple-element.27), channel_id=1, source_target_pairs={{0,1},{1,0},{2,3},{3,2},{4,5},{5,4},{6,7},{7,6},{8,9},{9,8},{10,11... | collective-permute-start | bytes 786440 | tf_op jit(solution)/shard_map/ppermute | solution.py:244
  3.2 6.4 %copy-start.2 = (bf16[4096]{0:T(1024)(128)(2,1)S(1)}, bf16[4096]{0:T(1024)(128)(2,1)}, u32[]{:S(2)}) copy-start(bf16[4096]{0:T(1024)(128)(2,1)} %param.6) | copy-start | bytes 24580
  3.9 5.8 %collective-permute-start.4 = (f32[384,128]{1,0:T(8,128)S(1)}, f32[384,128]{1,0:T(8,128)S(1)}, u32[]{:S(2)}, u32[]{:S(2)}) collective-permute-start(f32[384,128]{1,0:T(8,128)S(1)} %shard_map.57.squares), channel_id=1, source_target_pairs={{0,1},{1,0},{2,3},{3,2},{4,5},{5,4},{6,7},{7,6},{8,9},{9,8},{10,11... | collective-permute-start | bytes 589832 | tf_op jit(solution)/shard_map/ppermute | solution.py:244
  4.4 27.5 %collective-permute-start.1 = (bf16[512,512]{1,0:T(8,128)(2,1)S(1)}, bf16[512,512]{1,0:T(8,128)(2,1)S(1)}, u32[]{:S(2)}, u32[]{:S(2)}) collective-permute-start(bf16[512,512]{1,0:T(8,128)(2,1)S(1)} %shard_map.55.after.own), channel_id=1, source_target_pairs={{0,4},{1,5},{2,6},{3,7},{4,0},{5,1},{6,2},{7,3},{8,12},{9,13},{10,... | collective-permute-start | bytes 1572872 | tf_op jit(solution)/shard_map/ppermute | solution.py:241
  8.0 24.1 %collective-permute-start.2 = (bf16[512,512]{1,0:T(8,128)(2,1)S(1)}, bf16[512,512]{1,0:T(8,128)(2,1)S(1)}, u32[]{:S(2)}, u32[]{:S(2)}) collective-permute-start(bf16[512,512]{1,0:T(8,128)(2,1)S(1)} %shard_map.55.after.own), channel_id=1, source_target_pairs={{0,2},{1,3},{2,0},{3,1},{4,6},{5,7},{6,4},{7,5},{8,10},{9,11},{10,... | collective-permute-start | bytes 1572872 | tf_op jit(solution)/shard_map/ppermute | solution.py:241
  11.0 11.8 %collective-permute-start.6 = (bf16[2,384,256]{2,1,0:T(8,128)(2,1)S(1)}, bf16[2,384,256]{2,1,0:T(8,128)(2,1)S(1)}, u32[]{:S(2)}, u32[]{:S(2)}) collective-permute-start(bf16[2,384,256]{2,1,0:T(8,128)(2,1)S(1)} %get-tuple-element.19), channel_id=1, source_target_pairs={{0,24},{1,25},{2,26},{3,27},{4,28},{5,29},{6,30},{7,31}} | collective-permute-start | bytes 1179656 | tf_op jit(solution)/shard_map/ppermute | solution.py:241
  13.3 10.9 %collective-permute-start.8 = (bf16[2,384,256]{2,1,0:T(8,128)(2,1)S(1)}, bf16[2,384,256]{2,1,0:T(8,128)(2,1)S(1)}, u32[]{:S(2)}, u32[]{:S(2)}) collective-permute-start(bf16[2,384,256]{2,1,0:T(8,128)(2,1)S(1)} %get-tuple-element.20), channel_id=1, source_target_pairs={{0,16},{1,17},{2,18},{3,19},{4,20},{5,21},{6,22},{7,23}} | collective-permute-start | bytes 1179656 | tf_op jit(solution)/shard_map/ppermute | solution.py:241
  14.6 24.0 %collective-permute-start.5 = (bf16[4,384,256]{2,1,0:T(8,128)(2,1)S(1)}, bf16[4,384,256]{2,1,0:T(8,128)(2,1)S(1)}, u32[]{:S(2)}, u32[]{:S(2)}) collective-permute-start(bf16[4,384,256]{2,1,0:T(8,128)(2,1)S(1)} %get-tuple-element.17), channel_id=1, source_target_pairs={{0,8},{1,9},{2,10},{3,11},{4,12},{5,13},{6,14},{7,15}} | collective-permute-start | bytes 2359304 | tf_op jit(solution)/shard_map/ppermute | solution.py:241
  22.8 17.1 %collective-permute-start.7 = (bf16[4,384,256]{2,1,0:T(8,128)(2,1)S(1)}, bf16[4,384,256]{2,1,0:T(8,128)(2,1)S(1)}, u32[]{:S(2)}, u32[]{:S(2)}) collective-permute-start(bf16[4,384,256]{2,1,0:T(8,128)(2,1)S(1)} %shard_map.59), channel_id=1, source_target_pairs={{0,16},{1,17},{2,18},{3,19},{4,20},{5,21},{6,22},{7,23}} | collective-permute-start | bytes 2359304 | tf_op jit(solution)/shard_map/ppermute | solution.py:241
  24.2 9.5 %collective-permute-start.9 = (bf16[2,384,256]{2,1,0:T(8,128)(2,1)S(1)}, bf16[2,384,256]{2,1,0:T(8,128)(2,1)S(1)}, u32[]{:S(2)}, u32[]{:S(2)}) collective-permute-start(bf16[2,384,256]{2,1,0:T(8,128)(2,1)S(1)} %collective-permute-done.8), channel_id=1, source_target_pairs={{16,24},{17,25},{18,26},{19,27},{20,28},{21,29},{22,30},{23,31}} | collective-permute-start | bytes 1179656 | tf_op jit(solution)/shard_map/ppermute | solution.py:241
  32.1 13.5 %collective-permute-start.3 = (bf16[512,512]{1,0:T(8,128)(2,1)S(1)}, bf16[512,512]{1,0:T(8,128)(2,1)S(1)}, u32[]{:S(2)}, u32[]{:S(2)}) collective-permute-start(bf16[512,512]{1,0:T(8,128)(2,1)S(1)} %shard_map.56), channel_id=1, source_target_pairs={{0,2},{1,3},{2,0},{3,1},{4,6},{5,7},{6,4},{7,5},{8,10},{9,11},{10,... | collective-permute-start | bytes 1572872 | tf_op jit(solution)/shard_map/ppermute | solution.py:241
  40.0 1.8 %collective-permute-start.10 = (bf16[2,384,256]{2,1,0:T(8,128)(2,1)S(1)}, bf16[2,384,256]{2,1,0:T(8,128)(2,1)S(1)}, u32[]{:S(2)}, u32[]{:S(2)}) collective-permute-start(bf16[2,384,256]{2,1,0:T(8,128)(2,1)S(1)} %get-tuple-element.21.refs_0_), channel_id=1, source_target_pairs={{0,1},{1,0},{2,3},{3,2},{4,5},{5,4},{6,7},{7,6},{8,9},{9,8},{10,11... | collective-permute-start | bytes 1179656 | tf_op jit(solution)/shard_map/ppermute | solution.py:244
  40.1 2.3 %collective-permute-start.11 = (bf16[2,384,256]{2,1,0:T(8,128)(2,1)S(1)}, bf16[2,384,256]{2,1,0:T(8,128)(2,1)S(1)}, u32[]{:S(2)}, u32[]{:S(2)}) collective-permute-start(bf16[2,384,256]{2,1,0:T(8,128)(2,1)S(1)} %get-tuple-element.22.refs_1_), channel_id=1, source_target_pairs={{0,1},{1,0},{2,3},{3,2},{4,5},{5,4},{6,7},{7,6},{8,9},{9,8},{10,11... | collective-permute-start | bytes 1179656 | tf_op jit(solution)/shard_map/ppermute | solution.py:244
  43.1 6.5 %copy-start.3 = (s32[6]{0:T(128)S(1)}, s32[6]{0:T(128)}, u32[]{:S(2)}) copy-start(s32[6]{0:T(128)} %param.8) | copy-start | bytes 76
  43.1 10.9 %copy-start.1 = (bf16[256,2048]{1,0:T(8,128)(2,1)S(1)}, bf16[256,2048]{1,0:T(8,128)(2,1)}, u32[]{:S(2)}) copy-start(bf16[256,2048]{1,0:T(8,128)(2,1)} %q_ref.1) | copy-start | bytes 3145732
  46.1 6.6 %collective-permute-start.12 = (bf16[128,512]{1,0:T(8,128)(2,1)S(1)}, bf16[128,512]{1,0:T(8,128)(2,1)S(1)}, u32[]{:S(2)}, u32[]{:S(2)}) collective-permute-start(bf16[128,512]{1,0:T(8,128)(2,1)S(1)} %get-tuple-element.24), channel_id=1, source_target_pairs={{0,24},{1,25},{2,26},{3,27},{4,28},{5,29},{6,30},{7,31},{8,16},{9,... | collective-permute-start | bytes 393224 | tf_op jit(solution)/shard_map/ppermute | solution.py:241
  47.8 6.1 %collective-permute-start.13 = (bf16[128,512]{1,0:T(8,128)(2,1)S(1)}, bf16[128,512]{1,0:T(8,128)(2,1)S(1)}, u32[]{:S(2)}, u32[]{:S(2)}) collective-permute-start(bf16[128,512]{1,0:T(8,128)(2,1)S(1)} %get-tuple-element.25), channel_id=1, source_target_pairs={{0,8},{1,9},{2,10},{3,11},{4,12},{5,13},{6,14},{7,15},{8,0},{9,1},... | collective-permute-start | bytes 393224 | tf_op jit(solution)/shard_map/ppermute | solution.py:241
  48.4 5.6 %collective-permute-start.14 = (bf16[128,512]{1,0:T(8,128)(2,1)S(1)}, bf16[128,512]{1,0:T(8,128)(2,1)S(1)}, u32[]{:S(2)}, u32[]{:S(2)}) collective-permute-start(bf16[128,512]{1,0:T(8,128)(2,1)S(1)} %get-tuple-element.26), channel_id=1, source_target_pairs={{0,16},{1,17},{2,18},{3,19},{4,20},{5,21},{6,22},{7,23},{8,24},{9,... | collective-permute-start | bytes 393224 | tf_op jit(solution)/shard_map/ppermute | solution.py:241

commit v6 on v5

--- a/solution.py
+++ b/solution.py
@@ -19,6 +19,7 @@
 HBM = pl.BlockSpec(memory_space=pltpu.HBM)
 LIMIT = 16 * 1024 * 1024
 COST = 10
+EARLY = 10
 
 
 def attend_any(kv, tiles, queries, group):
@@ -86,6 +87,11 @@
     rows = kept.shape[0]
     out[:rows, :] = kept[...]
     out[rows:, :] = other[...]
+
+
+def join_later(kept, other, after, out):
+    del after
+    join(kept, other, out)
 
 
 def row_squares(x, after, squares):
@@ -247,12 +253,14 @@
     kept = lax.dynamic_slice_in_dim(w, t * half, half, axis=1)
     given = lax.dynamic_slice_in_dim(w, (1 - t) * half, half, axis=1)
     shape = (2 * quarter, half)
-    own = call(join, [(shape, bf16)], kept, swap(given), cost=1)[0]
+    other = swap(given)
+    own = call(join, [(shape, bf16)], kept, other, cost=1)[0]
 
     def swap_planes(x, k):
         return send(x, [((c, z), (c, z ^ k)) for c in range(4) for z in planes])
 
-    near, far = swap_planes(own, 1), swap_planes(own, 2)
+    near, far, other_far = swap_planes(own, 1), swap_planes(kept, 2), swap_planes(other, 2)
+    far = call(later, [(kept.shape, bf16)], far, kept, specs=[VMEM, ANY], cost=EARLY)[0]
 
     squares = call(row_squares, [((n_rows, 128), f32)], image_rows, own, specs=[VMEM, ANY])[0]
     whole, part = ((4, n_rows, quarter), bf16), ((2, n_rows, quarter), bf16)
@@ -265,11 +273,13 @@
         enc_gain.reshape(1, -1),
     )
     to_b, to_c, to_d = ([((0, z), (h, z)) for z in planes] for h in (1, 2, 3))
-    d_low, d_high = send(d_low, to_d), send(d_high, to_c)
-    c = call(later, [whole], c, d_low, specs=[VMEM, ANY], cost=0)[0]
-    b, c = send(b, to_b), send(c, to_c)
-    last = call(later, [(shape, bf16)], far, near, specs=[VMEM, ANY], cost=COST)[0]
-    last = swap_planes(last, 1)
+    d_high, b = send(d_high, to_c), send(b, to_b)
+    c = call(later, [whole], c, far, specs=[VMEM, ANY], cost=0)[0]
+    d_low = call(later, [part], d_low, b, specs=[VMEM, ANY], cost=0)[0]
+    c, d_low = send(c, to_c), send(d_low, to_d)
+    specs = [VMEM, VMEM, ANY]
+    far = call(join_later, [(shape, bf16)], far, other_far, near, specs=specs, cost=COST)[0]
+    last = swap_planes(far, 1)
     d_high = send(d_high, [((2, z), (3, z)) for z in planes])
     rows = call(landed, [part] * 2, a, b, c, d_low, d_high)
     rows = (*rows, *[swap(x) for x in rows])

time: 55.4 us -> 54.7 us (0.987)
  waiting for transfers between devices: 29.9 us -> 26.9 us
  starting transfers between devices: 18.9 us -> 21.3 us
    ppermute x11 -> x12, starting transfers between devices: 17.3 us -> 20 us  [send(): lax.ppermute(x, AXES, [(index(a, c), index(b, c)) for a, b in pairs for c...]
    ppermute x11 -> x12, waiting for transfers between devices: 27 us -> 25.1 us  [send(): lax.ppermute(x, AXES, [(index(a, c), index(b, c)) for a, b in pairs for c...]
    ppermute x4, waiting for transfers between devices: 2.94 us -> 1.78 us  [swap(): return lax.ppermute(x, 'tp', [(0, 1), (1, 0)])]
    pallas_call x9 -> x11, Pallas kernels: 4.4 us -> 4.44 us  [call(): pl.pallas_call(body, out_shape=outs, in_specs=specs or [VMEM] * len(args)...]
  transfers between devices with their start and end apart: 15 -> 16, of which waited for: 12 -> 10; matrix products, arithmetic and copies ran while one was open for 0% -> 0% of each run, Pallas kernels for 4% -> 5%
where the time goes in v6:
time: 54.7 us; the launch traced here: 54.4 us
  waiting for transfers between devices  26.9 us (49%)
  starting transfers between devices  21.3 us (39%)
  Pallas kernels  4.44 us (8%)
  local copies, waits for them, and re-layouts  1.46 us (3%)
    ppermute x12, waiting for transfers between devices, send(): lax.ppermute(x, AXES, [(index(a, c), index(b, c)) for a, b in pairs for c...  25.1 us
    ppermute x12, starting transfers between devices, send(): lax.ppermute(x, AXES, [(index(a, c), index(b, c)) for a, b in pairs for c...  20 us
    pallas_call x11, Pallas kernels, call(): pl.pallas_call(body, out_shape=outs, in_specs=specs or [VMEM] * len(args)...  4.44 us
    ppermute x4, waiting for transfers between devices, swap(): return lax.ppermute(x, 'tp', [(0, 1), (1, 0)])  1.78 us
    dynamic_slice x1, local copies, waits for them, and re-layouts, shards_line(): given = lax.dynamic_slice_in_dim(w, (1 - t) * half, half, axis=1)  1.35 us
    ppermute x4, starting transfers between devices, swap(): return lax.ppermute(x, 'tp', [(0, 1), (1, 0)])  1.31 us
  transfers between devices with their start and end apart: 16, of which 10 were waited for; matrix products, arithmetic and copies ran while one was open for 0% of the time, Pallas kernels for 5%

profile of v6, /device:TPU:0, one launch (start us, length us, event | category | flops | bytes accessed | tf_op | source)
XLA Modules:
  0.0 54.4 jit_solution(14297751619093871086)
XLA Ops:
  0.0 1.4 %fusion = (bf16[256,512]{1,0:T(8,128)(2,1)S(1)}, bf16[256,512]{1,0:T(8,128)(2,1)S(1)}) fusion(bf16[1024,1024]{1,0:T(8,128)(2,1)} %param.7, s32[]{:T(128)S(6)} %select_n.20, s32[]{:T(128)S(6)} %select_n.24, s32[]{:T(128)S(6)} %select_n.22), kind=kLoop, calls=%fused_computation.1 | loop fusion | bytes 1048588 | tf_op jit(solution)/shard_map/dynamic_slice | solution.py:254
  1.4 0.0 copy-start
  1.4 0.5 collective-permute-start.1
  1.9 3.7 %collective-permute-start = (bf16[256,512]{1,0:T(8,128)(2,1)S(1)}, bf16[256,512]{1,0:T(8,128)(2,1)S(1)}, u32[]{:S(2)}, u32[]{:S(2)}) collective-permute-start(bf16[256,512]{1,0:T(8,128)(2,1)S(1)} %get-tuple-element.28.rest_0_.kept), channel_id=1, source_target_pairs={{0,4},{1,5},{2,6},{3,7},{4,0},{5,1},{6,2},{7,3},{8,12},{9,13},{10,... | collective-permute-start | bytes 786440 | tf_op jit(solution)/shard_map/ppermute | solution.py:247
  5.5 0.0 collective-permute-done.1.other
  5.6 0.0 copy-done
  5.6 0.0 copy-start.2
  5.6 0.6 %shard_map.58.squares = f32[384,128]{1,0:T(8,128)S(1)} custom-call(bf16[384,4096]{1,0:T(8,128)(2,1)S(1)} %copy-done, bf16[512,512]{1,0:T(8,128)(2,1)S(1)} %shard_map.56.after.own), custom_call_target="tpu_custom_call" | custom-call | tf_op jit(solution)/shard_map/pallas_call | solution.py:75
  6.2 0.2 collective-permute-start.5
  6.5 0.0 copy-done.2
  6.5 1.6 %collective-permute-start.3 = (bf16[512,512]{1,0:T(8,128)(2,1)S(1)}, bf16[512,512]{1,0:T(8,128)(2,1)S(1)}, u32[]{:S(2)}, u32[]{:S(2)}) collective-permute-start(bf16[512,512]{1,0:T(8,128)(2,1)S(1)} %shard_map.56.after.own), channel_id=1, source_target_pairs={{0,2},{1,3},{2,0},{3,1},{4,6},{5,7},{6,4},{7,5},{8,10},{9,11},{10,... | collective-permute-start | bytes 1572872 | tf_op jit(solution)/shard_map/ppermute | solution.py:247
  8.1 1.5 %collective-permute-start.2 = (bf16[256,512]{1,0:T(8,128)(2,1)S(1)}, bf16[256,512]{1,0:T(8,128)(2,1)S(1)}, u32[]{:S(2)}, u32[]{:S(2)}) collective-permute-start(bf16[256,512]{1,0:T(8,128)(2,1)S(1)} %collective-permute-done.1.other), channel_id=1, source_target_pairs={{0,4},{1,5},{2,6},{3,7},{4,0},{5,1},{6,2},{7,3},{8,12},{9,13},{10,... | collective-permute-start | bytes 786440 | tf_op jit(solution)/shard_map/ppermute | solution.py:247
  9.6 0.0 collective-permute-done.5.other
  9.7 1.3 %shard_map.59 = (bf16[4,384,256]{2,1,0:T(8,128)(2,1)S(1)}, bf16[4,384,256]{2,1,0:T(8,128)(2,1)S(1)}, bf16[4,384,256]{2,1,0:T(8,128)(2,1)S(1)}, bf16[2,384,256]{2,1,0:T(8,128)(2,1)S(1)}, bf16[2,384,256]{2,1,0:T(8,128)(2,1)S(1)}) custom-call(bf16[384,4096]{1,0:T(8,128)(2,1)S(1)} %copy-done, f32[384,128]{1,0:T(8,128)S(1)} %shard_map.58.squares, ...), custom_call_target="tpu_custom_call" | custom-call | tf_op jit(solution)/shard_map/pallas_call | solution.py:75
  11.0 2.1 %collective-permute-start.6 = (bf16[4,384,256]{2,1,0:T(8,128)(2,1)S(1)}, bf16[4,384,256]{2,1,0:T(8,128)(2,1)S(1)}, u32[]{:S(2)}, u32[]{:S(2)}) collective-permute-start(bf16[4,384,256]{2,1,0:T(8,128)(2,1)S(1)} %get-tuple-element.17), channel_id=1, source_target_pairs={{0,8},{1,9},{2,10},{3,11},{4,12},{5,13},{6,14},{7,15}} | collective-permute-start | bytes 2359304 | tf_op jit(solution)/shard_map/ppermute | solution.py:247
  13.1 1.3 %collective-permute-start.9 = (bf16[2,384,256]{2,1,0:T(8,128)(2,1)S(1)}, bf16[2,384,256]{2,1,0:T(8,128)(2,1)S(1)}, u32[]{:S(2)}, u32[]{:S(2)}) collective-permute-start(bf16[2,384,256]{2,1,0:T(8,128)(2,1)S(1)} %get-tuple-element.20), channel_id=1, source_target_pairs={{0,16},{1,17},{2,18},{3,19},{4,20},{5,21},{6,22},{7,23}} | collective-permute-start | bytes 1179656 | tf_op jit(solution)/shard_map/ppermute | solution.py:247
  14.4 4.0 %collective-permute-done.x = bf16[256,512]{1,0:T(8,128)(2,1)S(1)} collective-permute-done((bf16[256,512]{1,0:T(8,128)(2,1)S(1)}, bf16[256,512]{1,0:T(8,128)(2,1)S(1)}, u32[]{:S(2)}, u32[]{:S(2)}) %collective-permute-start) | collective-permute-done | bytes 262176 | tf_op jit(solution)/shard_map/ppermute | solution.py:247
  18.4 0.1 shard_map.60
  18.5 3.7 %collective-permute-start.7 = (bf16[4,384,256]{2,1,0:T(8,128)(2,1)S(1)}, bf16[4,384,256]{2,1,0:T(8,128)(2,1)S(1)}, u32[]{:S(2)}, u32[]{:S(2)}) collective-permute-start(bf16[4,384,256]{2,1,0:T(8,128)(2,1)S(1)} %shard_map.60), channel_id=1, source_target_pairs={{0,16},{1,17},{2,18},{3,19},{4,20},{5,21},{6,22},{7,23}} | collective-permute-start | bytes 2359304 | tf_op jit(solution)/shard_map/ppermute | solution.py:247
  22.2 0.9 %collective-permute-done.9 = bf16[2,384,256]{2,1,0:T(8,128)(2,1)S(1)} collective-permute-done((bf16[2,384,256]{2,1,0:T(8,128)(2,1)S(1)}, bf16[2,384,256]{2,1,0:T(8,128)(2,1)S(1)}, u32[]{:S(2)}, u32[]{:S(2)}) %collective-permute-start.9) | collective-permute-done | bytes 393248 | tf_op jit(solution)/shard_map/ppermute | solution.py:247
  23.2 0.7 %collective-permute-start.10 = (bf16[2,384,256]{2,1,0:T(8,128)(2,1)S(1)}, bf16[2,384,256]{2,1,0:T(8,128)(2,1)S(1)}, u32[]{:S(2)}, u32[]{:S(2)}) collective-permute-start(bf16[2,384,256]{2,1,0:T(8,128)(2,1)S(1)} %collective-permute-done.9), channel_id=1, source_target_pairs={{16,24},{17,25},{18,26},{19,27},{20,28},{21,29},{22,30},{23,31}} | collective-permute-start | bytes 1179656 | tf_op jit(solution)/shard_map/ppermute | solution.py:247
  23.9 5.6 %collective-permute-done.6.rest_0_.b = bf16[4,384,256]{2,1,0:T(8,128)(2,1)S(1)} collective-permute-done((bf16[4,384,256]{2,1,0:T(8,128)(2,1)S(1)}, bf16[4,384,256]{2,1,0:T(8,128)(2,1)S(1)}, u32[]{:S(2)}, u32[]{:S(2)}) %collective-permute-start.6) | collective-permute-done | bytes 786464 | tf_op jit(solution)/shard_map/ppermute | solution.py:247
  29.5 1.3 %collective-permute-start.8 = (bf16[2,384,256]{2,1,0:T(8,128)(2,1)S(1)}, bf16[2,384,256]{2,1,0:T(8,128)(2,1)S(1)}, u32[]{:S(2)}, u32[]{:S(2)}) collective-permute-start(bf16[2,384,256]{2,1,0:T(8,128)(2,1)S(1)} %shard_map.61), channel_id=1, source_target_pairs={{0,24},{1,25},{2,26},{3,27},{4,28},{5,29},{6,30},{7,31}} | collective-permute-start | bytes 1179656 | tf_op jit(solution)/shard_map/ppermute | solution.py:247
  30.8 0.0 collective-permute-done.2.other
  30.8 0.0 collective-permute-done.3.after.near
  30.8 0.5 collective-permute-start.4
  31.4 7.8 %collective-permute-done.7.c = bf16[4,384,256]{2,1,0:T(8,128)(2,1)S(1)} collective-permute-done((bf16[4,384,256]{2,1,0:T(8,128)(2,1)S(1)}, bf16[4,384,256]{2,1,0:T(8,128)(2,1)S(1)}, u32[]{:S(2)}, u32[]{:S(2)}) %collective-permute-start.7) | collective-permute-done | bytes 786464 | tf_op jit(solution)/shard_map/ppermute | solution.py:247
  39.2 0.0 collective-permute-done.10.d_high
  39.2 0.0 collective-permute-done.8.d_low
  39.2 0.1 shard_map.62
  39.3 0.1 collective-permute-start.11
  39.4 0.5 collective-permute-start.12
  39.9 1.2 %collective-permute-done.11.refs_2_ = bf16[2,384,256]{2,1,0:T(8,128)(2,1)S(1)} collective-permute-done((bf16[2,384,256]{2,1,0:T(8,128)(2,1)S(1)}, bf16[2,384,256]{2,1,0:T(8,128)(2,1)S(1)}, u32[]{:S(2)}, u32[]{:S(2)}) %collective-permute-start.11) | collective-permute-done | bytes 393248 | tf_op jit(solution)/shard_map/ppermute | solution.py:250
  41.1 0.6 %collective-permute-done.12.refs_3_ = bf16[2,384,256]{2,1,0:T(8,128)(2,1)S(1)} collective-permute-done((bf16[2,384,256]{2,1,0:T(8,128)(2,1)S(1)}, bf16[2,384,256]{2,1,0:T(8,128)(2,1)S(1)}, u32[]{:S(2)}, u32[]{:S(2)}) %collective-permute-start.12) | collective-permute-done | bytes 393248 | tf_op jit(solution)/shard_map/ppermute | solution.py:250
  41.6 0.8 %shard_map.63.refs_4_ = f32[384,512]{1,0:T(8,128)S(1)} custom-call(bf16[512,512]{1,0:T(8,128)(2,1)S(1)} %shard_map.56.after.own, bf16[512,512]{1,0:T(8,128)(2,1)S(1)} %collective-permute-done.3.after.near, bf16[512,512]{1,0:T(8,128)(2,1)S(1)} %shard_map.57.far, bf16[2,384,256]{2,1,0:T(8,128)(2,1)S(1)} %get-tuple-element.21.refs_0_, ...), custom_call_target="tpu_custom_call" | custom-call | tf_op jit(solution)/shard_map/pallas_call | solution.py:75
  42.4 0.0 copy-start.3
  42.4 0.0 copy-start.1
  42.4 1.8 %collective-permute-done.4.last = bf16[512,512]{1,0:T(8,128)(2,1)S(1)} collective-permute-done((bf16[512,512]{1,0:T(8,128)(2,1)S(1)}, bf16[512,512]{1,0:T(8,128)(2,1)S(1)}, u32[]{:S(2)}, u32[]{:S(2)}) %collective-permute-start.4) | collective-permute-done | bytes 524320 | tf_op jit(solution)/shard_map/ppermute | solution.py:247
  44.3 0.4 shard_map.64
  44.7 2.0 %collective-permute-start.13 = (bf16[128,512]{1,0:T(8,128)(2,1)S(1)}, bf16[128,512]{1,0:T(8,128)(2,1)S(1)}, u32[]{:S(2)}, u32[]{:S(2)}) collective-permute-start(bf16[128,512]{1,0:T(8,128)(2,1)S(1)} %get-tuple-element.24), channel_id=1, source_target_pairs={{0,24},{1,25},{2,26},{3,27},{4,28},{5,29},{6,30},{7,31},{8,16},{9,... | collective-permute-start | bytes 393224 | tf_op jit(solution)/shard_map/ppermute | solution.py:247
  46.7 0.5 collective-permute-start.14
  47.3 1.0 %collective-permute-start.15 = (bf16[128,512]{1,0:T(8,128)(2,1)S(1)}, bf16[128,512]{1,0:T(8,128)(2,1)S(1)}, u32[]{:S(2)}, u32[]{:S(2)}) collective-permute-start(bf16[128,512]{1,0:T(8,128)(2,1)S(1)} %get-tuple-element.26), channel_id=1, source_target_pairs={{0,16},{1,17},{2,18},{3,19},{4,20},{5,21},{6,22},{7,23},{8,24},{9,... | collective-permute-start | bytes 393224 | tf_op jit(solution)/shard_map/ppermute | solution.py:247
  48.3 0.0 copy-done.3
  48.3 0.1 dynamic-slice_multiply_fusion
  48.3 2.8 %collective-permute-done.13.one = bf16[128,512]{1,0:T(8,128)(2,1)S(1)} collective-permute-done((bf16[128,512]{1,0:T(8,128)(2,1)S(1)}, bf16[128,512]{1,0:T(8,128)(2,1)S(1)}, u32[]{:S(2)}, u32[]{:S(2)}) %collective-permute-start.13) | collective-permute-done | bytes 131104 | tf_op jit(solution)/shard_map/ppermute | solution.py:247
  51.2 2.0 %collective-permute-done.14.two = bf16[128,512]{1,0:T(8,128)(2,1)S(1)} collective-permute-done((bf16[128,512]{1,0:T(8,128)(2,1)S(1)}, bf16[128,512]{1,0:T(8,128)(2,1)S(1)}, u32[]{:S(2)}, u32[]{:S(2)}) %collective-permute-start.14) | collective-permute-done | bytes 131104 | tf_op jit(solution)/shard_map/ppermute | solution.py:247
  53.2 0.1 collective-permute-done.15.three
  53.3 0.1 broadcast_in_dim.2.counts
  53.4 0.0 copy-done.1
  53.4 1.1 %shard_map.65 = bf16[256,2048]{1,0:T(8,128)(2,1)} custom-call(s32[2,128]{1,0:T(2,128)S(1)} %broadcast_in_dim.2.counts, f32[128,512]{1,0:T(8,128)S(1)} %get-tuple-element.23.mine, bf16[128,512]{1,0:T(8,128)(2,1)S(1)} %collective-permute-done.13.one, bf16[128,512]{1,0:T(8,128)(2,1)S(1)} %collective-permute-done.14.two, ...), custom_call_target="tpu_custom_call" | custom-call | tf_op jit(solution)/shard_map/pallas_call | solution.py:75
  (5 shorter events, 0.1 us)
Async XLA Ops:
  1.4 4.2 %copy-start = (bf16[384,4096]{1,0:T(8,128)(2,1)S(1)}, bf16[384,4096]{1,0:T(8,128)(2,1)}, u32[]{:S(2)}) copy-start(bf16[384,4096]{1,0:T(8,128)(2,1)} %x.3) | copy-start | bytes 9437188
  1.4 4.2 %collective-permute-start.1 = (bf16[256,512]{1,0:T(8,128)(2,1)S(1)}, bf16[256,512]{1,0:T(8,128)(2,1)S(1)}, u32[]{:S(2)}, u32[]{:S(2)}) collective-permute-start(bf16[256,512]{1,0:T(8,128)(2,1)S(1)} %get-tuple-element.27), channel_id=1, source_target_pairs={{0,1},{1,0},{2,3},{3,2},{4,5},{5,4},{6,7},{7,6},{8,9},{9,8},{10,11... | collective-permute-start | bytes 786440 | tf_op jit(solution)/shard_map/ppermute | solution.py:250
  1.9 16.5 %collective-permute-start = (bf16[256,512]{1,0:T(8,128)(2,1)S(1)}, bf16[256,512]{1,0:T(8,128)(2,1)S(1)}, u32[]{:S(2)}, u32[]{:S(2)}) collective-permute-start(bf16[256,512]{1,0:T(8,128)(2,1)S(1)} %get-tuple-element.28.rest_0_.kept), channel_id=1, source_target_pairs={{0,4},{1,5},{2,6},{3,7},{4,0},{5,1},{6,2},{7,3},{8,12},{9,13},{10,... | collective-permute-start | bytes 786440 | tf_op jit(solution)/shard_map/ppermute | solution.py:247
  5.6 0.9 %copy-start.2 = (bf16[4096]{0:T(1024)(128)(2,1)S(1)}, bf16[4096]{0:T(1024)(128)(2,1)}, u32[]{:S(2)}) copy-start(bf16[4096]{0:T(1024)(128)(2,1)} %param.6) | copy-start | bytes 24580
  6.2 3.4 %collective-permute-start.5 = (f32[384,128]{1,0:T(8,128)S(1)}, f32[384,128]{1,0:T(8,128)S(1)}, u32[]{:S(2)}, u32[]{:S(2)}) collective-permute-start(f32[384,128]{1,0:T(8,128)S(1)} %shard_map.58.squares), channel_id=1, source_target_pairs={{0,1},{1,0},{2,3},{3,2},{4,5},{5,4},{6,7},{7,6},{8,9},{9,8},{10,11... | collective-permute-start | bytes 589832 | tf_op jit(solution)/shard_map/ppermute | solution.py:250
  6.5 24.3 %collective-permute-start.3 = (bf16[512,512]{1,0:T(8,128)(2,1)S(1)}, bf16[512,512]{1,0:T(8,128)(2,1)S(1)}, u32[]{:S(2)}, u32[]{:S(2)}) collective-permute-start(bf16[512,512]{1,0:T(8,128)(2,1)S(1)} %shard_map.56.after.own), channel_id=1, source_target_pairs={{0,2},{1,3},{2,0},{3,1},{4,6},{5,7},{6,4},{7,5},{8,10},{9,11},{10,... | collective-permute-start | bytes 1572872 | tf_op jit(solution)/shard_map/ppermute | solution.py:247
  8.1 22.6 %collective-permute-start.2 = (bf16[256,512]{1,0:T(8,128)(2,1)S(1)}, bf16[256,512]{1,0:T(8,128)(2,1)S(1)}, u32[]{:S(2)}, u32[]{:S(2)}) collective-permute-start(bf16[256,512]{1,0:T(8,128)(2,1)S(1)} %collective-permute-done.1.other), channel_id=1, source_target_pairs={{0,4},{1,5},{2,6},{3,7},{4,0},{5,1},{6,2},{7,3},{8,12},{9,13},{10,... | collective-permute-start | bytes 786440 | tf_op jit(solution)/shard_map/ppermute | solution.py:247
  11.0 18.5 %collective-permute-start.6 = (bf16[4,384,256]{2,1,0:T(8,128)(2,1)S(1)}, bf16[4,384,256]{2,1,0:T(8,128)(2,1)S(1)}, u32[]{:S(2)}, u32[]{:S(2)}) collective-permute-start(bf16[4,384,256]{2,1,0:T(8,128)(2,1)S(1)} %get-tuple-element.17), channel_id=1, source_target_pairs={{0,8},{1,9},{2,10},{3,11},{4,12},{5,13},{6,14},{7,15}} | collective-permute-start | bytes 2359304 | tf_op jit(solution)/shard_map/ppermute | solution.py:247
  13.1 10.1 %collective-permute-start.9 = (bf16[2,384,256]{2,1,0:T(8,128)(2,1)S(1)}, bf16[2,384,256]{2,1,0:T(8,128)(2,1)S(1)}, u32[]{:S(2)}, u32[]{:S(2)}) collective-permute-start(bf16[2,384,256]{2,1,0:T(8,128)(2,1)S(1)} %get-tuple-element.20), channel_id=1, source_target_pairs={{0,16},{1,17},{2,18},{3,19},{4,20},{5,21},{6,22},{7,23}} | collective-permute-start | bytes 1179656 | tf_op jit(solution)/shard_map/ppermute | solution.py:247
  18.5 20.7 %collective-permute-start.7 = (bf16[4,384,256]{2,1,0:T(8,128)(2,1)S(1)}, bf16[4,384,256]{2,1,0:T(8,128)(2,1)S(1)}, u32[]{:S(2)}, u32[]{:S(2)}) collective-permute-start(bf16[4,384,256]{2,1,0:T(8,128)(2,1)S(1)} %shard_map.60), channel_id=1, source_target_pairs={{0,16},{1,17},{2,18},{3,19},{4,20},{5,21},{6,22},{7,23}} | collective-permute-start | bytes 2359304 | tf_op jit(solution)/shard_map/ppermute | solution.py:247
  23.2 16.0 %collective-permute-start.10 = (bf16[2,384,256]{2,1,0:T(8,128)(2,1)S(1)}, bf16[2,384,256]{2,1,0:T(8,128)(2,1)S(1)}, u32[]{:S(2)}, u32[]{:S(2)}) collective-permute-start(bf16[2,384,256]{2,1,0:T(8,128)(2,1)S(1)} %collective-permute-done.9), channel_id=1, source_target_pairs={{16,24},{17,25},{18,26},{19,27},{20,28},{21,29},{22,30},{23,31}} | collective-permute-start | bytes 1179656 | tf_op jit(solution)/shard_map/ppermute | solution.py:247
  29.5 9.8 %collective-permute-start.8 = (bf16[2,384,256]{2,1,0:T(8,128)(2,1)S(1)}, bf16[2,384,256]{2,1,0:T(8,128)(2,1)S(1)}, u32[]{:S(2)}, u32[]{:S(2)}) collective-permute-start(bf16[2,384,256]{2,1,0:T(8,128)(2,1)S(1)} %shard_map.61), channel_id=1, source_target_pairs={{0,24},{1,25},{2,26},{3,27},{4,28},{5,29},{6,30},{7,31}} | collective-permute-start | bytes 1179656 | tf_op jit(solution)/shard_map/ppermute | solution.py:247
  30.8 13.4 %collective-permute-start.4 = (bf16[512,512]{1,0:T(8,128)(2,1)S(1)}, bf16[512,512]{1,0:T(8,128)(2,1)S(1)}, u32[]{:S(2)}, u32[]{:S(2)}) collective-permute-start(bf16[512,512]{1,0:T(8,128)(2,1)S(1)} %shard_map.57.far), channel_id=1, source_target_pairs={{0,2},{1,3},{2,0},{3,1},{4,6},{5,7},{6,4},{7,5},{8,10},{9,11},{10,... | collective-permute-start | bytes 1572872 | tf_op jit(solution)/shard_map/ppermute | solution.py:247
  39.3 1.8 %collective-permute-start.11 = (bf16[2,384,256]{2,1,0:T(8,128)(2,1)S(1)}, bf16[2,384,256]{2,1,0:T(8,128)(2,1)S(1)}, u32[]{:S(2)}, u32[]{:S(2)}) collective-permute-start(bf16[2,384,256]{2,1,0:T(8,128)(2,1)S(1)} %get-tuple-element.21.refs_0_), channel_id=1, source_target_pairs={{0,1},{1,0},{2,3},{3,2},{4,5},{5,4},{6,7},{7,6},{8,9},{9,8},{10,11... | collective-permute-start | bytes 1179656 | tf_op jit(solution)/shard_map/ppermute | solution.py:250
  39.4 2.3 %collective-permute-start.12 = (bf16[2,384,256]{2,1,0:T(8,128)(2,1)S(1)}, bf16[2,384,256]{2,1,0:T(8,128)(2,1)S(1)}, u32[]{:S(2)}, u32[]{:S(2)}) collective-permute-start(bf16[2,384,256]{2,1,0:T(8,128)(2,1)S(1)} %get-tuple-element.22.refs_1_), channel_id=1, source_target_pairs={{0,1},{1,0},{2,3},{3,2},{4,5},{5,4},{6,7},{7,6},{8,9},{9,8},{10,11... | collective-permute-start | bytes 1179656 | tf_op jit(solution)/shard_map/ppermute | solution.py:250
  42.4 5.8 %copy-start.3 = (s32[6]{0:T(128)S(1)}, s32[6]{0:T(128)}, u32[]{:S(2)}) copy-start(s32[6]{0:T(128)} %param.8) | copy-start | bytes 76
  42.4 10.9 %copy-start.1 = (bf16[256,2048]{1,0:T(8,128)(2,1)S(1)}, bf16[256,2048]{1,0:T(8,128)(2,1)}, u32[]{:S(2)}) copy-start(bf16[256,2048]{1,0:T(8,128)(2,1)} %q_ref.1) | copy-start | bytes 3145732
  44.7 6.5 %collective-permute-start.13 = (bf16[128,512]{1,0:T(8,128)(2,1)S(1)}, bf16[128,512]{1,0:T(8,128)(2,1)S(1)}, u32[]{:S(2)}, u32[]{:S(2)}) collective-permute-start(bf16[128,512]{1,0:T(8,128)(2,1)S(1)} %get-tuple-element.24), channel_id=1, source_target_pairs={{0,24},{1,25},{2,26},{3,27},{4,28},{5,29},{6,30},{7,31},{8,16},{9,... | collective-permute-start | bytes 393224 | tf_op jit(solution)/shard_map/ppermute | solution.py:247
  46.7 6.5 %collective-permute-start.14 = (bf16[128,512]{1,0:T(8,128)(2,1)S(1)}, bf16[128,512]{1,0:T(8,128)(2,1)S(1)}, u32[]{:S(2)}, u32[]{:S(2)}) collective-permute-start(bf16[128,512]{1,0:T(8,128)(2,1)S(1)} %get-tuple-element.25), channel_id=1, source_target_pairs={{0,8},{1,9},{2,10},{3,11},{4,12},{5,13},{6,14},{7,15},{8,0},{9,1},... | collective-permute-start | bytes 393224 | tf_op jit(solution)/shard_map/ppermute | solution.py:247
  47.3 6.0 %collective-permute-start.15 = (bf16[128,512]{1,0:T(8,128)(2,1)S(1)}, bf16[128,512]{1,0:T(8,128)(2,1)S(1)}, u32[]{:S(2)}, u32[]{:S(2)}) collective-permute-start(bf16[128,512]{1,0:T(8,128)(2,1)S(1)} %get-tuple-element.26), channel_id=1, source_target_pairs={{0,16},{1,17},{2,18},{3,19},{4,20},{5,21},{6,22},{7,23},{8,24},{9,... | collective-permute-start | bytes 393224 | tf_op jit(solution)/shard_map/ppermute | solution.py:247

commit v7 on v6

--- a/solution.py
+++ b/solution.py
@@ -68,7 +68,7 @@
     return attend_any(heads.astype(jnp.bfloat16), tiles, queries, group)
 
 
-def call(body, outs, *args, specs=None, out_spec=VMEM, cost=None, scratch=()):
+def call(body, outs, *args, specs=None, out_spec=VMEM, cost=None, scratch=(), aliases=()):
     outs = [jax.ShapeDtypeStruct(s, d) for s, d in outs]
     if cost is not None:
         cost = pl.CostEstimate(flops=cost * 10**9, bytes_accessed=0, transcendentals=0)
@@ -76,9 +76,10 @@
         body,
         out_shape=outs,
         in_specs=specs or [VMEM] * len(args),
-        out_specs=[out_spec] * len(outs),
+        out_specs=out_spec if isinstance(out_spec, list) else [out_spec] * len(outs),
         cost_estimate=cost,
         scratch_shapes=list(scratch),
+        input_output_aliases=dict(aliases),
         compiler_params=pltpu.CompilerParams(vmem_limit_bytes=LIMIT),
     )(*args)
 
@@ -89,9 +90,8 @@
     out[rows:, :] = other[...]
 
 
-def join_later(kept, other, after, out):
-    del after
-    join(kept, other, out)
+def join_later(kept, other, *rest):
+    join(kept, other, rest[-1])
 
 
 def row_squares(x, after, squares):
@@ -140,7 +140,7 @@
         high[...] = d_high[...]
 
 
-def add_products(rows, blocks, total):
+def add_products(rows, blocks, cores, put):
     depth = rows[0].shape[2]
     for f in range(4):
 
@@ -149,21 +149,28 @@
             out = None
             for k, w in blocks.items():
                 z = f ^ k
-                for core in range(2):
+                for i, core in enumerate(cores):
                     y = jnp.dot(
-                        rows[2 * core + z // 2][z % 2],
+                        rows[2 * i + z // 2][z % 2],
                         w[core * depth : (core + 1) * depth, :],
                         preferred_element_type=jnp.float32,
                     )
                     out = y if out is None else out + y
-            total(out)
-
-
-def products(own, near, far, *refs):
+            put(out)
+
+
+def own_products(own, near, far, low, high, total):
     def put(x):
-        refs[4][...] = x
-
-    add_products(refs[:4], {0: own, 1: near, 2: far}, put)
+        total[...] = x
+
+    add_products((low, high), {0: own, 1: near, 2: far}, (0,), put)
+
+
+def other_products(own, near, far, low, high, before, total):
+    def put(x):
+        total[...] = before[...] + x
+
+    add_products((low, high), {0: own, 1: near, 2: far}, (1,), put)
 
 
 def last_product(last, *refs):
@@ -173,25 +180,32 @@
     def put(x):
         held[...] = total[...] + x
 
-    add_products(rows, {3: last}, put)
+    add_products(rows, {3: last}, (0, 1), put)
     for k, out in enumerate((mine, one, two, other)):
         at = pl.multiple_of(jnp.maximum((g ^ k) - 1, 0) * n, n)
         out[...] = held[pl.ds(at, n), :].astype(out.dtype)
 
 
-def attention(counts, mine, one, two, three, q_ref, out_ref, held, sems):
+def blank(after, out, token, held, sem):
+    del after
+    token[...] = jnp.zeros_like(token)
+
+    @pl.when(lax.axis_index("grp") == 0)
+    def _():
+        held[...] = jnp.zeros_like(held)
+        copy = pltpu.make_async_copy(held, out, sem)
+        copy.start()
+        copy.wait()
+
+
+def attention(counts, mine, one, two, three, q_ref, blank_ref, out_ref, held, sems):
+    del blank_ref
     g = lax.axis_index("grp")
     groups_q = QH // KVH
     copies = [
         pltpu.make_async_copy(held.at[at, :], out_ref.at[at, :], sems.at[s])
         for s, at in enumerate(pl.ds(s * TXT_S, TXT_S) for s in range(SAMP))
     ]
-
-    @pl.when(g == 0)
-    def _():
-        held[...] = jnp.zeros_like(held)
-        for copy in copies:
-            copy.start()
 
     @pl.when(g > 0)
     def _():
@@ -228,9 +242,8 @@
                 for j, h in enumerate(heads):
                     held[rows, h] = out[j * TXT_S : (j + 1) * TXT_S].astype(jnp.bfloat16)
             copy.start()
-
-    for copy in copies:
-        copy.wait()
+        for copy in copies:
+            copy.wait()
 
 
 def shards_line(image_rows, enc_gain, key_value_w, tiles, queries):
@@ -277,14 +290,25 @@
     c = call(later, [whole], c, far, specs=[VMEM, ANY], cost=0)[0]
     d_low = call(later, [part], d_low, b, specs=[VMEM, ANY], cost=0)[0]
     c, d_low = send(c, to_c), send(d_low, to_d)
-    specs = [VMEM, VMEM, ANY]
-    far = call(join_later, [(shape, bf16)], far, other_far, near, specs=specs, cost=COST)[0]
+    zeros, token = call(
+        blank,
+        [(queries.shape, bf16), ((8, 128), f32)],
+        d_high,
+        out_spec=[ANY, VMEM],
+        specs=[ANY],
+        cost=0,
+        scratch=[pltpu.VMEM(queries.shape, bf16), pltpu.SemaphoreType.DMA],
+    )
+    specs = [VMEM, VMEM, ANY, ANY]
+    far = call(join_later, [(shape, bf16)], far, other_far, near, token, specs=specs, cost=COST)[0]
     last = swap_planes(far, 1)
     d_high = send(d_high, [((2, z), (3, z)) for z in planes])
     rows = call(landed, [part] * 2, a, b, c, d_low, d_high)
-    rows = (*rows, *[swap(x) for x in rows])
-
-    total = call(products, [((n_rows, half), f32)], own, near, far, *rows)[0]
+    others = [swap(x) for x in rows]
+
+    total, blocks = [((n_rows, half), f32)], (own, near, far)
+    before = call(own_products, total, *blocks, *rows, cost=0)[0]
+    total = call(other_products, total, *blocks, *others, before, cost=0)[0]
     counts = lax.dynamic_slice_in_dim(tiles, jnp.maximum(g - 1, 0) * SAMP, SAMP) * TILE_TOK
     message = (per_group, half)
     mine, *parts = call(
@@ -292,6 +316,7 @@
         [(message, f32)] + [(message, bf16)] * 3,
         last,
         *rows,
+        *others,
         total,
         scratch=[pltpu.VMEM((n_rows, half), f32)],
     )
@@ -306,7 +331,10 @@
         mine,
         *parts,
         queries,
+        zeros,
+        specs=[VMEM] * 6 + [ANY],
         out_spec=ANY,
+        aliases={6: 0},
         scratch=[pltpu.VMEM(queries.shape, bf16), pltpu.SemaphoreType.DMA((SAMP,))],
     )[0]
 

time: 54.7 us -> 53.8 us (0.984)
  waiting for transfers between devices: 26.9 us -> 25.4 us
    ppermute x12, waiting for transfers between devices: 25.1 us -> 24.1 us  [send(): lax.ppermute(x, AXES, [(index(a, c), index(b, c)) for a, b in pairs for c...]
    pallas_call x11 -> x13, Pallas kernels: 4.44 us -> 4.64 us  [call(): pl.pallas_call(body, out_shape=outs, in_specs=specs or [VMEM] * len(args)...]
  transfers between devices with their start and end apart: 16 -> 16, of which waited for: 10 -> 10; matrix products, arithmetic and copies ran while one was open for 0% -> 0% of each run, Pallas kernels for 5% -> 8%
where the time goes in v7:
time: 53.8 us; the launch traced here: 53.1 us
  waiting for transfers between devices  25.4 us (47%)
  starting transfers between devices  21.3 us (40%)
  Pallas kernels  4.64 us (9%)
  local copies, waits for them, and re-layouts  1.46 us (3%)
    ppermute x12, waiting for transfers between devices, send(): lax.ppermute(x, AXES, [(index(a, c), index(b, c)) for a, b in pairs for c...  24.1 us
    ppermute x12, starting transfers between devices, send(): lax.ppermute(x, AXES, [(index(a, c), index(b, c)) for a, b in pairs for c...  20 us
    pallas_call x13, Pallas kernels, call(): pl.pallas_call(body, out_shape=outs, in_specs=specs or [VMEM] * len(args)...  4.64 us
    dynamic_slice x1, local copies, waits for them, and re-layouts, shards_line(): given = lax.dynamic_slice_in_dim(w, (1 - t) * half, half, axis=1)  1.35 us
    ppermute x4, starting transfers between devices, swap(): return lax.ppermute(x, 'tp', [(0, 1), (1, 0)])  1.31 us
    ppermute x4, waiting for transfers between devices, swap(): return lax.ppermute(x, 'tp', [(0, 1), (1, 0)])  1.3 us
  transfers between devices with their start and end apart: 16, of which 10 were waited for; matrix products, arithmetic and copies ran while one was open for 0% of the time, Pallas kernels for 8%

profile of v7, /device:TPU:0, one launch (start us, length us, event | category | flops | bytes accessed | tf_op | source)
XLA Modules:
  0.0 53.1 jit_solution(13036566057665571766)
XLA Ops:
  0.0 1.4 %fusion = (bf16[256,512]{1,0:T(8,128)(2,1)S(1)}, bf16[256,512]{1,0:T(8,128)(2,1)S(1)}) fusion(bf16[1024,1024]{1,0:T(8,128)(2,1)} %param.7, s32[]{:T(128)S(6)} %select_n.20, s32[]{:T(128)S(6)} %select_n.24, s32[]{:T(128)S(6)} %select_n.22), kind=kLoop, calls=%fused_computation.1 | loop fusion | bytes 1048588 | tf_op jit(solution)/shard_map/dynamic_slice | solution.py:267
  1.4 0.0 copy-start
  1.4 0.5 collective-permute-start.1
  1.9 3.7 %collective-permute-start = (bf16[256,512]{1,0:T(8,128)(2,1)S(1)}, bf16[256,512]{1,0:T(8,128)(2,1)S(1)}, u32[]{:S(2)}, u32[]{:S(2)}) collective-permute-start(bf16[256,512]{1,0:T(8,128)(2,1)S(1)} %get-tuple-element.32.rest_0_.kept), channel_id=1, source_target_pairs={{0,4},{1,5},{2,6},{3,7},{4,0},{5,1},{6,2},{7,3},{8,12},{9,13},{10,... | collective-permute-start | bytes 786440 | tf_op jit(solution)/shard_map/ppermute | solution.py:260
  5.5 0.0 collective-permute-done.1.other
  5.6 0.0 copy-done
  5.6 0.0 copy-start.2
  5.6 0.6 %shard_map.57.squares = f32[384,128]{1,0:T(8,128)S(1)} custom-call(bf16[384,4096]{1,0:T(8,128)(2,1)S(1)} %copy-done, bf16[512,512]{1,0:T(8,128)(2,1)S(1)} %shard_map.56.after.own), custom_call_target="tpu_custom_call" | custom-call | tf_op jit(solution)/shard_map/pallas_call | solution.py:75
  6.2 0.2 collective-permute-start.4
  6.5 0.0 copy-done.2
  6.5 1.6 %collective-permute-start.3 = (bf16[512,512]{1,0:T(8,128)(2,1)S(1)}, bf16[512,512]{1,0:T(8,128)(2,1)S(1)}, u32[]{:S(2)}, u32[]{:S(2)}) collective-permute-start(bf16[512,512]{1,0:T(8,128)(2,1)S(1)} %shard_map.56.after.own), channel_id=1, source_target_pairs={{0,2},{1,3},{2,0},{3,1},{4,6},{5,7},{6,4},{7,5},{8,10},{9,11},{10,... | collective-permute-start | bytes 1572872 | tf_op jit(solution)/shard_map/ppermute | solution.py:260
  8.1 1.5 %collective-permute-start.2 = (bf16[256,512]{1,0:T(8,128)(2,1)S(1)}, bf16[256,512]{1,0:T(8,128)(2,1)S(1)}, u32[]{:S(2)}, u32[]{:S(2)}) collective-permute-start(bf16[256,512]{1,0:T(8,128)(2,1)S(1)} %collective-permute-done.1.other), channel_id=1, source_target_pairs={{0,4},{1,5},{2,6},{3,7},{4,0},{5,1},{6,2},{7,3},{8,12},{9,13},{10,... | collective-permute-start | bytes 786440 | tf_op jit(solution)/shard_map/ppermute | solution.py:260
  9.6 0.0 collective-permute-done.4.other
  9.7 1.3 %shard_map.58 = (bf16[4,384,256]{2,1,0:T(8,128)(2,1)S(1)}, bf16[4,384,256]{2,1,0:T(8,128)(2,1)S(1)}, bf16[4,384,256]{2,1,0:T(8,128)(2,1)S(1)}, bf16[2,384,256]{2,1,0:T(8,128)(2,1)S(1)}, bf16[2,384,256]{2,1,0:T(8,128)(2,1)S(1)}) custom-call(bf16[384,4096]{1,0:T(8,128)(2,1)S(1)} %copy-done, f32[384,128]{1,0:T(8,128)S(1)} %shard_map.57.squares, ...), custom_call_target="tpu_custom_call" | custom-call | tf_op jit(solution)/shard_map/pallas_call | solution.py:75
  11.0 2.1 %collective-permute-start.7 = (bf16[4,384,256]{2,1,0:T(8,128)(2,1)S(1)}, bf16[4,384,256]{2,1,0:T(8,128)(2,1)S(1)}, u32[]{:S(2)}, u32[]{:S(2)}) collective-permute-start(bf16[4,384,256]{2,1,0:T(8,128)(2,1)S(1)} %get-tuple-element.21), channel_id=1, source_target_pairs={{0,8},{1,9},{2,10},{3,11},{4,12},{5,13},{6,14},{7,15}} | collective-permute-start | bytes 2359304 | tf_op jit(solution)/shard_map/ppermute | solution.py:260
  13.1 1.3 %collective-permute-start.5 = (bf16[2,384,256]{2,1,0:T(8,128)(2,1)S(1)}, bf16[2,384,256]{2,1,0:T(8,128)(2,1)S(1)}, u32[]{:S(2)}, u32[]{:S(2)}) collective-permute-start(bf16[2,384,256]{2,1,0:T(8,128)(2,1)S(1)} %get-tuple-element.18), channel_id=1, source_target_pairs={{0,16},{1,17},{2,18},{3,19},{4,20},{5,21},{6,22},{7,23}} | collective-permute-start | bytes 1179656 | tf_op jit(solution)/shard_map/ppermute | solution.py:260
  14.4 4.0 %collective-permute-done.x = bf16[256,512]{1,0:T(8,128)(2,1)S(1)} collective-permute-done((bf16[256,512]{1,0:T(8,128)(2,1)S(1)}, bf16[256,512]{1,0:T(8,128)(2,1)S(1)}, u32[]{:S(2)}, u32[]{:S(2)}) %collective-permute-start) | collective-permute-done | bytes 262176 | tf_op jit(solution)/shard_map/ppermute | solution.py:260
  18.4 0.1 shard_map.61
  18.5 3.7 %collective-permute-start.8 = (bf16[4,384,256]{2,1,0:T(8,128)(2,1)S(1)}, bf16[4,384,256]{2,1,0:T(8,128)(2,1)S(1)}, u32[]{:S(2)}, u32[]{:S(2)}) collective-permute-start(bf16[4,384,256]{2,1,0:T(8,128)(2,1)S(1)} %shard_map.61), channel_id=1, source_target_pairs={{0,16},{1,17},{2,18},{3,19},{4,20},{5,21},{6,22},{7,23}} | collective-permute-start | bytes 2359304 | tf_op jit(solution)/shard_map/ppermute | solution.py:260
  22.2 0.9 %collective-permute-done.5.after = bf16[2,384,256]{2,1,0:T(8,128)(2,1)S(1)} collective-permute-done((bf16[2,384,256]{2,1,0:T(8,128)(2,1)S(1)}, bf16[2,384,256]{2,1,0:T(8,128)(2,1)S(1)}, u32[]{:S(2)}, u32[]{:S(2)}) %collective-permute-start.5) | collective-permute-done | bytes 393248 | tf_op jit(solution)/shard_map/ppermute | solution.py:260
  23.2 0.7 %collective-permute-start.10 = (bf16[2,384,256]{2,1,0:T(8,128)(2,1)S(1)}, bf16[2,384,256]{2,1,0:T(8,128)(2,1)S(1)}, u32[]{:S(2)}, u32[]{:S(2)}) collective-permute-start(bf16[2,384,256]{2,1,0:T(8,128)(2,1)S(1)} %collective-permute-done.5.after), channel_id=1, source_target_pairs={{16,24},{17,25},{18,26},{19,27},{20,28},{21,29},{22,30},{23,31}} | collective-permute-start | bytes 1179656 | tf_op jit(solution)/shard_map/ppermute | solution.py:260
  23.9 1.1 %shard_map.59 = (bf16[256,2048]{1,0:T(8,128)(2,1)}, f32[8,128]{1,0:T(8,128)S(1)}) custom-call(bf16[2,384,256]{2,1,0:T(8,128)(2,1)S(1)} %collective-permute-done.5.after), custom_call_target="tpu_custom_call" | custom-call | tf_op jit(solution)/shard_map/pallas_call | solution.py:75
  24.9 4.5 %collective-permute-done.7.rest_0_.b = bf16[4,384,256]{2,1,0:T(8,128)(2,1)S(1)} collective-permute-done((bf16[4,384,256]{2,1,0:T(8,128)(2,1)S(1)}, bf16[4,384,256]{2,1,0:T(8,128)(2,1)S(1)}, u32[]{:S(2)}, u32[]{:S(2)}) %collective-permute-start.7) | collective-permute-done | bytes 786464 | tf_op jit(solution)/shard_map/ppermute | solution.py:260
  29.5 1.3 %collective-permute-start.9 = (bf16[2,384,256]{2,1,0:T(8,128)(2,1)S(1)}, bf16[2,384,256]{2,1,0:T(8,128)(2,1)S(1)}, u32[]{:S(2)}, u32[]{:S(2)}) collective-permute-start(bf16[2,384,256]{2,1,0:T(8,128)(2,1)S(1)} %shard_map.62), channel_id=1, source_target_pairs={{0,24},{1,25},{2,26},{3,27},{4,28},{5,29},{6,30},{7,31}} | collective-permute-start | bytes 1179656 | tf_op jit(solution)/shard_map/ppermute | solution.py:260
  30.8 0.0 collective-permute-done.2.other
  30.8 0.0 collective-permute-done.3.rest_0_.near
  30.8 0.5 collective-permute-start.6
  31.4 7.8 %collective-permute-done.8.c = bf16[4,384,256]{2,1,0:T(8,128)(2,1)S(1)} collective-permute-done((bf16[4,384,256]{2,1,0:T(8,128)(2,1)S(1)}, bf16[4,384,256]{2,1,0:T(8,128)(2,1)S(1)}, u32[]{:S(2)}, u32[]{:S(2)}) %collective-permute-start.8) | collective-permute-done | bytes 786464 | tf_op jit(solution)/shard_map/ppermute | solution.py:260
  39.2 0.0 collective-permute-done.10.d_high
  39.2 0.0 collective-permute-done.9.d_low
  39.2 0.1 shard_map.63
  39.3 0.1 collective-permute-start.11
  39.4 0.5 collective-permute-start.12
  39.9 0.5 shard_map.64.before
  40.3 0.7 %collective-permute-done.11.low.refs_2_ = bf16[2,384,256]{2,1,0:T(8,128)(2,1)S(1)} collective-permute-done((bf16[2,384,256]{2,1,0:T(8,128)(2,1)S(1)}, bf16[2,384,256]{2,1,0:T(8,128)(2,1)S(1)}, u32[]{:S(2)}, u32[]{:S(2)}) %collective-permute-start.11) | collective-permute-done | bytes 393248 | tf_op jit(solution)/shard_map/ppermute | solution.py:263
  41.1 0.6 %collective-permute-done.12.high.refs_3_ = bf16[2,384,256]{2,1,0:T(8,128)(2,1)S(1)} collective-permute-done((bf16[2,384,256]{2,1,0:T(8,128)(2,1)S(1)}, bf16[2,384,256]{2,1,0:T(8,128)(2,1)S(1)}, u32[]{:S(2)}, u32[]{:S(2)}) %collective-permute-start.12) | collective-permute-done | bytes 393248 | tf_op jit(solution)/shard_map/ppermute | solution.py:263
  41.6 0.5 shard_map.65.refs_4_
  42.1 0.0 copy-start.3
  42.1 0.0 copy-start.1
  42.1 2.1 %collective-permute-done.6.last = bf16[512,512]{1,0:T(8,128)(2,1)S(1)} collective-permute-done((bf16[512,512]{1,0:T(8,128)(2,1)S(1)}, bf16[512,512]{1,0:T(8,128)(2,1)S(1)}, u32[]{:S(2)}, u32[]{:S(2)}) %collective-permute-start.6) | collective-permute-done | bytes 524320 | tf_op jit(solution)/shard_map/ppermute | solution.py:260
  44.3 0.4 shard_map.66
  44.7 2.0 %collective-permute-start.13 = (bf16[128,512]{1,0:T(8,128)(2,1)S(1)}, bf16[128,512]{1,0:T(8,128)(2,1)S(1)}, u32[]{:S(2)}, u32[]{:S(2)}) collective-permute-start(bf16[128,512]{1,0:T(8,128)(2,1)S(1)} %get-tuple-element.27), channel_id=1, source_target_pairs={{0,24},{1,25},{2,26},{3,27},{4,28},{5,29},{6,30},{7,31},{8,16},{9,... | collective-permute-start | bytes 393224 | tf_op jit(solution)/shard_map/ppermute | solution.py:260
  46.7 0.5 %collective-permute-start.14 = (bf16[128,512]{1,0:T(8,128)(2,1)S(1)}, bf16[128,512]{1,0:T(8,128)(2,1)S(1)}, u32[]{:S(2)}, u32[]{:S(2)}) collective-permute-start(bf16[128,512]{1,0:T(8,128)(2,1)S(1)} %get-tuple-element.28), channel_id=1, source_target_pairs={{0,8},{1,9},{2,10},{3,11},{4,12},{5,13},{6,14},{7,15},{8,0},{9,1},... | collective-permute-start | bytes 393224 | tf_op jit(solution)/shard_map/ppermute | solution.py:260
  47.3 1.0 %collective-permute-start.15 = (bf16[128,512]{1,0:T(8,128)(2,1)S(1)}, bf16[128,512]{1,0:T(8,128)(2,1)S(1)}, u32[]{:S(2)}, u32[]{:S(2)}) collective-permute-start(bf16[128,512]{1,0:T(8,128)(2,1)S(1)} %get-tuple-element.29), channel_id=1, source_target_pairs={{0,16},{1,17},{2,18},{3,19},{4,20},{5,21},{6,22},{7,23},{8,24},{9,... | collective-permute-start | bytes 393224 | tf_op jit(solution)/shard_map/ppermute | solution.py:260
  48.3 0.0 copy-done.3
  48.3 0.1 dynamic-slice_multiply_fusion
  48.3 2.8 %collective-permute-done.13.one = bf16[128,512]{1,0:T(8,128)(2,1)S(1)} collective-permute-done((bf16[128,512]{1,0:T(8,128)(2,1)S(1)}, bf16[128,512]{1,0:T(8,128)(2,1)S(1)}, u32[]{:S(2)}, u32[]{:S(2)}) %collective-permute-start.13) | collective-permute-done | bytes 131104 | tf_op jit(solution)/shard_map/ppermute | solution.py:260
  51.2 1.8 %collective-permute-done.14.two = bf16[128,512]{1,0:T(8,128)(2,1)S(1)} collective-permute-done((bf16[128,512]{1,0:T(8,128)(2,1)S(1)}, bf16[128,512]{1,0:T(8,128)(2,1)S(1)}, u32[]{:S(2)}, u32[]{:S(2)}) %collective-permute-start.14) | collective-permute-done | bytes 131104 | tf_op jit(solution)/shard_map/ppermute | solution.py:260
  52.9 0.1 collective-permute-done.15.three
  53.0 0.1 broadcast_in_dim.2.counts
  53.1 0.0 copy-done.1
  (6 shorter events, 0.1 us)
Async XLA Ops:
  1.4 4.2 %copy-start = (bf16[384,4096]{1,0:T(8,128)(2,1)S(1)}, bf16[384,4096]{1,0:T(8,128)(2,1)}, u32[]{:S(2)}) copy-start(bf16[384,4096]{1,0:T(8,128)(2,1)} %x.3) | copy-start | bytes 9437188
  1.4 4.2 %collective-permute-start.1 = (bf16[256,512]{1,0:T(8,128)(2,1)S(1)}, bf16[256,512]{1,0:T(8,128)(2,1)S(1)}, u32[]{:S(2)}, u32[]{:S(2)}) collective-permute-start(bf16[256,512]{1,0:T(8,128)(2,1)S(1)} %get-tuple-element.31), channel_id=1, source_target_pairs={{0,1},{1,0},{2,3},{3,2},{4,5},{5,4},{6,7},{7,6},{8,9},{9,8},{10,11... | collective-permute-start | bytes 786440 | tf_op jit(solution)/shard_map/ppermute | solution.py:263
  1.9 16.5 %collective-permute-start = (bf16[256,512]{1,0:T(8,128)(2,1)S(1)}, bf16[256,512]{1,0:T(8,128)(2,1)S(1)}, u32[]{:S(2)}, u32[]{:S(2)}) collective-permute-start(bf16[256,512]{1,0:T(8,128)(2,1)S(1)} %get-tuple-element.32.rest_0_.kept), channel_id=1, source_target_pairs={{0,4},{1,5},{2,6},{3,7},{4,0},{5,1},{6,2},{7,3},{8,12},{9,13},{10,... | collective-permute-start | bytes 786440 | tf_op jit(solution)/shard_map/ppermute | solution.py:260
  5.6 0.9 %copy-start.2 = (bf16[4096]{0:T(1024)(128)(2,1)S(1)}, bf16[4096]{0:T(1024)(128)(2,1)}, u32[]{:S(2)}) copy-start(bf16[4096]{0:T(1024)(128)(2,1)} %param.6) | copy-start | bytes 24580
  6.2 3.4 %collective-permute-start.4 = (f32[384,128]{1,0:T(8,128)S(1)}, f32[384,128]{1,0:T(8,128)S(1)}, u32[]{:S(2)}, u32[]{:S(2)}) collective-permute-start(f32[384,128]{1,0:T(8,128)S(1)} %shard_map.57.squares), channel_id=1, source_target_pairs={{0,1},{1,0},{2,3},{3,2},{4,5},{5,4},{6,7},{7,6},{8,9},{9,8},{10,11... | collective-permute-start | bytes 589832 | tf_op jit(solution)/shard_map/ppermute | solution.py:263
  6.5 24.3 %collective-permute-start.3 = (bf16[512,512]{1,0:T(8,128)(2,1)S(1)}, bf16[512,512]{1,0:T(8,128)(2,1)S(1)}, u32[]{:S(2)}, u32[]{:S(2)}) collective-permute-start(bf16[512,512]{1,0:T(8,128)(2,1)S(1)} %shard_map.56.after.own), channel_id=1, source_target_pairs={{0,2},{1,3},{2,0},{3,1},{4,6},{5,7},{6,4},{7,5},{8,10},{9,11},{10,... | collective-permute-start | bytes 1572872 | tf_op jit(solution)/shard_map/ppermute | solution.py:260
  8.1 22.6 %collective-permute-start.2 = (bf16[256,512]{1,0:T(8,128)(2,1)S(1)}, bf16[256,512]{1,0:T(8,128)(2,1)S(1)}, u32[]{:S(2)}, u32[]{:S(2)}) collective-permute-start(bf16[256,512]{1,0:T(8,128)(2,1)S(1)} %collective-permute-done.1.other), channel_id=1, source_target_pairs={{0,4},{1,5},{2,6},{3,7},{4,0},{5,1},{6,2},{7,3},{8,12},{9,13},{10,... | collective-permute-start | bytes 786440 | tf_op jit(solution)/shard_map/ppermute | solution.py:260
  11.0 18.5 %collective-permute-start.7 = (bf16[4,384,256]{2,1,0:T(8,128)(2,1)S(1)}, bf16[4,384,256]{2,1,0:T(8,128)(2,1)S(1)}, u32[]{:S(2)}, u32[]{:S(2)}) collective-permute-start(bf16[4,384,256]{2,1,0:T(8,128)(2,1)S(1)} %get-tuple-element.21), channel_id=1, source_target_pairs={{0,8},{1,9},{2,10},{3,11},{4,12},{5,13},{6,14},{7,15}} | collective-permute-start | bytes 2359304 | tf_op jit(solution)/shard_map/ppermute | solution.py:260
  13.1 10.1 %collective-permute-start.5 = (bf16[2,384,256]{2,1,0:T(8,128)(2,1)S(1)}, bf16[2,384,256]{2,1,0:T(8,128)(2,1)S(1)}, u32[]{:S(2)}, u32[]{:S(2)}) collective-permute-start(bf16[2,384,256]{2,1,0:T(8,128)(2,1)S(1)} %get-tuple-element.18), channel_id=1, source_target_pairs={{0,16},{1,17},{2,18},{3,19},{4,20},{5,21},{6,22},{7,23}} | collective-permute-start | bytes 1179656 | tf_op jit(solution)/shard_map/ppermute | solution.py:260
  18.5 20.7 %collective-permute-start.8 = (bf16[4,384,256]{2,1,0:T(8,128)(2,1)S(1)}, bf16[4,384,256]{2,1,0:T(8,128)(2,1)S(1)}, u32[]{:S(2)}, u32[]{:S(2)}) collective-permute-start(bf16[4,384,256]{2,1,0:T(8,128)(2,1)S(1)} %shard_map.61), channel_id=1, source_target_pairs={{0,16},{1,17},{2,18},{3,19},{4,20},{5,21},{6,22},{7,23}} | collective-permute-start | bytes 2359304 | tf_op jit(solution)/shard_map/ppermute | solution.py:260
  23.2 16.0 %collective-permute-start.10 = (bf16[2,384,256]{2,1,0:T(8,128)(2,1)S(1)}, bf16[2,384,256]{2,1,0:T(8,128)(2,1)S(1)}, u32[]{:S(2)}, u32[]{:S(2)}) collective-permute-start(bf16[2,384,256]{2,1,0:T(8,128)(2,1)S(1)} %collective-permute-done.5.after), channel_id=1, source_target_pairs={{16,24},{17,25},{18,26},{19,27},{20,28},{21,29},{22,30},{23,31}} | collective-permute-start | bytes 1179656 | tf_op jit(solution)/shard_map/ppermute | solution.py:260
  29.5 9.8 %collective-permute-start.9 = (bf16[2,384,256]{2,1,0:T(8,128)(2,1)S(1)}, bf16[2,384,256]{2,1,0:T(8,128)(2,1)S(1)}, u32[]{:S(2)}, u32[]{:S(2)}) collective-permute-start(bf16[2,384,256]{2,1,0:T(8,128)(2,1)S(1)} %shard_map.62), channel_id=1, source_target_pairs={{0,24},{1,25},{2,26},{3,27},{4,28},{5,29},{6,30},{7,31}} | collective-permute-start | bytes 1179656 | tf_op jit(solution)/shard_map/ppermute | solution.py:260
  30.8 13.4 %collective-permute-start.6 = (bf16[512,512]{1,0:T(8,128)(2,1)S(1)}, bf16[512,512]{1,0:T(8,128)(2,1)S(1)}, u32[]{:S(2)}, u32[]{:S(2)}) collective-permute-start(bf16[512,512]{1,0:T(8,128)(2,1)S(1)} %shard_map.60.far), channel_id=1, source_target_pairs={{0,2},{1,3},{2,0},{3,1},{4,6},{5,7},{6,4},{7,5},{8,10},{9,11},{10,... | collective-permute-start | bytes 1572872 | tf_op jit(solution)/shard_map/ppermute | solution.py:260
  39.3 1.8 %collective-permute-start.11 = (bf16[2,384,256]{2,1,0:T(8,128)(2,1)S(1)}, bf16[2,384,256]{2,1,0:T(8,128)(2,1)S(1)}, u32[]{:S(2)}, u32[]{:S(2)}) collective-permute-start(bf16[2,384,256]{2,1,0:T(8,128)(2,1)S(1)} %get-tuple-element.24.low.refs_0_), channel_id=1, source_target_pairs={{0,1},{1,0},{2,3},{3,2},{4,5},{5,4},{6,7},{7,6},{8,9},{9,8},{10,11... | collective-permute-start | bytes 1179656 | tf_op jit(solution)/shard_map/ppermute | solution.py:263
  39.4 2.3 %collective-permute-start.12 = (bf16[2,384,256]{2,1,0:T(8,128)(2,1)S(1)}, bf16[2,384,256]{2,1,0:T(8,128)(2,1)S(1)}, u32[]{:S(2)}, u32[]{:S(2)}) collective-permute-start(bf16[2,384,256]{2,1,0:T(8,128)(2,1)S(1)} %get-tuple-element.25.high.refs_1_), channel_id=1, source_target_pairs={{0,1},{1,0},{2,3},{3,2},{4,5},{5,4},{6,7},{7,6},{8,9},{9,8},{10,11... | collective-permute-start | bytes 1179656 | tf_op jit(solution)/shard_map/ppermute | solution.py:263
  42.1 6.1 %copy-start.3 = (s32[6]{0:T(128)S(1)}, s32[6]{0:T(128)}, u32[]{:S(2)}) copy-start(s32[6]{0:T(128)} %param.8) | copy-start | bytes 76
  42.1 10.9 %copy-start.1 = (bf16[256,2048]{1,0:T(8,128)(2,1)S(1)}, bf16[256,2048]{1,0:T(8,128)(2,1)}, u32[]{:S(2)}) copy-start(bf16[256,2048]{1,0:T(8,128)(2,1)} %q_ref.1) | copy-start | bytes 3145732
  44.7 6.5 %collective-permute-start.13 = (bf16[128,512]{1,0:T(8,128)(2,1)S(1)}, bf16[128,512]{1,0:T(8,128)(2,1)S(1)}, u32[]{:S(2)}, u32[]{:S(2)}) collective-permute-start(bf16[128,512]{1,0:T(8,128)(2,1)S(1)} %get-tuple-element.27), channel_id=1, source_target_pairs={{0,24},{1,25},{2,26},{3,27},{4,28},{5,29},{6,30},{7,31},{8,16},{9,... | collective-permute-start | bytes 393224 | tf_op jit(solution)/shard_map/ppermute | solution.py:260
  46.7 6.2 %collective-permute-start.14 = (bf16[128,512]{1,0:T(8,128)(2,1)S(1)}, bf16[128,512]{1,0:T(8,128)(2,1)S(1)}, u32[]{:S(2)}, u32[]{:S(2)}) collective-permute-start(bf16[128,512]{1,0:T(8,128)(2,1)S(1)} %get-tuple-element.28), channel_id=1, source_target_pairs={{0,8},{1,9},{2,10},{3,11},{4,12},{5,13},{6,14},{7,15},{8,0},{9,1},... | collective-permute-start | bytes 393224 | tf_op jit(solution)/shard_map/ppermute | solution.py:260
  47.3 5.7 %collective-permute-start.15 = (bf16[128,512]{1,0:T(8,128)(2,1)S(1)}, bf16[128,512]{1,0:T(8,128)(2,1)S(1)}, u32[]{:S(2)}, u32[]{:S(2)}) collective-permute-start(bf16[128,512]{1,0:T(8,128)(2,1)S(1)} %get-tuple-element.29), channel_id=1, source_target_pairs={{0,16},{1,17},{2,18},{3,19},{4,20},{5,21},{6,22},{7,23},{8,24},{9,... | collective-permute-start | bytes 393224 | tf_op jit(solution)/shard_map/ppermute | solution.py:260

commit v8 on v7

--- a/solution.py
+++ b/solution.py
@@ -214,33 +214,41 @@
             kv = kv + part[...].astype(jnp.float32)
         kv = kv.astype(jnp.bfloat16)
         slot = lax.broadcasted_iota(jnp.int32, (CAP, 1), 0)
+        width = 2 * HD
+        pairs = [(s, k) for s in range(SAMP) for k in range(kv.shape[1] // width)]
+        block = {
+            (s, k): kv[s * CAP : s * CAP + CAP, k * width : (k + 1) * width] for s, k in pairs
+        }
+        rows = [slice(s * TXT_S, s * TXT_S + TXT_S) for s in range(SAMP)]
+
+        def heads(k):
+            return [slice(h * HD, (h + 1) * HD) for h in range(k * groups_q, (k + 1) * groups_q)]
+
+        scores = {}
+        for s, k in pairs:
+            query = jnp.concatenate([q_ref[rows[s], h] for h in heads(k)], axis=0)
+            scores[s, k] = lax.dot_general(
+                block[s, k][:, :HD],
+                query,
+                (((1,), (1,)), ((), ())),
+                preferred_element_type=jnp.float32,
+            ) * (1.0 / HD**0.5)
         for s, copy in enumerate(copies):
             live = slot < counts[s : s + 1, :1]
-            rows = slice(s * TXT_S, s * TXT_S + TXT_S)
-            for k in range(kv.shape[1] // (2 * HD)):
-                block = kv[s * CAP : s * CAP + CAP, k * 2 * HD : (k + 1) * 2 * HD]
-                heads = [
-                    slice((k * groups_q + j) * HD, (k * groups_q + j + 1) * HD)
-                    for j in range(groups_q)
-                ]
-                query = jnp.concatenate([q_ref[rows, h] for h in heads], axis=0)
-                scores = lax.dot_general(
-                    block[:, :HD],
-                    query,
-                    (((1,), (1,)), ((), ())),
-                    preferred_element_type=jnp.float32,
-                ) * (1.0 / HD**0.5)
-                scores = jnp.where(live, scores, -1e30)
-                expo = jnp.exp(scores - jnp.max(scores, axis=0, keepdims=True))
-                weights = (expo / jnp.sum(expo, axis=0, keepdims=True)).astype(jnp.bfloat16)
+            weights = {}
+            for k in [k for r, k in pairs if r == s]:
+                x = jnp.where(live, scores[s, k], -1e30)
+                expo = jnp.exp(x - jnp.max(x, axis=0, keepdims=True))
+                weights[k] = (expo / jnp.sum(expo, axis=0, keepdims=True)).astype(jnp.bfloat16)
+            for k, w in weights.items():
                 out = lax.dot_general(
-                    weights,
-                    block[:, HD:],
+                    w,
+                    block[s, k][:, HD:],
                     (((0,), (0,)), ((), ())),
                     preferred_element_type=jnp.float32,
                 )
-                for j, h in enumerate(heads):
-                    held[rows, h] = out[j * TXT_S : (j + 1) * TXT_S].astype(jnp.bfloat16)
+                for j, h in enumerate(heads(k)):
+                    held[rows[s], h] = out[j * TXT_S : (j + 1) * TXT_S].astype(jnp.bfloat16)
             copy.start()
         for copy in copies:
             copy.wait()

time: 53.8 us -> 53.5 us (level)
  no operation moved by 1% of the time
where the time goes in v8:
time: 53.5 us; the launch traced here: 53.1 us
  waiting for transfers between devices  25.4 us (47%)
  starting transfers between devices  21.3 us (40%)
  Pallas kernels  4.64 us (9%)
  local copies, waits for them, and re-layouts  1.46 us (3%)
    ppermute x12, waiting for transfers between devices, send(): lax.ppermute(x, AXES, [(index(a, c), index(b, c)) for a, b in pairs for c...  24.1 us
    ppermute x12, starting transfers between devices, send(): lax.ppermute(x, AXES, [(index(a, c), index(b, c)) for a, b in pairs for c...  20 us
    pallas_call x13, Pallas kernels, call(): pl.pallas_call(body, out_shape=outs, in_specs=specs or [VMEM] * len(args)...  4.64 us
    dynamic_slice x1, local copies, waits for them, and re-layouts, shards_line(): given = lax.dynamic_slice_in_dim(w, (1 - t) * half, half, axis=1)  1.35 us
    ppermute x4, starting transfers between devices, swap(): return lax.ppermute(x, 'tp', [(0, 1), (1, 0)])  1.31 us
    ppermute x4, waiting for transfers between devices, swap(): return lax.ppermute(x, 'tp', [(0, 1), (1, 0)])  1.3 us
  transfers between devices with their start and end apart: 16, of which 10 were waited for; matrix products, arithmetic and copies ran while one was open for 0% of the time, Pallas kernels for 8%

profile of v8, /device:TPU:0, one launch (start us, length us, event | category | flops | bytes accessed | tf_op | source)
XLA Modules:
  0.0 53.1 jit_solution(4018063070287437494)
XLA Ops:
  0.0 1.4 %fusion = (bf16[256,512]{1,0:T(8,128)(2,1)S(1)}, bf16[256,512]{1,0:T(8,128)(2,1)S(1)}) fusion(bf16[1024,1024]{1,0:T(8,128)(2,1)} %param.7, s32[]{:T(128)S(6)} %select_n.20, s32[]{:T(128)S(6)} %select_n.24, s32[]{:T(128)S(6)} %select_n.22), kind=kLoop, calls=%fused_computation.1 | loop fusion | bytes 1048588 | tf_op jit(solution)/shard_map/dynamic_slice | solution.py:275
  1.4 0.0 copy-start
  1.4 0.5 collective-permute-start.1
  1.9 3.7 %collective-permute-start = (bf16[256,512]{1,0:T(8,128)(2,1)S(1)}, bf16[256,512]{1,0:T(8,128)(2,1)S(1)}, u32[]{:S(2)}, u32[]{:S(2)}) collective-permute-start(bf16[256,512]{1,0:T(8,128)(2,1)S(1)} %get-tuple-element.32.rest_0_.kept), channel_id=1, source_target_pairs={{0,4},{1,5},{2,6},{3,7},{4,0},{5,1},{6,2},{7,3},{8,12},{9,13},{10,... | collective-permute-start | bytes 786440 | tf_op jit(solution)/shard_map/ppermute | solution.py:268
  5.5 0.0 collective-permute-done.1.other
  5.6 0.0 copy-done
  5.6 0.0 copy-start.2
  5.6 0.6 %shard_map.57.squares = f32[384,128]{1,0:T(8,128)S(1)} custom-call(bf16[384,4096]{1,0:T(8,128)(2,1)S(1)} %copy-done, bf16[512,512]{1,0:T(8,128)(2,1)S(1)} %shard_map.56.after.own), custom_call_target="tpu_custom_call" | custom-call | tf_op jit(solution)/shard_map/pallas_call | solution.py:75
  6.2 0.2 collective-permute-start.4
  6.5 0.0 copy-done.2
  6.5 1.6 %collective-permute-start.3 = (bf16[512,512]{1,0:T(8,128)(2,1)S(1)}, bf16[512,512]{1,0:T(8,128)(2,1)S(1)}, u32[]{:S(2)}, u32[]{:S(2)}) collective-permute-start(bf16[512,512]{1,0:T(8,128)(2,1)S(1)} %shard_map.56.after.own), channel_id=1, source_target_pairs={{0,2},{1,3},{2,0},{3,1},{4,6},{5,7},{6,4},{7,5},{8,10},{9,11},{10,... | collective-permute-start | bytes 1572872 | tf_op jit(solution)/shard_map/ppermute | solution.py:268
  8.1 1.5 %collective-permute-start.2 = (bf16[256,512]{1,0:T(8,128)(2,1)S(1)}, bf16[256,512]{1,0:T(8,128)(2,1)S(1)}, u32[]{:S(2)}, u32[]{:S(2)}) collective-permute-start(bf16[256,512]{1,0:T(8,128)(2,1)S(1)} %collective-permute-done.1.other), channel_id=1, source_target_pairs={{0,4},{1,5},{2,6},{3,7},{4,0},{5,1},{6,2},{7,3},{8,12},{9,13},{10,... | collective-permute-start | bytes 786440 | tf_op jit(solution)/shard_map/ppermute | solution.py:268
  9.6 0.0 collective-permute-done.4.other
  9.7 1.3 %shard_map.58 = (bf16[4,384,256]{2,1,0:T(8,128)(2,1)S(1)}, bf16[4,384,256]{2,1,0:T(8,128)(2,1)S(1)}, bf16[4,384,256]{2,1,0:T(8,128)(2,1)S(1)}, bf16[2,384,256]{2,1,0:T(8,128)(2,1)S(1)}, bf16[2,384,256]{2,1,0:T(8,128)(2,1)S(1)}) custom-call(bf16[384,4096]{1,0:T(8,128)(2,1)S(1)} %copy-done, f32[384,128]{1,0:T(8,128)S(1)} %shard_map.57.squares, ...), custom_call_target="tpu_custom_call" | custom-call | tf_op jit(solution)/shard_map/pallas_call | solution.py:75
  11.0 2.1 %collective-permute-start.7 = (bf16[4,384,256]{2,1,0:T(8,128)(2,1)S(1)}, bf16[4,384,256]{2,1,0:T(8,128)(2,1)S(1)}, u32[]{:S(2)}, u32[]{:S(2)}) collective-permute-start(bf16[4,384,256]{2,1,0:T(8,128)(2,1)S(1)} %get-tuple-element.21), channel_id=1, source_target_pairs={{0,8},{1,9},{2,10},{3,11},{4,12},{5,13},{6,14},{7,15}} | collective-permute-start | bytes 2359304 | tf_op jit(solution)/shard_map/ppermute | solution.py:268
  13.1 1.3 %collective-permute-start.5 = (bf16[2,384,256]{2,1,0:T(8,128)(2,1)S(1)}, bf16[2,384,256]{2,1,0:T(8,128)(2,1)S(1)}, u32[]{:S(2)}, u32[]{:S(2)}) collective-permute-start(bf16[2,384,256]{2,1,0:T(8,128)(2,1)S(1)} %get-tuple-element.18), channel_id=1, source_target_pairs={{0,16},{1,17},{2,18},{3,19},{4,20},{5,21},{6,22},{7,23}} | collective-permute-start | bytes 1179656 | tf_op jit(solution)/shard_map/ppermute | solution.py:268
  14.4 4.0 %collective-permute-done.x = bf16[256,512]{1,0:T(8,128)(2,1)S(1)} collective-permute-done((bf16[256,512]{1,0:T(8,128)(2,1)S(1)}, bf16[256,512]{1,0:T(8,128)(2,1)S(1)}, u32[]{:S(2)}, u32[]{:S(2)}) %collective-permute-start) | collective-permute-done | bytes 262176 | tf_op jit(solution)/shard_map/ppermute | solution.py:268
  18.4 0.1 shard_map.61
  18.5 3.7 %collective-permute-start.8 = (bf16[4,384,256]{2,1,0:T(8,128)(2,1)S(1)}, bf16[4,384,256]{2,1,0:T(8,128)(2,1)S(1)}, u32[]{:S(2)}, u32[]{:S(2)}) collective-permute-start(bf16[4,384,256]{2,1,0:T(8,128)(2,1)S(1)} %shard_map.61), channel_id=1, source_target_pairs={{0,16},{1,17},{2,18},{3,19},{4,20},{5,21},{6,22},{7,23}} | collective-permute-start | bytes 2359304 | tf_op jit(solution)/shard_map/ppermute | solution.py:268
  22.2 0.9 %collective-permute-done.5.after = bf16[2,384,256]{2,1,0:T(8,128)(2,1)S(1)} collective-permute-done((bf16[2,384,256]{2,1,0:T(8,128)(2,1)S(1)}, bf16[2,384,256]{2,1,0:T(8,128)(2,1)S(1)}, u32[]{:S(2)}, u32[]{:S(2)}) %collective-permute-start.5) | collective-permute-done | bytes 393248 | tf_op jit(solution)/shard_map/ppermute | solution.py:268
  23.2 0.7 %collective-permute-start.10 = (bf16[2,384,256]{2,1,0:T(8,128)(2,1)S(1)}, bf16[2,384,256]{2,1,0:T(8,128)(2,1)S(1)}, u32[]{:S(2)}, u32[]{:S(2)}) collective-permute-start(bf16[2,384,256]{2,1,0:T(8,128)(2,1)S(1)} %collective-permute-done.5.after), channel_id=1, source_target_pairs={{16,24},{17,25},{18,26},{19,27},{20,28},{21,29},{22,30},{23,31}} | collective-permute-start | bytes 1179656 | tf_op jit(solution)/shard_map/ppermute | solution.py:268
  23.9 1.1 %shard_map.59 = (bf16[256,2048]{1,0:T(8,128)(2,1)}, f32[8,128]{1,0:T(8,128)S(1)}) custom-call(bf16[2,384,256]{2,1,0:T(8,128)(2,1)S(1)} %collective-permute-done.5.after), custom_call_target="tpu_custom_call" | custom-call | tf_op jit(solution)/shard_map/pallas_call | solution.py:75
  24.9 4.5 %collective-permute-done.7.rest_0_.b = bf16[4,384,256]{2,1,0:T(8,128)(2,1)S(1)} collective-permute-done((bf16[4,384,256]{2,1,0:T(8,128)(2,1)S(1)}, bf16[4,384,256]{2,1,0:T(8,128)(2,1)S(1)}, u32[]{:S(2)}, u32[]{:S(2)}) %collective-permute-start.7) | collective-permute-done | bytes 786464 | tf_op jit(solution)/shard_map/ppermute | solution.py:268
  29.5 1.3 %collective-permute-start.9 = (bf16[2,384,256]{2,1,0:T(8,128)(2,1)S(1)}, bf16[2,384,256]{2,1,0:T(8,128)(2,1)S(1)}, u32[]{:S(2)}, u32[]{:S(2)}) collective-permute-start(bf16[2,384,256]{2,1,0:T(8,128)(2,1)S(1)} %shard_map.62), channel_id=1, source_target_pairs={{0,24},{1,25},{2,26},{3,27},{4,28},{5,29},{6,30},{7,31}} | collective-permute-start | bytes 1179656 | tf_op jit(solution)/shard_map/ppermute | solution.py:268
  30.8 0.0 collective-permute-done.2.other
  30.8 0.0 collective-permute-done.3.rest_0_.near
  30.8 0.5 collective-permute-start.6
  31.4 7.8 %collective-permute-done.8.c = bf16[4,384,256]{2,1,0:T(8,128)(2,1)S(1)} collective-permute-done((bf16[4,384,256]{2,1,0:T(8,128)(2,1)S(1)}, bf16[4,384,256]{2,1,0:T(8,128)(2,1)S(1)}, u32[]{:S(2)}, u32[]{:S(2)}) %collective-permute-start.8) | collective-permute-done | bytes 786464 | tf_op jit(solution)/shard_map/ppermute | solution.py:268
  39.2 0.0 collective-permute-done.10.d_high
  39.2 0.0 collective-permute-done.9.d_low
  39.2 0.1 shard_map.63
  39.3 0.1 collective-permute-start.11
  39.4 0.5 collective-permute-start.12
  39.9 0.5 shard_map.64.before
  40.3 0.7 %collective-permute-done.11.low.refs_2_ = bf16[2,384,256]{2,1,0:T(8,128)(2,1)S(1)} collective-permute-done((bf16[2,384,256]{2,1,0:T(8,128)(2,1)S(1)}, bf16[2,384,256]{2,1,0:T(8,128)(2,1)S(1)}, u32[]{:S(2)}, u32[]{:S(2)}) %collective-permute-start.11) | collective-permute-done | bytes 393248 | tf_op jit(solution)/shard_map/ppermute | solution.py:271
  41.1 0.6 %collective-permute-done.12.high.refs_3_ = bf16[2,384,256]{2,1,0:T(8,128)(2,1)S(1)} collective-permute-done((bf16[2,384,256]{2,1,0:T(8,128)(2,1)S(1)}, bf16[2,384,256]{2,1,0:T(8,128)(2,1)S(1)}, u32[]{:S(2)}, u32[]{:S(2)}) %collective-permute-start.12) | collective-permute-done | bytes 393248 | tf_op jit(solution)/shard_map/ppermute | solution.py:271
  41.6 0.5 shard_map.65.refs_4_
  42.1 0.0 copy-start.3
  42.1 0.0 copy-start.1
  42.1 2.1 %collective-permute-done.6.last = bf16[512,512]{1,0:T(8,128)(2,1)S(1)} collective-permute-done((bf16[512,512]{1,0:T(8,128)(2,1)S(1)}, bf16[512,512]{1,0:T(8,128)(2,1)S(1)}, u32[]{:S(2)}, u32[]{:S(2)}) %collective-permute-start.6) | collective-permute-done | bytes 524320 | tf_op jit(solution)/shard_map/ppermute | solution.py:268
  44.3 0.4 shard_map.66
  44.7 2.0 %collective-permute-start.13 = (bf16[128,512]{1,0:T(8,128)(2,1)S(1)}, bf16[128,512]{1,0:T(8,128)(2,1)S(1)}, u32[]{:S(2)}, u32[]{:S(2)}) collective-permute-start(bf16[128,512]{1,0:T(8,128)(2,1)S(1)} %get-tuple-element.27), channel_id=1, source_target_pairs={{0,24},{1,25},{2,26},{3,27},{4,28},{5,29},{6,30},{7,31},{8,16},{9,... | collective-permute-start | bytes 393224 | tf_op jit(solution)/shard_map/ppermute | solution.py:268
  46.7 0.5 %collective-permute-start.14 = (bf16[128,512]{1,0:T(8,128)(2,1)S(1)}, bf16[128,512]{1,0:T(8,128)(2,1)S(1)}, u32[]{:S(2)}, u32[]{:S(2)}) collective-permute-start(bf16[128,512]{1,0:T(8,128)(2,1)S(1)} %get-tuple-element.28), channel_id=1, source_target_pairs={{0,8},{1,9},{2,10},{3,11},{4,12},{5,13},{6,14},{7,15},{8,0},{9,1},... | collective-permute-start | bytes 393224 | tf_op jit(solution)/shard_map/ppermute | solution.py:268
  47.3 1.0 %collective-permute-start.15 = (bf16[128,512]{1,0:T(8,128)(2,1)S(1)}, bf16[128,512]{1,0:T(8,128)(2,1)S(1)}, u32[]{:S(2)}, u32[]{:S(2)}) collective-permute-start(bf16[128,512]{1,0:T(8,128)(2,1)S(1)} %get-tuple-element.29), channel_id=1, source_target_pairs={{0,16},{1,17},{2,18},{3,19},{4,20},{5,21},{6,22},{7,23},{8,24},{9,... | collective-permute-start | bytes 393224 | tf_op jit(solution)/shard_map/ppermute | solution.py:268
  48.3 0.0 copy-done.3
  48.3 0.1 dynamic-slice_multiply_fusion
  48.3 2.8 %collective-permute-done.13.one = bf16[128,512]{1,0:T(8,128)(2,1)S(1)} collective-permute-done((bf16[128,512]{1,0:T(8,128)(2,1)S(1)}, bf16[128,512]{1,0:T(8,128)(2,1)S(1)}, u32[]{:S(2)}, u32[]{:S(2)}) %collective-permute-start.13) | collective-permute-done | bytes 131104 | tf_op jit(solution)/shard_map/ppermute | solution.py:268
  51.2 1.8 %collective-permute-done.14.two = bf16[128,512]{1,0:T(8,128)(2,1)S(1)} collective-permute-done((bf16[128,512]{1,0:T(8,128)(2,1)S(1)}, bf16[128,512]{1,0:T(8,128)(2,1)S(1)}, u32[]{:S(2)}, u32[]{:S(2)}) %collective-permute-start.14) | collective-permute-done | bytes 131104 | tf_op jit(solution)/shard_map/ppermute | solution.py:268
  52.9 0.1 collective-permute-done.15.three
  53.0 0.1 broadcast_in_dim.2.counts
  53.1 0.0 copy-done.1
  (6 shorter events, 0.1 us)
Async XLA Ops:
  1.4 4.2 %copy-start = (bf16[384,4096]{1,0:T(8,128)(2,1)S(1)}, bf16[384,4096]{1,0:T(8,128)(2,1)}, u32[]{:S(2)}) copy-start(bf16[384,4096]{1,0:T(8,128)(2,1)} %x.3) | copy-start | bytes 9437188
  1.4 4.2 %collective-permute-start.1 = (bf16[256,512]{1,0:T(8,128)(2,1)S(1)}, bf16[256,512]{1,0:T(8,128)(2,1)S(1)}, u32[]{:S(2)}, u32[]{:S(2)}) collective-permute-start(bf16[256,512]{1,0:T(8,128)(2,1)S(1)} %get-tuple-element.31), channel_id=1, source_target_pairs={{0,1},{1,0},{2,3},{3,2},{4,5},{5,4},{6,7},{7,6},{8,9},{9,8},{10,11... | collective-permute-start | bytes 786440 | tf_op jit(solution)/shard_map/ppermute | solution.py:271
  1.9 16.5 %collective-permute-start = (bf16[256,512]{1,0:T(8,128)(2,1)S(1)}, bf16[256,512]{1,0:T(8,128)(2,1)S(1)}, u32[]{:S(2)}, u32[]{:S(2)}) collective-permute-start(bf16[256,512]{1,0:T(8,128)(2,1)S(1)} %get-tuple-element.32.rest_0_.kept), channel_id=1, source_target_pairs={{0,4},{1,5},{2,6},{3,7},{4,0},{5,1},{6,2},{7,3},{8,12},{9,13},{10,... | collective-permute-start | bytes 786440 | tf_op jit(solution)/shard_map/ppermute | solution.py:268
  5.6 0.9 %copy-start.2 = (bf16[4096]{0:T(1024)(128)(2,1)S(1)}, bf16[4096]{0:T(1024)(128)(2,1)}, u32[]{:S(2)}) copy-start(bf16[4096]{0:T(1024)(128)(2,1)} %param.6) | copy-start | bytes 24580
  6.2 3.4 %collective-permute-start.4 = (f32[384,128]{1,0:T(8,128)S(1)}, f32[384,128]{1,0:T(8,128)S(1)}, u32[]{:S(2)}, u32[]{:S(2)}) collective-permute-start(f32[384,128]{1,0:T(8,128)S(1)} %shard_map.57.squares), channel_id=1, source_target_pairs={{0,1},{1,0},{2,3},{3,2},{4,5},{5,4},{6,7},{7,6},{8,9},{9,8},{10,11... | collective-permute-start | bytes 589832 | tf_op jit(solution)/shard_map/ppermute | solution.py:271
  6.5 24.3 %collective-permute-start.3 = (bf16[512,512]{1,0:T(8,128)(2,1)S(1)}, bf16[512,512]{1,0:T(8,128)(2,1)S(1)}, u32[]{:S(2)}, u32[]{:S(2)}) collective-permute-start(bf16[512,512]{1,0:T(8,128)(2,1)S(1)} %shard_map.56.after.own), channel_id=1, source_target_pairs={{0,2},{1,3},{2,0},{3,1},{4,6},{5,7},{6,4},{7,5},{8,10},{9,11},{10,... | collective-permute-start | bytes 1572872 | tf_op jit(solution)/shard_map/ppermute | solution.py:268
  8.1 22.6 %collective-permute-start.2 = (bf16[256,512]{1,0:T(8,128)(2,1)S(1)}, bf16[256,512]{1,0:T(8,128)(2,1)S(1)}, u32[]{:S(2)}, u32[]{:S(2)}) collective-permute-start(bf16[256,512]{1,0:T(8,128)(2,1)S(1)} %collective-permute-done.1.other), channel_id=1, source_target_pairs={{0,4},{1,5},{2,6},{3,7},{4,0},{5,1},{6,2},{7,3},{8,12},{9,13},{10,... | collective-permute-start | bytes 786440 | tf_op jit(solution)/shard_map/ppermute | solution.py:268
  11.0 18.5 %collective-permute-start.7 = (bf16[4,384,256]{2,1,0:T(8,128)(2,1)S(1)}, bf16[4,384,256]{2,1,0:T(8,128)(2,1)S(1)}, u32[]{:S(2)}, u32[]{:S(2)}) collective-permute-start(bf16[4,384,256]{2,1,0:T(8,128)(2,1)S(1)} %get-tuple-element.21), channel_id=1, source_target_pairs={{0,8},{1,9},{2,10},{3,11},{4,12},{5,13},{6,14},{7,15}} | collective-permute-start | bytes 2359304 | tf_op jit(solution)/shard_map/ppermute | solution.py:268
  13.1 10.1 %collective-permute-start.5 = (bf16[2,384,256]{2,1,0:T(8,128)(2,1)S(1)}, bf16[2,384,256]{2,1,0:T(8,128)(2,1)S(1)}, u32[]{:S(2)}, u32[]{:S(2)}) collective-permute-start(bf16[2,384,256]{2,1,0:T(8,128)(2,1)S(1)} %get-tuple-element.18), channel_id=1, source_target_pairs={{0,16},{1,17},{2,18},{3,19},{4,20},{5,21},{6,22},{7,23}} | collective-permute-start | bytes 1179656 | tf_op jit(solution)/shard_map/ppermute | solution.py:268
  18.5 20.7 %collective-permute-start.8 = (bf16[4,384,256]{2,1,0:T(8,128)(2,1)S(1)}, bf16[4,384,256]{2,1,0:T(8,128)(2,1)S(1)}, u32[]{:S(2)}, u32[]{:S(2)}) collective-permute-start(bf16[4,384,256]{2,1,0:T(8,128)(2,1)S(1)} %shard_map.61), channel_id=1, source_target_pairs={{0,16},{1,17},{2,18},{3,19},{4,20},{5,21},{6,22},{7,23}} | collective-permute-start | bytes 2359304 | tf_op jit(solution)/shard_map/ppermute | solution.py:268
  23.2 16.0 %collective-permute-start.10 = (bf16[2,384,256]{2,1,0:T(8,128)(2,1)S(1)}, bf16[2,384,256]{2,1,0:T(8,128)(2,1)S(1)}, u32[]{:S(2)}, u32[]{:S(2)}) collective-permute-start(bf16[2,384,256]{2,1,0:T(8,128)(2,1)S(1)} %collective-permute-done.5.after), channel_id=1, source_target_pairs={{16,24},{17,25},{18,26},{19,27},{20,28},{21,29},{22,30},{23,31}} | collective-permute-start | bytes 1179656 | tf_op jit(solution)/shard_map/ppermute | solution.py:268
  29.5 9.8 %collective-permute-start.9 = (bf16[2,384,256]{2,1,0:T(8,128)(2,1)S(1)}, bf16[2,384,256]{2,1,0:T(8,128)(2,1)S(1)}, u32[]{:S(2)}, u32[]{:S(2)}) collective-permute-start(bf16[2,384,256]{2,1,0:T(8,128)(2,1)S(1)} %shard_map.62), channel_id=1, source_target_pairs={{0,24},{1,25},{2,26},{3,27},{4,28},{5,29},{6,30},{7,31}} | collective-permute-start | bytes 1179656 | tf_op jit(solution)/shard_map/ppermute | solution.py:268
  30.8 13.4 %collective-permute-start.6 = (bf16[512,512]{1,0:T(8,128)(2,1)S(1)}, bf16[512,512]{1,0:T(8,128)(2,1)S(1)}, u32[]{:S(2)}, u32[]{:S(2)}) collective-permute-start(bf16[512,512]{1,0:T(8,128)(2,1)S(1)} %shard_map.60.far), channel_id=1, source_target_pairs={{0,2},{1,3},{2,0},{3,1},{4,6},{5,7},{6,4},{7,5},{8,10},{9,11},{10,... | collective-permute-start | bytes 1572872 | tf_op jit(solution)/shard_map/ppermute | solution.py:268
  39.3 1.8 %collective-permute-start.11 = (bf16[2,384,256]{2,1,0:T(8,128)(2,1)S(1)}, bf16[2,384,256]{2,1,0:T(8,128)(2,1)S(1)}, u32[]{:S(2)}, u32[]{:S(2)}) collective-permute-start(bf16[2,384,256]{2,1,0:T(8,128)(2,1)S(1)} %get-tuple-element.24.low.refs_0_), channel_id=1, source_target_pairs={{0,1},{1,0},{2,3},{3,2},{4,5},{5,4},{6,7},{7,6},{8,9},{9,8},{10,11... | collective-permute-start | bytes 1179656 | tf_op jit(solution)/shard_map/ppermute | solution.py:271
  39.4 2.3 %collective-permute-start.12 = (bf16[2,384,256]{2,1,0:T(8,128)(2,1)S(1)}, bf16[2,384,256]{2,1,0:T(8,128)(2,1)S(1)}, u32[]{:S(2)}, u32[]{:S(2)}) collective-permute-start(bf16[2,384,256]{2,1,0:T(8,128)(2,1)S(1)} %get-tuple-element.25.high.refs_1_), channel_id=1, source_target_pairs={{0,1},{1,0},{2,3},{3,2},{4,5},{5,4},{6,7},{7,6},{8,9},{9,8},{10,11... | collective-permute-start | bytes 1179656 | tf_op jit(solution)/shard_map/ppermute | solution.py:271
  42.1 6.1 %copy-start.3 = (s32[6]{0:T(128)S(1)}, s32[6]{0:T(128)}, u32[]{:S(2)}) copy-start(s32[6]{0:T(128)} %param.8) | copy-start | bytes 76
  42.1 10.9 %copy-start.1 = (bf16[256,2048]{1,0:T(8,128)(2,1)S(1)}, bf16[256,2048]{1,0:T(8,128)(2,1)}, u32[]{:S(2)}) copy-start(bf16[256,2048]{1,0:T(8,128)(2,1)} %q_ref.1) | copy-start | bytes 3145732
  44.7 6.5 %collective-permute-start.13 = (bf16[128,512]{1,0:T(8,128)(2,1)S(1)}, bf16[128,512]{1,0:T(8,128)(2,1)S(1)}, u32[]{:S(2)}, u32[]{:S(2)}) collective-permute-start(bf16[128,512]{1,0:T(8,128)(2,1)S(1)} %get-tuple-element.27), channel_id=1, source_target_pairs={{0,24},{1,25},{2,26},{3,27},{4,28},{5,29},{6,30},{7,31},{8,16},{9,... | collective-permute-start | bytes 393224 | tf_op jit(solution)/shard_map/ppermute | solution.py:268
  46.7 6.2 %collective-permute-start.14 = (bf16[128,512]{1,0:T(8,128)(2,1)S(1)}, bf16[128,512]{1,0:T(8,128)(2,1)S(1)}, u32[]{:S(2)}, u32[]{:S(2)}) collective-permute-start(bf16[128,512]{1,0:T(8,128)(2,1)S(1)} %get-tuple-element.28), channel_id=1, source_target_pairs={{0,8},{1,9},{2,10},{3,11},{4,12},{5,13},{6,14},{7,15},{8,0},{9,1},... | collective-permute-start | bytes 393224 | tf_op jit(solution)/shard_map/ppermute | solution.py:268
  47.3 5.7 %collective-permute-start.15 = (bf16[128,512]{1,0:T(8,128)(2,1)S(1)}, bf16[128,512]{1,0:T(8,128)(2,1)S(1)}, u32[]{:S(2)}, u32[]{:S(2)}) collective-permute-start(bf16[128,512]{1,0:T(8,128)(2,1)S(1)} %get-tuple-element.29), channel_id=1, source_target_pairs={{0,16},{1,17},{2,18},{3,19},{4,20},{5,21},{6,22},{7,23},{8,24},{9,... | collective-permute-start | bytes 393224 | tf_op jit(solution)/shard_map/ppermute | solution.py:268

commit v9 on v8

--- a/solution.py
+++ b/solution.py
@@ -107,18 +107,22 @@
 
 
 def normalise(x, squares, other, gain, a, b, c, d_low, d_high):
-    width = x.shape[1] // 16
+    lanes = gain.shape[1]
+    tiles = x.shape[1] // 16 // lanes
 
     @pl.when(lax.axis_index("grp") == 0)
     def _():
         total = jnp.sum(squares[...] + other[...], axis=1, keepdims=True)
         scale = lax.rsqrt(total / D + 1e-05)
+        gains = gain[...].astype(jnp.float32)
         for z in range(4):
             for h in range(4):
-                cols = slice((z * 4 + h) * width, (z * 4 + h + 1) * width)
-                y = x[:, cols].astype(jnp.float32) * scale * gain[:, cols].astype(jnp.float32)
                 out, at = ((a, b, c)[h], z) if h < 3 else ((d_low, d_high)[z // 2], z % 2)
-                out[at] = y.astype(jnp.bfloat16)
+                for i in range(tiles):
+                    k = (z * 4 + h) * tiles + i
+                    y = x[:, k * lanes : (k + 1) * lanes].astype(jnp.float32) * scale
+                    y = y * gains[k : k + 1]
+                    out[at, :, i * lanes : (i + 1) * lanes] = y.astype(jnp.bfloat16)
 
 
 def later(x, *rest):
@@ -280,7 +284,7 @@
     def swap_planes(x, k):
         return send(x, [((c, z), (c, z ^ k)) for c in range(4) for z in planes])
 
-    near, far, other_far = swap_planes(own, 1), swap_planes(kept, 2), swap_planes(other, 2)
+    near, far = swap_planes(own, 1), swap_planes(kept, 2)
     far = call(later, [(kept.shape, bf16)], far, kept, specs=[VMEM, ANY], cost=EARLY)[0]
 
     squares = call(row_squares, [((n_rows, 128), f32)], image_rows, own, specs=[VMEM, ANY])[0]
@@ -291,8 +295,10 @@
         image_rows,
         squares,
         swap(squares),
-        enc_gain.reshape(1, -1),
-    )
+        enc_gain.reshape(-1, 128),
+    )
+    other_far = call(later, [(kept.shape, bf16)], other, a, specs=[VMEM, ANY], cost=0)[0]
+    other_far = swap_planes(other_far, 2)
     to_b, to_c, to_d = ([((0, z), (h, z)) for z in planes] for h in (1, 2, 3))
     d_high, b = send(d_high, to_c), send(b, to_b)
     c = call(later, [whole], c, far, specs=[VMEM, ANY], cost=0)[0]

time: 53.5 us -> 53.2 us (level)
  starting transfers between devices: 21.3 us -> 20.5 us
    ppermute x12, starting transfers between devices: 20 us -> 19.2 us  [send(): lax.ppermute(x, AXES, [(index(a, c), index(b, c)) for a, b in pairs for c...]
    pallas_call x13 -> x14, Pallas kernels: 4.64 us -> 4.68 us  [call(): pl.pallas_call(body, out_shape=outs, in_specs=specs or [VMEM] * len(args)...]
where the time goes in v9:
time: 53.2 us; the launch traced here: 52.5 us
  waiting for transfers between devices  25.6 us (48%)
  starting transfers between devices  20.5 us (39%)
  Pallas kernels  4.68 us (9%)
  local copies, waits for them, and re-layouts  1.44 us (3%)
    ppermute x12, waiting for transfers between devices, send(): lax.ppermute(x, AXES, [(index(a, c), index(b, c)) for a, b in pairs for c...  24.3 us
    ppermute x12, starting transfers between devices, send(): lax.ppermute(x, AXES, [(index(a, c), index(b, c)) for a, b in pairs for c...  19.2 us
    pallas_call x14, Pallas kernels, call(): pl.pallas_call(body, out_shape=outs, in_specs=specs or [VMEM] * len(args)...  4.68 us
    dynamic_slice x1, local copies, waits for them, and re-layouts, shards_line(): given = lax.dynamic_slice_in_dim(w, (1 - t) * half, half, axis=1)  1.35 us
    ppermute x4, starting transfers between devices, swap(): return lax.ppermute(x, 'tp', [(0, 1), (1, 0)])  1.31 us
    ppermute x4, waiting for transfers between devices, swap(): return lax.ppermute(x, 'tp', [(0, 1), (1, 0)])  1.3 us
  transfers between devices with their start and end apart: 16, of which 10 were waited for; matrix products, arithmetic and copies ran while one was open for 0% of the time, Pallas kernels for 8%

profile of v9, /device:TPU:0, one launch (start us, length us, event | category | flops | bytes accessed | tf_op | source)
XLA Modules:
  0.0 52.5 jit_solution(7463872000044006091)
XLA Ops:
  0.0 1.4 %fusion = (bf16[256,512]{1,0:T(8,128)(2,1)S(1)}, bf16[256,512]{1,0:T(8,128)(2,1)S(1)}) fusion(bf16[1024,1024]{1,0:T(8,128)(2,1)} %param.7, s32[]{:T(128)S(6)} %select_n.20, s32[]{:T(128)S(6)} %select_n.24, s32[]{:T(128)S(6)} %select_n.22), kind=kLoop, calls=%fused_computation.1 | loop fusion | bytes 1048588 | tf_op jit(solution)/shard_map/dynamic_slice | solution.py:279
  1.4 0.0 copy-start
  1.4 0.5 collective-permute-start.1
  1.9 3.7 %collective-permute-start = (bf16[256,512]{1,0:T(8,128)(2,1)S(1)}, bf16[256,512]{1,0:T(8,128)(2,1)S(1)}, u32[]{:S(2)}, u32[]{:S(2)}) collective-permute-start(bf16[256,512]{1,0:T(8,128)(2,1)S(1)} %get-tuple-element.32.rest_0_.kept), channel_id=1, source_target_pairs={{0,4},{1,5},{2,6},{3,7},{4,0},{5,1},{6,2},{7,3},{8,12},{9,13},{10,... | collective-permute-start | bytes 786440 | tf_op jit(solution)/shard_map/ppermute | solution.py:272
  5.5 0.0 collective-permute-done.1.other.x
  5.6 0.0 copy-done
  5.6 0.0 copy-start.2
  5.6 0.6 %shard_map.57.squares = f32[384,128]{1,0:T(8,128)S(1)} custom-call(bf16[384,4096]{1,0:T(8,128)(2,1)S(1)} %copy-done, bf16[512,512]{1,0:T(8,128)(2,1)S(1)} %shard_map.56.after.own), custom_call_target="tpu_custom_call" | custom-call | tf_op jit(solution)/shard_map/pallas_call | solution.py:75
  6.2 0.2 collective-permute-start.2
  6.5 1.6 %collective-permute-start.4 = (bf16[512,512]{1,0:T(8,128)(2,1)S(1)}, bf16[512,512]{1,0:T(8,128)(2,1)S(1)}, u32[]{:S(2)}, u32[]{:S(2)}) collective-permute-start(bf16[512,512]{1,0:T(8,128)(2,1)S(1)} %shard_map.56.after.own), channel_id=1, source_target_pairs={{0,2},{1,3},{2,0},{3,1},{4,6},{5,7},{6,4},{7,5},{8,10},{9,11},{10,... | collective-permute-start | bytes 1572872 | tf_op jit(solution)/shard_map/ppermute | solution.py:272
  8.0 0.0 collective-permute-done.2.other
  8.1 0.0 copy-done.2
  8.1 1.3 %shard_map.58 = (bf16[4,384,256]{2,1,0:T(8,128)(2,1)S(1)}, bf16[4,384,256]{2,1,0:T(8,128)(2,1)S(1)}, bf16[4,384,256]{2,1,0:T(8,128)(2,1)S(1)}, bf16[2,384,256]{2,1,0:T(8,128)(2,1)S(1)}, bf16[2,384,256]{2,1,0:T(8,128)(2,1)S(1)}) custom-call(bf16[384,4096]{1,0:T(8,128)(2,1)S(1)} %copy-done, f32[384,128]{1,0:T(8,128)S(1)} %shard_map.57.squares, ...), custom_call_target="tpu_custom_call" | custom-call | tf_op jit(solution)/shard_map/pallas_call | solution.py:75
  9.4 1.5 %collective-permute-start.7 = (bf16[4,384,256]{2,1,0:T(8,128)(2,1)S(1)}, bf16[4,384,256]{2,1,0:T(8,128)(2,1)S(1)}, u32[]{:S(2)}, u32[]{:S(2)}) collective-permute-start(bf16[4,384,256]{2,1,0:T(8,128)(2,1)S(1)} %get-tuple-element.21), channel_id=1, source_target_pairs={{0,8},{1,9},{2,10},{3,11},{4,12},{5,13},{6,14},{7,15}} | collective-permute-start | bytes 2359304 | tf_op jit(solution)/shard_map/ppermute | solution.py:272
  10.9 1.3 %collective-permute-start.5 = (bf16[2,384,256]{2,1,0:T(8,128)(2,1)S(1)}, bf16[2,384,256]{2,1,0:T(8,128)(2,1)S(1)}, u32[]{:S(2)}, u32[]{:S(2)}) collective-permute-start(bf16[2,384,256]{2,1,0:T(8,128)(2,1)S(1)} %get-tuple-element.19), channel_id=1, source_target_pairs={{0,16},{1,17},{2,18},{3,19},{4,20},{5,21},{6,22},{7,23}} | collective-permute-start | bytes 1179656 | tf_op jit(solution)/shard_map/ppermute | solution.py:272
  12.2 1.5 %collective-permute-start.3 = (bf16[256,512]{1,0:T(8,128)(2,1)S(1)}, bf16[256,512]{1,0:T(8,128)(2,1)S(1)}, u32[]{:S(2)}, u32[]{:S(2)}) collective-permute-start(bf16[256,512]{1,0:T(8,128)(2,1)S(1)} %shard_map.59), channel_id=1, source_target_pairs={{0,4},{1,5},{2,6},{3,7},{4,0},{5,1},{6,2},{7,3},{8,12},{9,13},{10,... | collective-permute-start | bytes 786440 | tf_op jit(solution)/shard_map/ppermute | solution.py:272
  13.7 4.7 %collective-permute-done.x = bf16[256,512]{1,0:T(8,128)(2,1)S(1)} collective-permute-done((bf16[256,512]{1,0:T(8,128)(2,1)S(1)}, bf16[256,512]{1,0:T(8,128)(2,1)S(1)}, u32[]{:S(2)}, u32[]{:S(2)}) %collective-permute-start) | collective-permute-done | bytes 262176 | tf_op jit(solution)/shard_map/ppermute | solution.py:272
  18.4 0.1 shard_map.62
  18.5 3.7 %collective-permute-start.8 = (bf16[4,384,256]{2,1,0:T(8,128)(2,1)S(1)}, bf16[4,384,256]{2,1,0:T(8,128)(2,1)S(1)}, u32[]{:S(2)}, u32[]{:S(2)}) collective-permute-start(bf16[4,384,256]{2,1,0:T(8,128)(2,1)S(1)} %shard_map.62), channel_id=1, source_target_pairs={{0,16},{1,17},{2,18},{3,19},{4,20},{5,21},{6,22},{7,23}} | collective-permute-start | bytes 2359304 | tf_op jit(solution)/shard_map/ppermute | solution.py:272
  22.2 0.0 collective-permute-done.5.after
  22.3 0.7 %collective-permute-start.10 = (bf16[2,384,256]{2,1,0:T(8,128)(2,1)S(1)}, bf16[2,384,256]{2,1,0:T(8,128)(2,1)S(1)}, u32[]{:S(2)}, u32[]{:S(2)}) collective-permute-start(bf16[2,384,256]{2,1,0:T(8,128)(2,1)S(1)} %collective-permute-done.5.after), channel_id=1, source_target_pairs={{16,24},{17,25},{18,26},{19,27},{20,28},{21,29},{22,30},{23,31}} | collective-permute-start | bytes 1179656 | tf_op jit(solution)/shard_map/ppermute | solution.py:272
  23.0 1.1 %shard_map.60 = (bf16[256,2048]{1,0:T(8,128)(2,1)}, f32[8,128]{1,0:T(8,128)S(1)}) custom-call(bf16[2,384,256]{2,1,0:T(8,128)(2,1)S(1)} %collective-permute-done.5.after), custom_call_target="tpu_custom_call" | custom-call | tf_op jit(solution)/shard_map/pallas_call | solution.py:75
  24.0 4.0 %collective-permute-done.7.rest_0_.b = bf16[4,384,256]{2,1,0:T(8,128)(2,1)S(1)} collective-permute-done((bf16[4,384,256]{2,1,0:T(8,128)(2,1)S(1)}, bf16[4,384,256]{2,1,0:T(8,128)(2,1)S(1)}, u32[]{:S(2)}, u32[]{:S(2)}) %collective-permute-start.7) | collective-permute-done | bytes 786464 | tf_op jit(solution)/shard_map/ppermute | solution.py:272
  28.0 1.3 %collective-permute-start.9 = (bf16[2,384,256]{2,1,0:T(8,128)(2,1)S(1)}, bf16[2,384,256]{2,1,0:T(8,128)(2,1)S(1)}, u32[]{:S(2)}, u32[]{:S(2)}) collective-permute-start(bf16[2,384,256]{2,1,0:T(8,128)(2,1)S(1)} %shard_map.63), channel_id=1, source_target_pairs={{0,24},{1,25},{2,26},{3,27},{4,28},{5,29},{6,30},{7,31}} | collective-permute-start | bytes 1179656 | tf_op jit(solution)/shard_map/ppermute | solution.py:272
  29.3 0.0 collective-permute-done.3.other
  29.3 1.4 %collective-permute-done.4.rest_0_.near = bf16[512,512]{1,0:T(8,128)(2,1)S(1)} collective-permute-done((bf16[512,512]{1,0:T(8,128)(2,1)S(1)}, bf16[512,512]{1,0:T(8,128)(2,1)S(1)}, u32[]{:S(2)}, u32[]{:S(2)}) %collective-permute-start.4) | collective-permute-done | bytes 524320 | tf_op jit(solution)/shard_map/ppermute | solution.py:272
  30.7 0.4 collective-permute-start.6
  31.1 7.2 %collective-permute-done.8.c = bf16[4,384,256]{2,1,0:T(8,128)(2,1)S(1)} collective-permute-done((bf16[4,384,256]{2,1,0:T(8,128)(2,1)S(1)}, bf16[4,384,256]{2,1,0:T(8,128)(2,1)S(1)}, u32[]{:S(2)}, u32[]{:S(2)}) %collective-permute-start.8) | collective-permute-done | bytes 786464 | tf_op jit(solution)/shard_map/ppermute | solution.py:272
  38.3 0.0 collective-permute-done.10.d_high
  38.3 0.0 collective-permute-done.9.d_low
  38.3 0.1 shard_map.64
  38.4 0.1 collective-permute-start.11
  38.5 0.5 collective-permute-start.12
  39.0 0.5 shard_map.65.before
  39.4 0.7 %collective-permute-done.11.low.refs_2_ = bf16[2,384,256]{2,1,0:T(8,128)(2,1)S(1)} collective-permute-done((bf16[2,384,256]{2,1,0:T(8,128)(2,1)S(1)}, bf16[2,384,256]{2,1,0:T(8,128)(2,1)S(1)}, u32[]{:S(2)}, u32[]{:S(2)}) %collective-permute-start.11) | collective-permute-done | bytes 393248 | tf_op jit(solution)/shard_map/ppermute | solution.py:275
  40.2 0.6 %collective-permute-done.12.high.refs_3_ = bf16[2,384,256]{2,1,0:T(8,128)(2,1)S(1)} collective-permute-done((bf16[2,384,256]{2,1,0:T(8,128)(2,1)S(1)}, bf16[2,384,256]{2,1,0:T(8,128)(2,1)S(1)}, u32[]{:S(2)}, u32[]{:S(2)}) %collective-permute-start.12) | collective-permute-done | bytes 393248 | tf_op jit(solution)/shard_map/ppermute | solution.py:275
  40.7 0.5 shard_map.66.refs_4_
  41.2 0.0 copy-start.3
  41.2 0.0 copy-start.1
  41.2 2.9 %collective-permute-done.6.last = bf16[512,512]{1,0:T(8,128)(2,1)S(1)} collective-permute-done((bf16[512,512]{1,0:T(8,128)(2,1)S(1)}, bf16[512,512]{1,0:T(8,128)(2,1)S(1)}, u32[]{:S(2)}, u32[]{:S(2)}) %collective-permute-start.6) | collective-permute-done | bytes 524320 | tf_op jit(solution)/shard_map/ppermute | solution.py:272
  44.2 0.4 shard_map.67
  44.6 2.0 %collective-permute-start.13 = (bf16[128,512]{1,0:T(8,128)(2,1)S(1)}, bf16[128,512]{1,0:T(8,128)(2,1)S(1)}, u32[]{:S(2)}, u32[]{:S(2)}) collective-permute-start(bf16[128,512]{1,0:T(8,128)(2,1)S(1)} %get-tuple-element.27), channel_id=1, source_target_pairs={{0,24},{1,25},{2,26},{3,27},{4,28},{5,29},{6,30},{7,31},{8,16},{9,... | collective-permute-start | bytes 393224 | tf_op jit(solution)/shard_map/ppermute | solution.py:272
  46.6 0.5 %collective-permute-start.14 = (bf16[128,512]{1,0:T(8,128)(2,1)S(1)}, bf16[128,512]{1,0:T(8,128)(2,1)S(1)}, u32[]{:S(2)}, u32[]{:S(2)}) collective-permute-start(bf16[128,512]{1,0:T(8,128)(2,1)S(1)} %get-tuple-element.28), channel_id=1, source_target_pairs={{0,8},{1,9},{2,10},{3,11},{4,12},{5,13},{6,14},{7,15},{8,0},{9,1},... | collective-permute-start | bytes 393224 | tf_op jit(solution)/shard_map/ppermute | solution.py:272
  47.1 1.0 %collective-permute-start.15 = (bf16[128,512]{1,0:T(8,128)(2,1)S(1)}, bf16[128,512]{1,0:T(8,128)(2,1)S(1)}, u32[]{:S(2)}, u32[]{:S(2)}) collective-permute-start(bf16[128,512]{1,0:T(8,128)(2,1)S(1)} %get-tuple-element.29), channel_id=1, source_target_pairs={{0,16},{1,17},{2,18},{3,19},{4,20},{5,21},{6,22},{7,23},{8,24},{9,... | collective-permute-start | bytes 393224 | tf_op jit(solution)/shard_map/ppermute | solution.py:272
  48.2 0.0 copy-done.3
  48.2 0.1 dynamic-slice_multiply_fusion
  48.3 2.8 %collective-permute-done.13.one = bf16[128,512]{1,0:T(8,128)(2,1)S(1)} collective-permute-done((bf16[128,512]{1,0:T(8,128)(2,1)S(1)}, bf16[128,512]{1,0:T(8,128)(2,1)S(1)}, u32[]{:S(2)}, u32[]{:S(2)}) %collective-permute-start.13) | collective-permute-done | bytes 131104 | tf_op jit(solution)/shard_map/ppermute | solution.py:272
  51.0 1.0 %collective-permute-done.14.two = bf16[128,512]{1,0:T(8,128)(2,1)S(1)} collective-permute-done((bf16[128,512]{1,0:T(8,128)(2,1)S(1)}, bf16[128,512]{1,0:T(8,128)(2,1)S(1)}, u32[]{:S(2)}, u32[]{:S(2)}) %collective-permute-start.14) | collective-permute-done | bytes 131104 | tf_op jit(solution)/shard_map/ppermute | solution.py:272
  52.0 0.4 collective-permute-done.15.three
  52.4 0.1 broadcast_in_dim.2.counts
  52.5 0.0 copy-done.1
  (6 shorter events, 0.2 us)
Async XLA Ops:
  1.4 4.2 %copy-start = (bf16[384,4096]{1,0:T(8,128)(2,1)S(1)}, bf16[384,4096]{1,0:T(8,128)(2,1)}, u32[]{:S(2)}) copy-start(bf16[384,4096]{1,0:T(8,128)(2,1)} %x.3) | copy-start | bytes 9437188
  1.4 4.2 %collective-permute-start.1 = (bf16[256,512]{1,0:T(8,128)(2,1)S(1)}, bf16[256,512]{1,0:T(8,128)(2,1)S(1)}, u32[]{:S(2)}, u32[]{:S(2)}) collective-permute-start(bf16[256,512]{1,0:T(8,128)(2,1)S(1)} %get-tuple-element.31), channel_id=1, source_target_pairs={{0,1},{1,0},{2,3},{3,2},{4,5},{5,4},{6,7},{7,6},{8,9},{9,8},{10,11... | collective-permute-start | bytes 786440 | tf_op jit(solution)/shard_map/ppermute | solution.py:275
  1.9 16.5 %collective-permute-start = (bf16[256,512]{1,0:T(8,128)(2,1)S(1)}, bf16[256,512]{1,0:T(8,128)(2,1)S(1)}, u32[]{:S(2)}, u32[]{:S(2)}) collective-permute-start(bf16[256,512]{1,0:T(8,128)(2,1)S(1)} %get-tuple-element.32.rest_0_.kept), channel_id=1, source_target_pairs={{0,4},{1,5},{2,6},{3,7},{4,0},{5,1},{6,2},{7,3},{8,12},{9,13},{10,... | collective-permute-start | bytes 786440 | tf_op jit(solution)/shard_map/ppermute | solution.py:272
  5.6 2.5 %copy-start.2 = (bf16[4096]{0:T(1024)(128)(2,1)S(1)}, bf16[4096]{0:T(1024)(128)(2,1)}, u32[]{:S(2)}) copy-start(bf16[4096]{0:T(1024)(128)(2,1)} %param.6) | copy-start | bytes 24580
  6.2 1.8 %collective-permute-start.2 = (f32[384,128]{1,0:T(8,128)S(1)}, f32[384,128]{1,0:T(8,128)S(1)}, u32[]{:S(2)}, u32[]{:S(2)}) collective-permute-start(f32[384,128]{1,0:T(8,128)S(1)} %shard_map.57.squares), channel_id=1, source_target_pairs={{0,1},{1,0},{2,3},{3,2},{4,5},{5,4},{6,7},{7,6},{8,9},{9,8},{10,11... | collective-permute-start | bytes 589832 | tf_op jit(solution)/shard_map/ppermute | solution.py:275
  6.5 24.2 %collective-permute-start.4 = (bf16[512,512]{1,0:T(8,128)(2,1)S(1)}, bf16[512,512]{1,0:T(8,128)(2,1)S(1)}, u32[]{:S(2)}, u32[]{:S(2)}) collective-permute-start(bf16[512,512]{1,0:T(8,128)(2,1)S(1)} %shard_map.56.after.own), channel_id=1, source_target_pairs={{0,2},{1,3},{2,0},{3,1},{4,6},{5,7},{6,4},{7,5},{8,10},{9,11},{10,... | collective-permute-start | bytes 1572872 | tf_op jit(solution)/shard_map/ppermute | solution.py:272
  9.4 18.6 %collective-permute-start.7 = (bf16[4,384,256]{2,1,0:T(8,128)(2,1)S(1)}, bf16[4,384,256]{2,1,0:T(8,128)(2,1)S(1)}, u32[]{:S(2)}, u32[]{:S(2)}) collective-permute-start(bf16[4,384,256]{2,1,0:T(8,128)(2,1)S(1)} %get-tuple-element.21), channel_id=1, source_target_pairs={{0,8},{1,9},{2,10},{3,11},{4,12},{5,13},{6,14},{7,15}} | collective-permute-start | bytes 2359304 | tf_op jit(solution)/shard_map/ppermute | solution.py:272
  10.9 11.4 %collective-permute-start.5 = (bf16[2,384,256]{2,1,0:T(8,128)(2,1)S(1)}, bf16[2,384,256]{2,1,0:T(8,128)(2,1)S(1)}, u32[]{:S(2)}, u32[]{:S(2)}) collective-permute-start(bf16[2,384,256]{2,1,0:T(8,128)(2,1)S(1)} %get-tuple-element.19), channel_id=1, source_target_pairs={{0,16},{1,17},{2,18},{3,19},{4,20},{5,21},{6,22},{7,23}} | collective-permute-start | bytes 1179656 | tf_op jit(solution)/shard_map/ppermute | solution.py:272
  12.2 17.1 %collective-permute-start.3 = (bf16[256,512]{1,0:T(8,128)(2,1)S(1)}, bf16[256,512]{1,0:T(8,128)(2,1)S(1)}, u32[]{:S(2)}, u32[]{:S(2)}) collective-permute-start(bf16[256,512]{1,0:T(8,128)(2,1)S(1)} %shard_map.59), channel_id=1, source_target_pairs={{0,4},{1,5},{2,6},{3,7},{4,0},{5,1},{6,2},{7,3},{8,12},{9,13},{10,... | collective-permute-start | bytes 786440 | tf_op jit(solution)/shard_map/ppermute | solution.py:272
  18.5 19.8 %collective-permute-start.8 = (bf16[4,384,256]{2,1,0:T(8,128)(2,1)S(1)}, bf16[4,384,256]{2,1,0:T(8,128)(2,1)S(1)}, u32[]{:S(2)}, u32[]{:S(2)}) collective-permute-start(bf16[4,384,256]{2,1,0:T(8,128)(2,1)S(1)} %shard_map.62), channel_id=1, source_target_pairs={{0,16},{1,17},{2,18},{3,19},{4,20},{5,21},{6,22},{7,23}} | collective-permute-start | bytes 2359304 | tf_op jit(solution)/shard_map/ppermute | solution.py:272
  22.3 16.0 %collective-permute-start.10 = (bf16[2,384,256]{2,1,0:T(8,128)(2,1)S(1)}, bf16[2,384,256]{2,1,0:T(8,128)(2,1)S(1)}, u32[]{:S(2)}, u32[]{:S(2)}) collective-permute-start(bf16[2,384,256]{2,1,0:T(8,128)(2,1)S(1)} %collective-permute-done.5.after), channel_id=1, source_target_pairs={{16,24},{17,25},{18,26},{19,27},{20,28},{21,29},{22,30},{23,31}} | collective-permute-start | bytes 1179656 | tf_op jit(solution)/shard_map/ppermute | solution.py:272
  28.0 10.3 %collective-permute-start.9 = (bf16[2,384,256]{2,1,0:T(8,128)(2,1)S(1)}, bf16[2,384,256]{2,1,0:T(8,128)(2,1)S(1)}, u32[]{:S(2)}, u32[]{:S(2)}) collective-permute-start(bf16[2,384,256]{2,1,0:T(8,128)(2,1)S(1)} %shard_map.63), channel_id=1, source_target_pairs={{0,24},{1,25},{2,26},{3,27},{4,28},{5,29},{6,30},{7,31}} | collective-permute-start | bytes 1179656 | tf_op jit(solution)/shard_map/ppermute | solution.py:272
  30.7 13.4 %collective-permute-start.6 = (bf16[512,512]{1,0:T(8,128)(2,1)S(1)}, bf16[512,512]{1,0:T(8,128)(2,1)S(1)}, u32[]{:S(2)}, u32[]{:S(2)}) collective-permute-start(bf16[512,512]{1,0:T(8,128)(2,1)S(1)} %shard_map.61.far), channel_id=1, source_target_pairs={{0,2},{1,3},{2,0},{3,1},{4,6},{5,7},{6,4},{7,5},{8,10},{9,11},{10,... | collective-permute-start | bytes 1572872 | tf_op jit(solution)/shard_map/ppermute | solution.py:272
  38.4 1.8 %collective-permute-start.11 = (bf16[2,384,256]{2,1,0:T(8,128)(2,1)S(1)}, bf16[2,384,256]{2,1,0:T(8,128)(2,1)S(1)}, u32[]{:S(2)}, u32[]{:S(2)}) collective-permute-start(bf16[2,384,256]{2,1,0:T(8,128)(2,1)S(1)} %get-tuple-element.24.low.refs_0_), channel_id=1, source_target_pairs={{0,1},{1,0},{2,3},{3,2},{4,5},{5,4},{6,7},{7,6},{8,9},{9,8},{10,11... | collective-permute-start | bytes 1179656 | tf_op jit(solution)/shard_map/ppermute | solution.py:275
  38.5 2.3 %collective-permute-start.12 = (bf16[2,384,256]{2,1,0:T(8,128)(2,1)S(1)}, bf16[2,384,256]{2,1,0:T(8,128)(2,1)S(1)}, u32[]{:S(2)}, u32[]{:S(2)}) collective-permute-start(bf16[2,384,256]{2,1,0:T(8,128)(2,1)S(1)} %get-tuple-element.25.high.refs_1_), channel_id=1, source_target_pairs={{0,1},{1,0},{2,3},{3,2},{4,5},{5,4},{6,7},{7,6},{8,9},{9,8},{10,11... | collective-permute-start | bytes 1179656 | tf_op jit(solution)/shard_map/ppermute | solution.py:275
  41.2 7.0 %copy-start.3 = (s32[6]{0:T(128)S(1)}, s32[6]{0:T(128)}, u32[]{:S(2)}) copy-start(s32[6]{0:T(128)} %param.8) | copy-start | bytes 76
  41.2 11.3 %copy-start.1 = (bf16[256,2048]{1,0:T(8,128)(2,1)S(1)}, bf16[256,2048]{1,0:T(8,128)(2,1)}, u32[]{:S(2)}) copy-start(bf16[256,2048]{1,0:T(8,128)(2,1)} %q_ref.1) | copy-start | bytes 3145732
  44.6 6.4 %collective-permute-start.13 = (bf16[128,512]{1,0:T(8,128)(2,1)S(1)}, bf16[128,512]{1,0:T(8,128)(2,1)S(1)}, u32[]{:S(2)}, u32[]{:S(2)}) collective-permute-start(bf16[128,512]{1,0:T(8,128)(2,1)S(1)} %get-tuple-element.27), channel_id=1, source_target_pairs={{0,24},{1,25},{2,26},{3,27},{4,28},{5,29},{6,30},{7,31},{8,16},{9,... | collective-permute-start | bytes 393224 | tf_op jit(solution)/shard_map/ppermute | solution.py:272
  46.6 5.4 %collective-permute-start.14 = (bf16[128,512]{1,0:T(8,128)(2,1)S(1)}, bf16[128,512]{1,0:T(8,128)(2,1)S(1)}, u32[]{:S(2)}, u32[]{:S(2)}) collective-permute-start(bf16[128,512]{1,0:T(8,128)(2,1)S(1)} %get-tuple-element.28), channel_id=1, source_target_pairs={{0,8},{1,9},{2,10},{3,11},{4,12},{5,13},{6,14},{7,15},{8,0},{9,1},... | collective-permute-start | bytes 393224 | tf_op jit(solution)/shard_map/ppermute | solution.py:272
  47.1 5.3 %collective-permute-start.15 = (bf16[128,512]{1,0:T(8,128)(2,1)S(1)}, bf16[128,512]{1,0:T(8,128)(2,1)S(1)}, u32[]{:S(2)}, u32[]{:S(2)}) collective-permute-start(bf16[128,512]{1,0:T(8,128)(2,1)S(1)} %get-tuple-element.29), channel_id=1, source_target_pairs={{0,16},{1,17},{2,18},{3,19},{4,20},{5,21},{6,22},{7,23},{8,24},{9,... | collective-permute-start | bytes 393224 | tf_op jit(solution)/shard_map/ppermute | solution.py:272

commit v10 on v9

--- a/solution.py
+++ b/solution.py
@@ -336,7 +336,7 @@
     )
     parts = [
         send(x, [((c, z), (c ^ k, z)) for c in range(4) for z in planes])
-        for k, x in zip((3, 1, 2), (parts[2], parts[0], parts[1]))
+        for k, x in zip((3, 2, 1), (parts[2], parts[1], parts[0]))
     ]
     return call(
         attention,

time: 53.2 us -> 53.2 us (level)
  transfers between devices with their start and end apart: 16 -> 16, of which waited for: 10 -> 9; matrix products, arithmetic and copies ran while one was open for 0% -> 0% of each run, Pallas kernels for 8% -> 8%
where the time goes in v10:
time: 53.2 us; the launch traced here: 52.5 us
  waiting for transfers between devices  25.6 us (48%)
  starting transfers between devices  20.5 us (39%)
  Pallas kernels  4.68 us (9%)
  local copies, waits for them, and re-layouts  1.44 us (3%)
    ppermute x12, waiting for transfers between devices, send(): lax.ppermute(x, AXES, [(index(a, c), index(b, c)) for a, b in pairs for c...  24.3 us
    ppermute x12, starting transfers between devices, send(): lax.ppermute(x, AXES, [(index(a, c), index(b, c)) for a, b in pairs for c...  19.2 us
    pallas_call x14, Pallas kernels, call(): pl.pallas_call(body, out_shape=outs, in_specs=specs or [VMEM] * len(args)...  4.68 us
    dynamic_slice x1, local copies, waits for them, and re-layouts, shards_line(): given = lax.dynamic_slice_in_dim(w, (1 - t) * half, half, axis=1)  1.35 us
    ppermute x4, starting transfers between devices, swap(): return lax.ppermute(x, 'tp', [(0, 1), (1, 0)])  1.31 us
    ppermute x4, waiting for transfers between devices, swap(): return lax.ppermute(x, 'tp', [(0, 1), (1, 0)])  1.3 us
  transfers between devices with their start and end apart: 16, of which 9 were waited for; matrix products, arithmetic and copies ran while one was open for 0% of the time, Pallas kernels for 8%

profile of v10, /device:TPU:0, one launch (start us, length us, event | category | flops | bytes accessed | tf_op | source)
XLA Modules:
  0.0 52.5 jit_solution(6457208577024730359)
XLA Ops:
  0.0 1.4 %fusion = (bf16[256,512]{1,0:T(8,128)(2,1)S(1)}, bf16[256,512]{1,0:T(8,128)(2,1)S(1)}) fusion(bf16[1024,1024]{1,0:T(8,128)(2,1)} %param.7, s32[]{:T(128)S(6)} %select_n.20, s32[]{:T(128)S(6)} %select_n.24, s32[]{:T(128)S(6)} %select_n.22), kind=kLoop, calls=%fused_computation.1 | loop fusion | bytes 1048588 | tf_op jit(solution)/shard_map/dynamic_slice | solution.py:279
  1.4 0.0 copy-start
  1.4 0.5 collective-permute-start.1
  1.9 3.7 %collective-permute-start = (bf16[256,512]{1,0:T(8,128)(2,1)S(1)}, bf16[256,512]{1,0:T(8,128)(2,1)S(1)}, u32[]{:S(2)}, u32[]{:S(2)}) collective-permute-start(bf16[256,512]{1,0:T(8,128)(2,1)S(1)} %get-tuple-element.32.rest_0_.kept), channel_id=1, source_target_pairs={{0,4},{1,5},{2,6},{3,7},{4,0},{5,1},{6,2},{7,3},{8,12},{9,13},{10,... | collective-permute-start | bytes 786440 | tf_op jit(solution)/shard_map/ppermute | solution.py:272
  5.5 0.0 collective-permute-done.1.other.x
  5.6 0.0 copy-done
  5.6 0.0 copy-start.2
  5.6 0.6 %shard_map.57.squares = f32[384,128]{1,0:T(8,128)S(1)} custom-call(bf16[384,4096]{1,0:T(8,128)(2,1)S(1)} %copy-done, bf16[512,512]{1,0:T(8,128)(2,1)S(1)} %shard_map.56.after.own), custom_call_target="tpu_custom_call" | custom-call | tf_op jit(solution)/shard_map/pallas_call | solution.py:75
  6.2 0.2 collective-permute-start.2
  6.5 1.6 %collective-permute-start.4 = (bf16[512,512]{1,0:T(8,128)(2,1)S(1)}, bf16[512,512]{1,0:T(8,128)(2,1)S(1)}, u32[]{:S(2)}, u32[]{:S(2)}) collective-permute-start(bf16[512,512]{1,0:T(8,128)(2,1)S(1)} %shard_map.56.after.own), channel_id=1, source_target_pairs={{0,2},{1,3},{2,0},{3,1},{4,6},{5,7},{6,4},{7,5},{8,10},{9,11},{10,... | collective-permute-start | bytes 1572872 | tf_op jit(solution)/shard_map/ppermute | solution.py:272
  8.0 0.0 collective-permute-done.2.other
  8.1 0.0 copy-done.2
  8.1 1.3 %shard_map.58 = (bf16[4,384,256]{2,1,0:T(8,128)(2,1)S(1)}, bf16[4,384,256]{2,1,0:T(8,128)(2,1)S(1)}, bf16[4,384,256]{2,1,0:T(8,128)(2,1)S(1)}, bf16[2,384,256]{2,1,0:T(8,128)(2,1)S(1)}, bf16[2,384,256]{2,1,0:T(8,128)(2,1)S(1)}) custom-call(bf16[384,4096]{1,0:T(8,128)(2,1)S(1)} %copy-done, f32[384,128]{1,0:T(8,128)S(1)} %shard_map.57.squares, ...), custom_call_target="tpu_custom_call" | custom-call | tf_op jit(solution)/shard_map/pallas_call | solution.py:75
  9.4 1.5 %collective-permute-start.7 = (bf16[4,384,256]{2,1,0:T(8,128)(2,1)S(1)}, bf16[4,384,256]{2,1,0:T(8,128)(2,1)S(1)}, u32[]{:S(2)}, u32[]{:S(2)}) collective-permute-start(bf16[4,384,256]{2,1,0:T(8,128)(2,1)S(1)} %get-tuple-element.21), channel_id=1, source_target_pairs={{0,8},{1,9},{2,10},{3,11},{4,12},{5,13},{6,14},{7,15}} | collective-permute-start | bytes 2359304 | tf_op jit(solution)/shard_map/ppermute | solution.py:272
  10.9 1.3 %collective-permute-start.5 = (bf16[2,384,256]{2,1,0:T(8,128)(2,1)S(1)}, bf16[2,384,256]{2,1,0:T(8,128)(2,1)S(1)}, u32[]{:S(2)}, u32[]{:S(2)}) collective-permute-start(bf16[2,384,256]{2,1,0:T(8,128)(2,1)S(1)} %get-tuple-element.19), channel_id=1, source_target_pairs={{0,16},{1,17},{2,18},{3,19},{4,20},{5,21},{6,22},{7,23}} | collective-permute-start | bytes 1179656 | tf_op jit(solution)/shard_map/ppermute | solution.py:272
  12.2 1.5 %collective-permute-start.3 = (bf16[256,512]{1,0:T(8,128)(2,1)S(1)}, bf16[256,512]{1,0:T(8,128)(2,1)S(1)}, u32[]{:S(2)}, u32[]{:S(2)}) collective-permute-start(bf16[256,512]{1,0:T(8,128)(2,1)S(1)} %shard_map.59), channel_id=1, source_target_pairs={{0,4},{1,5},{2,6},{3,7},{4,0},{5,1},{6,2},{7,3},{8,12},{9,13},{10,... | collective-permute-start | bytes 786440 | tf_op jit(solution)/shard_map/ppermute | solution.py:272
  13.7 4.7 %collective-permute-done.x = bf16[256,512]{1,0:T(8,128)(2,1)S(1)} collective-permute-done((bf16[256,512]{1,0:T(8,128)(2,1)S(1)}, bf16[256,512]{1,0:T(8,128)(2,1)S(1)}, u32[]{:S(2)}, u32[]{:S(2)}) %collective-permute-start) | collective-permute-done | bytes 262176 | tf_op jit(solution)/shard_map/ppermute | solution.py:272
  18.4 0.1 shard_map.62
  18.5 3.7 %collective-permute-start.8 = (bf16[4,384,256]{2,1,0:T(8,128)(2,1)S(1)}, bf16[4,384,256]{2,1,0:T(8,128)(2,1)S(1)}, u32[]{:S(2)}, u32[]{:S(2)}) collective-permute-start(bf16[4,384,256]{2,1,0:T(8,128)(2,1)S(1)} %shard_map.62), channel_id=1, source_target_pairs={{0,16},{1,17},{2,18},{3,19},{4,20},{5,21},{6,22},{7,23}} | collective-permute-start | bytes 2359304 | tf_op jit(solution)/shard_map/ppermute | solution.py:272
  22.2 0.0 collective-permute-done.5.after
  22.3 0.7 %collective-permute-start.10 = (bf16[2,384,256]{2,1,0:T(8,128)(2,1)S(1)}, bf16[2,384,256]{2,1,0:T(8,128)(2,1)S(1)}, u32[]{:S(2)}, u32[]{:S(2)}) collective-permute-start(bf16[2,384,256]{2,1,0:T(8,128)(2,1)S(1)} %collective-permute-done.5.after), channel_id=1, source_target_pairs={{16,24},{17,25},{18,26},{19,27},{20,28},{21,29},{22,30},{23,31}} | collective-permute-start | bytes 1179656 | tf_op jit(solution)/shard_map/ppermute | solution.py:272
  23.0 1.1 %shard_map.60 = (bf16[256,2048]{1,0:T(8,128)(2,1)}, f32[8,128]{1,0:T(8,128)S(1)}) custom-call(bf16[2,384,256]{2,1,0:T(8,128)(2,1)S(1)} %collective-permute-done.5.after), custom_call_target="tpu_custom_call" | custom-call | tf_op jit(solution)/shard_map/pallas_call | solution.py:75
  24.0 4.0 %collective-permute-done.7.rest_0_.b = bf16[4,384,256]{2,1,0:T(8,128)(2,1)S(1)} collective-permute-done((bf16[4,384,256]{2,1,0:T(8,128)(2,1)S(1)}, bf16[4,384,256]{2,1,0:T(8,128)(2,1)S(1)}, u32[]{:S(2)}, u32[]{:S(2)}) %collective-permute-start.7) | collective-permute-done | bytes 786464 | tf_op jit(solution)/shard_map/ppermute | solution.py:272
  28.0 1.3 %collective-permute-start.9 = (bf16[2,384,256]{2,1,0:T(8,128)(2,1)S(1)}, bf16[2,384,256]{2,1,0:T(8,128)(2,1)S(1)}, u32[]{:S(2)}, u32[]{:S(2)}) collective-permute-start(bf16[2,384,256]{2,1,0:T(8,128)(2,1)S(1)} %shard_map.63), channel_id=1, source_target_pairs={{0,24},{1,25},{2,26},{3,27},{4,28},{5,29},{6,30},{7,31}} | collective-permute-start | bytes 1179656 | tf_op jit(solution)/shard_map/ppermute | solution.py:272
  29.3 0.0 collective-permute-done.3.other
  29.3 1.4 %collective-permute-done.4.rest_0_.near = bf16[512,512]{1,0:T(8,128)(2,1)S(1)} collective-permute-done((bf16[512,512]{1,0:T(8,128)(2,1)S(1)}, bf16[512,512]{1,0:T(8,128)(2,1)S(1)}, u32[]{:S(2)}, u32[]{:S(2)}) %collective-permute-start.4) | collective-permute-done | bytes 524320 | tf_op jit(solution)/shard_map/ppermute | solution.py:272
  30.7 0.4 collective-permute-start.6
  31.1 7.2 %collective-permute-done.8.c = bf16[4,384,256]{2,1,0:T(8,128)(2,1)S(1)} collective-permute-done((bf16[4,384,256]{2,1,0:T(8,128)(2,1)S(1)}, bf16[4,384,256]{2,1,0:T(8,128)(2,1)S(1)}, u32[]{:S(2)}, u32[]{:S(2)}) %collective-permute-start.8) | collective-permute-done | bytes 786464 | tf_op jit(solution)/shard_map/ppermute | solution.py:272
  38.3 0.0 collective-permute-done.10.d_high
  38.3 0.0 collective-permute-done.9.d_low
  38.3 0.1 shard_map.64
  38.4 0.1 collective-permute-start.11
  38.5 0.5 collective-permute-start.12
  39.0 0.5 shard_map.65.before
  39.4 0.7 %collective-permute-done.11.low.refs_2_ = bf16[2,384,256]{2,1,0:T(8,128)(2,1)S(1)} collective-permute-done((bf16[2,384,256]{2,1,0:T(8,128)(2,1)S(1)}, bf16[2,384,256]{2,1,0:T(8,128)(2,1)S(1)}, u32[]{:S(2)}, u32[]{:S(2)}) %collective-permute-start.11) | collective-permute-done | bytes 393248 | tf_op jit(solution)/shard_map/ppermute | solution.py:275
  40.2 0.6 %collective-permute-done.12.high.refs_3_ = bf16[2,384,256]{2,1,0:T(8,128)(2,1)S(1)} collective-permute-done((bf16[2,384,256]{2,1,0:T(8,128)(2,1)S(1)}, bf16[2,384,256]{2,1,0:T(8,128)(2,1)S(1)}, u32[]{:S(2)}, u32[]{:S(2)}) %collective-permute-start.12) | collective-permute-done | bytes 393248 | tf_op jit(solution)/shard_map/ppermute | solution.py:275
  40.7 0.5 shard_map.66.refs_4_
  41.2 0.0 copy-start.3
  41.2 0.0 copy-start.1
  41.2 2.9 %collective-permute-done.6.last = bf16[512,512]{1,0:T(8,128)(2,1)S(1)} collective-permute-done((bf16[512,512]{1,0:T(8,128)(2,1)S(1)}, bf16[512,512]{1,0:T(8,128)(2,1)S(1)}, u32[]{:S(2)}, u32[]{:S(2)}) %collective-permute-start.6) | collective-permute-done | bytes 524320 | tf_op jit(solution)/shard_map/ppermute | solution.py:272
  44.2 0.4 shard_map.67
  44.6 2.0 %collective-permute-start.13 = (bf16[128,512]{1,0:T(8,128)(2,1)S(1)}, bf16[128,512]{1,0:T(8,128)(2,1)S(1)}, u32[]{:S(2)}, u32[]{:S(2)}) collective-permute-start(bf16[128,512]{1,0:T(8,128)(2,1)S(1)} %get-tuple-element.27), channel_id=1, source_target_pairs={{0,24},{1,25},{2,26},{3,27},{4,28},{5,29},{6,30},{7,31},{8,16},{9,... | collective-permute-start | bytes 393224 | tf_op jit(solution)/shard_map/ppermute | solution.py:272
  46.6 0.5 collective-permute-start.14
  47.1 1.1 %collective-permute-start.15 = (bf16[128,512]{1,0:T(8,128)(2,1)S(1)}, bf16[128,512]{1,0:T(8,128)(2,1)S(1)}, u32[]{:S(2)}, u32[]{:S(2)}) collective-permute-start(bf16[128,512]{1,0:T(8,128)(2,1)S(1)} %get-tuple-element.29), channel_id=1, source_target_pairs={{0,8},{1,9},{2,10},{3,11},{4,12},{5,13},{6,14},{7,15},{8,0},{9,1},... | collective-permute-start | bytes 393224 | tf_op jit(solution)/shard_map/ppermute | solution.py:272
  48.2 0.0 copy-done.3
  48.2 0.1 dynamic-slice_multiply_fusion
  48.3 3.3 %collective-permute-done.13.one = bf16[128,512]{1,0:T(8,128)(2,1)S(1)} collective-permute-done((bf16[128,512]{1,0:T(8,128)(2,1)S(1)}, bf16[128,512]{1,0:T(8,128)(2,1)S(1)}, u32[]{:S(2)}, u32[]{:S(2)}) %collective-permute-start.13) | collective-permute-done | bytes 131104 | tf_op jit(solution)/shard_map/ppermute | solution.py:272
  51.6 0.9 %collective-permute-done.14.two = bf16[128,512]{1,0:T(8,128)(2,1)S(1)} collective-permute-done((bf16[128,512]{1,0:T(8,128)(2,1)S(1)}, bf16[128,512]{1,0:T(8,128)(2,1)S(1)}, u32[]{:S(2)}, u32[]{:S(2)}) %collective-permute-start.14) | collective-permute-done | bytes 131104 | tf_op jit(solution)/shard_map/ppermute | solution.py:272
  52.4 0.0 collective-permute-done.15.three
  52.4 0.1 broadcast_in_dim.2.counts
  52.5 0.0 copy-done.1
  (6 shorter events, 0.2 us)
Async XLA Ops:
  1.4 4.2 %copy-start = (bf16[384,4096]{1,0:T(8,128)(2,1)S(1)}, bf16[384,4096]{1,0:T(8,128)(2,1)}, u32[]{:S(2)}) copy-start(bf16[384,4096]{1,0:T(8,128)(2,1)} %x.3) | copy-start | bytes 9437188
  1.4 4.2 %collective-permute-start.1 = (bf16[256,512]{1,0:T(8,128)(2,1)S(1)}, bf16[256,512]{1,0:T(8,128)(2,1)S(1)}, u32[]{:S(2)}, u32[]{:S(2)}) collective-permute-start(bf16[256,512]{1,0:T(8,128)(2,1)S(1)} %get-tuple-element.31), channel_id=1, source_target_pairs={{0,1},{1,0},{2,3},{3,2},{4,5},{5,4},{6,7},{7,6},{8,9},{9,8},{10,11... | collective-permute-start | bytes 786440 | tf_op jit(solution)/shard_map/ppermute | solution.py:275
  1.9 16.5 %collective-permute-start = (bf16[256,512]{1,0:T(8,128)(2,1)S(1)}, bf16[256,512]{1,0:T(8,128)(2,1)S(1)}, u32[]{:S(2)}, u32[]{:S(2)}) collective-permute-start(bf16[256,512]{1,0:T(8,128)(2,1)S(1)} %get-tuple-element.32.rest_0_.kept), channel_id=1, source_target_pairs={{0,4},{1,5},{2,6},{3,7},{4,0},{5,1},{6,2},{7,3},{8,12},{9,13},{10,... | collective-permute-start | bytes 786440 | tf_op jit(solution)/shard_map/ppermute | solution.py:272
  5.6 2.5 %copy-start.2 = (bf16[4096]{0:T(1024)(128)(2,1)S(1)}, bf16[4096]{0:T(1024)(128)(2,1)}, u32[]{:S(2)}) copy-start(bf16[4096]{0:T(1024)(128)(2,1)} %param.6) | copy-start | bytes 24580
  6.2 1.8 %collective-permute-start.2 = (f32[384,128]{1,0:T(8,128)S(1)}, f32[384,128]{1,0:T(8,128)S(1)}, u32[]{:S(2)}, u32[]{:S(2)}) collective-permute-start(f32[384,128]{1,0:T(8,128)S(1)} %shard_map.57.squares), channel_id=1, source_target_pairs={{0,1},{1,0},{2,3},{3,2},{4,5},{5,4},{6,7},{7,6},{8,9},{9,8},{10,11... | collective-permute-start | bytes 589832 | tf_op jit(solution)/shard_map/ppermute | solution.py:275
  6.5 24.2 %collective-permute-start.4 = (bf16[512,512]{1,0:T(8,128)(2,1)S(1)}, bf16[512,512]{1,0:T(8,128)(2,1)S(1)}, u32[]{:S(2)}, u32[]{:S(2)}) collective-permute-start(bf16[512,512]{1,0:T(8,128)(2,1)S(1)} %shard_map.56.after.own), channel_id=1, source_target_pairs={{0,2},{1,3},{2,0},{3,1},{4,6},{5,7},{6,4},{7,5},{8,10},{9,11},{10,... | collective-permute-start | bytes 1572872 | tf_op jit(solution)/shard_map/ppermute | solution.py:272
  9.4 18.6 %collective-permute-start.7 = (bf16[4,384,256]{2,1,0:T(8,128)(2,1)S(1)}, bf16[4,384,256]{2,1,0:T(8,128)(2,1)S(1)}, u32[]{:S(2)}, u32[]{:S(2)}) collective-permute-start(bf16[4,384,256]{2,1,0:T(8,128)(2,1)S(1)} %get-tuple-element.21), channel_id=1, source_target_pairs={{0,8},{1,9},{2,10},{3,11},{4,12},{5,13},{6,14},{7,15}} | collective-permute-start | bytes 2359304 | tf_op jit(solution)/shard_map/ppermute | solution.py:272
  10.9 11.4 %collective-permute-start.5 = (bf16[2,384,256]{2,1,0:T(8,128)(2,1)S(1)}, bf16[2,384,256]{2,1,0:T(8,128)(2,1)S(1)}, u32[]{:S(2)}, u32[]{:S(2)}) collective-permute-start(bf16[2,384,256]{2,1,0:T(8,128)(2,1)S(1)} %get-tuple-element.19), channel_id=1, source_target_pairs={{0,16},{1,17},{2,18},{3,19},{4,20},{5,21},{6,22},{7,23}} | collective-permute-start | bytes 1179656 | tf_op jit(solution)/shard_map/ppermute | solution.py:272
  12.2 17.1 %collective-permute-start.3 = (bf16[256,512]{1,0:T(8,128)(2,1)S(1)}, bf16[256,512]{1,0:T(8,128)(2,1)S(1)}, u32[]{:S(2)}, u32[]{:S(2)}) collective-permute-start(bf16[256,512]{1,0:T(8,128)(2,1)S(1)} %shard_map.59), channel_id=1, source_target_pairs={{0,4},{1,5},{2,6},{3,7},{4,0},{5,1},{6,2},{7,3},{8,12},{9,13},{10,... | collective-permute-start | bytes 786440 | tf_op jit(solution)/shard_map/ppermute | solution.py:272
  18.5 19.8 %collective-permute-start.8 = (bf16[4,384,256]{2,1,0:T(8,128)(2,1)S(1)}, bf16[4,384,256]{2,1,0:T(8,128)(2,1)S(1)}, u32[]{:S(2)}, u32[]{:S(2)}) collective-permute-start(bf16[4,384,256]{2,1,0:T(8,128)(2,1)S(1)} %shard_map.62), channel_id=1, source_target_pairs={{0,16},{1,17},{2,18},{3,19},{4,20},{5,21},{6,22},{7,23}} | collective-permute-start | bytes 2359304 | tf_op jit(solution)/shard_map/ppermute | solution.py:272
  22.3 16.0 %collective-permute-start.10 = (bf16[2,384,256]{2,1,0:T(8,128)(2,1)S(1)}, bf16[2,384,256]{2,1,0:T(8,128)(2,1)S(1)}, u32[]{:S(2)}, u32[]{:S(2)}) collective-permute-start(bf16[2,384,256]{2,1,0:T(8,128)(2,1)S(1)} %collective-permute-done.5.after), channel_id=1, source_target_pairs={{16,24},{17,25},{18,26},{19,27},{20,28},{21,29},{22,30},{23,31}} | collective-permute-start | bytes 1179656 | tf_op jit(solution)/shard_map/ppermute | solution.py:272
  28.0 10.3 %collective-permute-start.9 = (bf16[2,384,256]{2,1,0:T(8,128)(2,1)S(1)}, bf16[2,384,256]{2,1,0:T(8,128)(2,1)S(1)}, u32[]{:S(2)}, u32[]{:S(2)}) collective-permute-start(bf16[2,384,256]{2,1,0:T(8,128)(2,1)S(1)} %shard_map.63), channel_id=1, source_target_pairs={{0,24},{1,25},{2,26},{3,27},{4,28},{5,29},{6,30},{7,31}} | collective-permute-start | bytes 1179656 | tf_op jit(solution)/shard_map/ppermute | solution.py:272
  30.7 13.4 %collective-permute-start.6 = (bf16[512,512]{1,0:T(8,128)(2,1)S(1)}, bf16[512,512]{1,0:T(8,128)(2,1)S(1)}, u32[]{:S(2)}, u32[]{:S(2)}) collective-permute-start(bf16[512,512]{1,0:T(8,128)(2,1)S(1)} %shard_map.61.far), channel_id=1, source_target_pairs={{0,2},{1,3},{2,0},{3,1},{4,6},{5,7},{6,4},{7,5},{8,10},{9,11},{10,... | collective-permute-start | bytes 1572872 | tf_op jit(solution)/shard_map/ppermute | solution.py:272
  38.4 1.8 %collective-permute-start.11 = (bf16[2,384,256]{2,1,0:T(8,128)(2,1)S(1)}, bf16[2,384,256]{2,1,0:T(8,128)(2,1)S(1)}, u32[]{:S(2)}, u32[]{:S(2)}) collective-permute-start(bf16[2,384,256]{2,1,0:T(8,128)(2,1)S(1)} %get-tuple-element.24.low.refs_0_), channel_id=1, source_target_pairs={{0,1},{1,0},{2,3},{3,2},{4,5},{5,4},{6,7},{7,6},{8,9},{9,8},{10,11... | collective-permute-start | bytes 1179656 | tf_op jit(solution)/shard_map/ppermute | solution.py:275
  38.5 2.3 %collective-permute-start.12 = (bf16[2,384,256]{2,1,0:T(8,128)(2,1)S(1)}, bf16[2,384,256]{2,1,0:T(8,128)(2,1)S(1)}, u32[]{:S(2)}, u32[]{:S(2)}) collective-permute-start(bf16[2,384,256]{2,1,0:T(8,128)(2,1)S(1)} %get-tuple-element.25.high.refs_1_), channel_id=1, source_target_pairs={{0,1},{1,0},{2,3},{3,2},{4,5},{5,4},{6,7},{7,6},{8,9},{9,8},{10,11... | collective-permute-start | bytes 1179656 | tf_op jit(solution)/shard_map/ppermute | solution.py:275
  41.2 7.0 %copy-start.3 = (s32[6]{0:T(128)S(1)}, s32[6]{0:T(128)}, u32[]{:S(2)}) copy-start(s32[6]{0:T(128)} %param.8) | copy-start | bytes 76
  41.2 11.3 %copy-start.1 = (bf16[256,2048]{1,0:T(8,128)(2,1)S(1)}, bf16[256,2048]{1,0:T(8,128)(2,1)}, u32[]{:S(2)}) copy-start(bf16[256,2048]{1,0:T(8,128)(2,1)} %q_ref.1) | copy-start | bytes 3145732
  44.6 6.9 %collective-permute-start.13 = (bf16[128,512]{1,0:T(8,128)(2,1)S(1)}, bf16[128,512]{1,0:T(8,128)(2,1)S(1)}, u32[]{:S(2)}, u32[]{:S(2)}) collective-permute-start(bf16[128,512]{1,0:T(8,128)(2,1)S(1)} %get-tuple-element.27), channel_id=1, source_target_pairs={{0,24},{1,25},{2,26},{3,27},{4,28},{5,29},{6,30},{7,31},{8,16},{9,... | collective-permute-start | bytes 393224 | tf_op jit(solution)/shard_map/ppermute | solution.py:272
  46.6 5.8 %collective-permute-start.14 = (bf16[128,512]{1,0:T(8,128)(2,1)S(1)}, bf16[128,512]{1,0:T(8,128)(2,1)S(1)}, u32[]{:S(2)}, u32[]{:S(2)}) collective-permute-start(bf16[128,512]{1,0:T(8,128)(2,1)S(1)} %get-tuple-element.28), channel_id=1, source_target_pairs={{0,16},{1,17},{2,18},{3,19},{4,20},{5,21},{6,22},{7,23},{8,24},{9,... | collective-permute-start | bytes 393224 | tf_op jit(solution)/shard_map/ppermute | solution.py:272
  47.1 5.3 %collective-permute-start.15 = (bf16[128,512]{1,0:T(8,128)(2,1)S(1)}, bf16[128,512]{1,0:T(8,128)(2,1)S(1)}, u32[]{:S(2)}, u32[]{:S(2)}) collective-permute-start(bf16[128,512]{1,0:T(8,128)(2,1)S(1)} %get-tuple-element.29), channel_id=1, source_target_pairs={{0,8},{1,9},{2,10},{3,11},{4,12},{5,13},{6,14},{7,15},{8,0},{9,1},... | collective-permute-start | bytes 393224 | tf_op jit(solution)/shard_map/ppermute | solution.py:272
